TPU v7x, 512 devices: a whole 4x8x8 slice. The times are simulated.
512 devices in a mesh: blk: 128 (over z, x_hi, y), grp: 4 (over x_lo, core).
Axes of the slice: x: 4 (x_hi: 2, x_lo: 2; x = x_hi * 2 + x_lo), y: 8, z: 8, core: 2. Of those that a mesh axis runs over, the one named last changes fastest.
Arguments:
- feats: bfloat16 [131072, 1152], P(('blk', 'grp')), may hold values from -6 to 6
- proj_weight: bfloat16 [1152, 1152], P('grp'), may hold values from -0.1875 to 0.1875
- text_embed: bfloat16 [131072, 1152], P(('blk', 'grp')), may hold values from -6 to 6
- row_ids: int32 [131072], P(('blk', 'grp')), may hold values from 0 to 127
- logit_scale: float32 [1], replicated, may hold values from 2 to 10
- logit_bias: float32 [1], replicated, may hold values from -4 to -1
Outputs:
- weight_grad: float32 [1152, 1152], P('grp')
- text_grad: float32 [131072, 1152], P(('blk', 'grp'))
All inputs are finite; a program needn't handle non-finite values.
Results may differ from a plain program's by a relative error of at most 0.014.
Values may be sent and summed in bfloat16 or wider, within the bound.
No kernel may reach another device: no remote copies, remote signals or barrier semaphores. Data moves between devices by JAX's collectives and lax.ppermute only.
A program may use at most 64 MiB of HBM per device.

v0:
```python
import jax
import jax.numpy as jnp
from jax import lax
from jax.sharding import PartitionSpec as P

STEPS = 4


def from_behind(block, axis, distance):
    devices = range(lax.axis_size(axis))
    route = [((i - distance) % len(devices), i) for i in devices]
    return lax.ppermute(block, axis, route)


def on_device(feats, proj_weight, text_embed, row_ids, logit_scale, logit_bias):
    scale = logit_scale[0]
    bias = logit_bias[0]
    columns = feats
    raw = jnp.dot(
        columns,
        lax.all_gather(proj_weight, "grp", axis=0, tiled=True),
        preferred_element_type=jnp.float32,
    )
    radius = jnp.sqrt(jnp.sum(raw * raw, -1, keepdims=True) + 1e-06)
    unit = raw / radius
    image_unit = unit.astype(jnp.bfloat16)
    text_f = text_embed.astype(jnp.float32)
    text_unit = (text_f / jnp.sqrt(jnp.sum(text_f * text_f, -1, keepdims=True) + 1e-06)).astype(
        jnp.bfloat16
    )
    held = text_unit
    held_ids = row_ids
    image_grad = jnp.zeros(raw.shape, jnp.float32)
    carried = jnp.zeros(raw.shape, jnp.float32)
    for step in range(STEPS):
        if step > 0:
            held, held_ids = from_behind((held, held_ids), "blk", 1)
        logits = (
            scale
            * lax.dot_general(
                image_unit, held, (((1,), (1,)), ((), ())), preferred_element_type=jnp.float32
            )
            + bias
        )
        sign = jnp.where(row_ids[:, None] == held_ids[None, :], 1.0, -1.0).astype(jnp.float32)
        pair_weight = (-sign * jax.nn.sigmoid(-sign * logits)).astype(jnp.bfloat16)
        image_part = scale * jnp.dot(pair_weight, held, preferred_element_type=jnp.float32)
        text_part = scale * lax.dot_general(
            pair_weight, image_unit, (((0,), (0,)), ((), ())), preferred_element_type=jnp.float32
        )
        image_part, text_part = (image_part, text_part)
        image_grad = image_grad + image_part
        if step == 0:
            carried = text_part
        else:
            carried = (
                from_behind(carried.astype(jnp.bfloat16), "blk", 1).astype(carried.dtype)
                + text_part
            )
    text_grad = from_behind(carried.astype(jnp.bfloat16), "blk", 1 - STEPS).astype(carried.dtype)
    inner = jnp.sum(image_grad * unit, -1, keepdims=True)
    raw_grad = ((image_grad - unit * inner) / radius).astype(jnp.bfloat16)
    columns = feats
    shared = lax.psum_scatter(
        lax.dot_general(
            columns, raw_grad, (((0,), (0,)), ((), ())), preferred_element_type=jnp.float32
        ).astype(jnp.bfloat16),
        "grp",
        scatter_dimension=0,
        tiled=True,
    ).astype(jnp.float32)
    weight_grad = lax.psum(shared, "blk")
    return (weight_grad, text_grad)


def solution(mesh):
    return jax.shard_map(
        on_device,
        mesh=mesh,
        in_specs=(
            P(("blk", "grp"), None),
            P("grp", None),
            P(("blk", "grp"), None),
            P(("blk", "grp")),
            P(),
            P(),
        ),
        out_specs=(P("grp", None), P(("blk", "grp"), None)),
        check_vma=False,
    )
```

profile of v0, /device:TPU:2, one launch (start us, length us, event | category | flops | bytes accessed | tf_op | source)
XLA Modules:
  0.0 925.3 jit_solution(3009781956771162995)
XLA Ops:
  7.2 0.0 copy-start
  7.2 0.0 copy-start.1
  7.2 0.0 copy-start.2
  7.2 0.0 all-gather.2.cloned.1.call-start
  7.2 0.7 all-gather.2.cloned.1.call-update
  7.9 0.0 reduce-scatter.4.cloned.1.call-start
  8.0 1.3 fusion.3
  9.2 0.0 copy-done.1
  9.3 0.2 fusion.4
  9.5 3.5 collective-permute-start.1
  13.0 25.3 %collective-permute-done.1 = bf16[256,1152]{1,0:T(8,128)(2,1)S(1)} collective-permute-done((bf16[256,1152]{1,0:T(8,128)(2,1)S(1)}, bf16[256,1152]{1,0:T(8,128)(2,1)S(1)}, u32[]{:S(2)}, u32[]{:S(2)}) %collective-permute-start.1) | collective-permute-done | bytes 589856 | tf_op jit(solution)/shard_map/ppermute | solution.py:12
  38.3 1.9 collective-permute-start.3
  40.2 0.0 copy-done.2
  40.3 1.9 collective-permute-start
  42.2 18.3 %collective-permute-done = s32[256]{0:T(256)S(1)} collective-permute-done((s32[256]{0:T(256)S(1)}, s32[256]{0:T(256)S(1)}, u32[]{:S(2)}, u32[]{:S(2)}) %collective-permute-start) | collective-permute-done | bytes 1056 | tf_op jit(solution)/shard_map/ppermute | solution.py:12
  60.5 1.9 collective-permute-start.2
  63.7 8.0 collective-permute-done.2
  71.7 1.9 collective-permute-start.4
  73.6 0.0 collective-permute-done.3
  73.6 1.9 collective-permute-start.5
  75.5 2.0 all-gather.2.cloned.1.call-done
  77.5 0.0 copy-done
  77.5 2.8 multiply_reduce_fusion.1
  80.4 0.2 fusion.39
  80.5 0.4 fusion.33
  80.9 0.3 fusion.40
  81.3 0.4 fusion.34
  81.7 0.4 fusion.35
  82.2 0.3 convolution_add_fusion.2
  82.5 0.3 convolution_add_fusion.1
  82.9 0.1 collective-permute-done.4
  82.9 10.6 %collective-permute-done.5 = bf16[256,1152]{1,0:T(8,128)(2,1)} collective-permute-done((bf16[256,1152]{1,0:T(8,128)(2,1)S(1)}, bf16[256,1152]{1,0:T(8,128)(2,1)}, u32[]{:S(2)}, u32[]{:S(2)}) %collective-permute-start.5) | collective-permute-done | bytes 589856 | tf_op jit(solution)/shard_map/ppermute | solution.py:12
  93.5 1.5 fusion.36
  95.0 1.6 multiply_reduce_fusion
  96.6 2.7 fusion
  99.3 5.2 copy.10
  104.5 0.0 reduce-scatter.4.cloned.1.call-update
  104.6 0.4 fusion.2
  104.9 1.9 collective-permute-start.6
  106.9 17.1 %collective-permute-done.6 = bf16[256,1152]{1,0:T(8,128)(2,1)S(1)} collective-permute-done((bf16[256,1152]{1,0:T(8,128)(2,1)S(1)}, bf16[256,1152]{1,0:T(8,128)(2,1)S(1)}, u32[]{:S(2)}, u32[]{:S(2)}) %collective-permute-start.6) | collective-permute-done | bytes 589856 | tf_op jit(solution)/shard_map/ppermute | solution.py:12
  123.9 0.4 add_convert_fusion.2
  124.3 1.9 collective-permute-start.7
  126.2 0.4 convolution_multiply_fusion.1
  126.6 15.7 %collective-permute-done.7 = bf16[256,1152]{1,0:T(8,128)(2,1)S(1)} collective-permute-done((bf16[256,1152]{1,0:T(8,128)(2,1)S(1)}, bf16[256,1152]{1,0:T(8,128)(2,1)S(1)}, u32[]{:S(2)}, u32[]{:S(2)}) %collective-permute-start.7) | collective-permute-done | bytes 589856 | tf_op jit(solution)/shard_map/ppermute | solution.py:12
  142.3 0.1 add_convert_fusion.1
  142.4 1.9 collective-permute-start.8
  144.3 0.4 convolution_multiply_fusion
  144.7 15.3 %collective-permute-done.8 = bf16[256,1152]{1,0:T(8,128)(2,1)S(1)} collective-permute-done((bf16[256,1152]{1,0:T(8,128)(2,1)S(1)}, bf16[256,1152]{1,0:T(8,128)(2,1)S(1)}, u32[]{:S(2)}, u32[]{:S(2)}) %collective-permute-start.8) | collective-permute-done | bytes 589856 | tf_op jit(solution)/shard_map/ppermute | solution.py:12
  160.0 0.1 add_convert_fusion
  160.1 1.9 collective-permute-start.9
  162.0 34.0 %collective-permute-done.9 = bf16[256,1152]{1,0:T(8,128)(2,1)S(1)} collective-permute-done((bf16[256,1152]{1,0:T(8,128)(2,1)S(1)}, bf16[256,1152]{1,0:T(8,128)(2,1)S(1)}, u32[]{:S(2)}, u32[]{:S(2)}) %collective-permute-start.9) | collective-permute-done | bytes 589856 | tf_op jit(solution)/shard_map/ppermute | solution.py:12
  196.0 1.1 convert_element_type.75
  197.1 0.0 reduce-scatter.4.cloned.1.call-done
  197.1 1.5 copy.11
  198.6 718.3 %all-reduce.1 = f32[288,1152]{0,1:T(8,128)S(1)} all-reduce(bf16[288,1152]{0,1:T(8,128)(2,1)S(1)} %copy.11), channel_id=1, replica_groups=mesh['blk'=128,'grp'=4] {'blk'}, use_global_device_ids=true, to_apply=%region_4.5 | all-reduce | flops 331776 | bytes 1990656 | tf_op jit(solution)/shard_map/psum | solution.py:72
  916.9 1.6 copy.9
  (2 shorter events, 0.0 us)
Async XLA Ops:
  7.2 70.4 %copy-start = (bf16[256,1152]{1,0:T(8,128)(2,1)S(1)}, bf16[256,1152]{1,0:T(8,128)(2,1)}, u32[]{:S(2)}) copy-start(bf16[256,1152]{1,0:T(8,128)(2,1)} %param.6) | copy-start | bytes 1769476
  7.2 2.1 copy-start.1
  7.2 33.1 %copy-start.2 = (s32[256]{0:T(256)S(1)}, s32[256]{0:T(256)}, u32[]{:S(2)}) copy-start(s32[256]{0:T(256)} %param.9) | copy-start | bytes 3076
  7.2 70.3 %all-gather.2.cloned.1.call-start = ((), (), s32[]{:S(2)}) async-start(), calls=%async_computation.1 | async-start | bytes 3317760 | tf_op jit(solution)/shard_map/all_gather | solution.py:21
  7.9 189.2 %reduce-scatter.4.cloned.1.call-start = ((), (), s32[]{:S(2)}) async-start(), calls=%async_computation.2 | async-start | bytes 3317760
  9.5 28.8 %collective-permute-start.1 = (bf16[256,1152]{1,0:T(8,128)(2,1)S(1)}, bf16[256,1152]{1,0:T(8,128)(2,1)S(1)}, u32[]{:S(2)}, u32[]{:S(2)}) collective-permute-start(bf16[256,1152]{1,0:T(8,128)(2,1)S(1)} %fusion.4), channel_id=1, source_target_pairs={{508,0},{0,4},{4,8},{8,12},{12,16},{16,20},{20,24},{24,28},{28,32}... | collective-permute-start | bytes 1769480 | tf_op jit(solution)/shard_map/ppermute | solution.py:12
  38.3 35.3 %collective-permute-start.3 = (bf16[256,1152]{1,0:T(8,128)(2,1)S(1)}, bf16[256,1152]{1,0:T(8,128)(2,1)S(1)}, u32[]{:S(2)}, u32[]{:S(2)}) collective-permute-start(bf16[256,1152]{1,0:T(8,128)(2,1)S(1)} %collective-permute-done.1), channel_id=1, source_target_pairs={{508,0},{0,4},{4,8},{8,12},{12,16},{16,20},{20,24},{24,28},{28,32}... | collective-permute-start | bytes 1769480 | tf_op jit(solution)/shard_map/ppermute | solution.py:12
  40.3 20.3 %collective-permute-start = (s32[256]{0:T(256)S(1)}, s32[256]{0:T(256)S(1)}, u32[]{:S(2)}, u32[]{:S(2)}) collective-permute-start(s32[256]{0:T(256)S(1)} %copy-done.2), channel_id=1, source_target_pairs={{508,0},{0,4},{4,8},{8,12},{12,16},{16,20},{20,24},{24,28},{28,32}... | collective-permute-start | bytes 3080 | tf_op jit(solution)/shard_map/ppermute | solution.py:12
  60.5 11.2 %collective-permute-start.2 = (s32[256]{0:T(256)S(1)}, s32[256]{0:T(256)S(1)}, u32[]{:S(2)}, u32[]{:S(2)}) collective-permute-start(s32[256]{0:T(256)S(1)} %collective-permute-done), channel_id=1, source_target_pairs={{508,0},{0,4},{4,8},{8,12},{12,16},{16,20},{20,24},{24,28},{28,32}... | collective-permute-start | bytes 3080 | tf_op jit(solution)/shard_map/ppermute | solution.py:12
  71.7 11.2 %collective-permute-start.4 = (s32[256]{0:T(256)S(1)}, s32[256]{0:T(256)S(1)}, u32[]{:S(2)}, u32[]{:S(2)}) collective-permute-start(s32[256]{0:T(256)S(1)} %collective-permute-done.2), channel_id=1, source_target_pairs={{508,0},{0,4},{4,8},{8,12},{12,16},{16,20},{20,24},{24,28},{28,32}... | collective-permute-start | bytes 3080 | tf_op jit(solution)/shard_map/ppermute | solution.py:12
  73.6 19.9 %collective-permute-start.5 = (bf16[256,1152]{1,0:T(8,128)(2,1)S(1)}, bf16[256,1152]{1,0:T(8,128)(2,1)}, u32[]{:S(2)}, u32[]{:S(2)}) collective-permute-start(bf16[256,1152]{1,0:T(8,128)(2,1)S(1)} %collective-permute-done.3), channel_id=1, source_target_pairs={{508,0},{0,4},{4,8},{8,12},{12,16},{16,20},{20,24},{24,28},{28,32}... | collective-permute-start | bytes 1769480 | tf_op jit(solution)/shard_map/ppermute | solution.py:12
  104.9 19.0 %collective-permute-start.6 = (bf16[256,1152]{1,0:T(8,128)(2,1)S(1)}, bf16[256,1152]{1,0:T(8,128)(2,1)S(1)}, u32[]{:S(2)}, u32[]{:S(2)}) collective-permute-start(bf16[256,1152]{1,0:T(8,128)(2,1)S(1)} %fusion.2), channel_id=1, source_target_pairs={{508,0},{0,4},{4,8},{8,12},{12,16},{16,20},{20,24},{24,28},{28,32}... | collective-permute-start | bytes 1769480 | tf_op jit(solution)/shard_map/ppermute | solution.py:12
  124.3 18.0 %collective-permute-start.7 = (bf16[256,1152]{1,0:T(8,128)(2,1)S(1)}, bf16[256,1152]{1,0:T(8,128)(2,1)S(1)}, u32[]{:S(2)}, u32[]{:S(2)}) collective-permute-start(bf16[256,1152]{1,0:T(8,128)(2,1)S(1)} %add_convert_fusion.2), channel_id=1, source_target_pairs={{508,0},{0,4},{4,8},{8,12},{12,16},{16,20},{20,24},{24,28},{28,32}... | collective-permute-start | bytes 1769480 | tf_op jit(solution)/shard_map/ppermute | solution.py:12
  142.4 17.6 %collective-permute-start.8 = (bf16[256,1152]{1,0:T(8,128)(2,1)S(1)}, bf16[256,1152]{1,0:T(8,128)(2,1)S(1)}, u32[]{:S(2)}, u32[]{:S(2)}) collective-permute-start(bf16[256,1152]{1,0:T(8,128)(2,1)S(1)} %add_convert_fusion.1), channel_id=1, source_target_pairs={{508,0},{0,4},{4,8},{8,12},{12,16},{16,20},{20,24},{24,28},{28,32}... | collective-permute-start | bytes 1769480 | tf_op jit(solution)/shard_map/ppermute | solution.py:12
  160.1 35.9 %collective-permute-start.9 = (bf16[256,1152]{1,0:T(8,128)(2,1)S(1)}, bf16[256,1152]{1,0:T(8,128)(2,1)S(1)}, u32[]{:S(2)}, u32[]{:S(2)}) collective-permute-start(bf16[256,1152]{1,0:T(8,128)(2,1)S(1)} %add_convert_fusion), channel_id=1, source_target_pairs={{12,0},{16,4},{20,8},{24,12},{28,16},{32,20},{36,24},{40,28},{44,3... | collective-permute-start | bytes 1769480 | tf_op jit(solution)/shard_map/ppermute | solution.py:12
Sparse Core Ops, SparseCore 0:
  10.1 67.3 all-gather.1
  104.7 52.8 reduce-scatter.3
where the time goes:
time: 926 us; the launch traced here: 925 us
  blocking collectives  718 us (78%)
  waiting for transfers between devices  147 us (16%)
  starting transfers between devices  20.8 us (2%)
  between operations  15.6 us (2%)
  matrix products  12.4 us (1%)
    psum x1, blocking collectives, on_device(): weight_grad = lax.psum(shared, 'blk')  718 us
    ppermute x10, waiting for transfers between devices, from_behind(): return lax.ppermute(block, axis, route)  144 us
    ppermute x10, starting transfers between devices, from_behind(): return lax.ppermute(block, axis, route)  20.7 us
  transfers between devices with their start and end apart: 12, of which 10 were waited for; matrix products, arithmetic and copies ran while one was open for 1% of the time, Pallas kernels for 0%

commit v1 on v0

v1 whole, which is shorter than its diff:
```python
import jax
import jax.numpy as jnp
from jax import lax
from jax.sharding import Mesh, PartitionSpec as P

BF = jnp.bfloat16
F32 = jnp.float32
ROWS = 256
D = 1152
SHARD = D // 4
SUB = SHARD // 4
SPLIT = ("z2", "z1", "z0", "xh", "y2", "y1", "y0", "xl", "core")
BLK = SPLIT[:7]
NEAR = ("z0", "y0")
FAR = ("z2", "z1", "xh", "y2", "y1")


def shift(block, distance):
    n = 128
    return lax.ppermute(block, BLK, [((i - distance) % n, i) for i in range(n)])


def swap(block, axis):
    return lax.ppermute(block, axis, [(0, 1), (1, 0)])


def exchange(chunks, axes):
    return lax.all_to_all(chunks, axes, 0, 0, tiled=True)


def spread(chunk, axes, n):
    return exchange(jnp.broadcast_to(chunk[None], (n,) + chunk.shape), axes)


def total(chunks):
    return jnp.sum(chunks.astype(F32), 0).astype(BF)


def gather_weight(shard):
    xl, core = lax.axis_index("xl"), lax.axis_index("core")
    other = swap(shard, "xl")
    pair = jnp.where(xl == 0, jnp.stack([shard, other]), jnp.stack([other, shard]))
    far = swap(pair, "core")
    return jnp.where(core == 0, jnp.stack([pair, far], 1), jnp.stack([far, pair], 1)).reshape(D, D)


def reduce_weight_grad(part):
    core = lax.axis_index("core")
    quarters = part.reshape(2, 2, SHARD, D)
    send = lax.dynamic_index_in_dim(quarters, 1 - core, 1, False)
    keep = lax.dynamic_index_in_dim(quarters, core, 1, False)
    halves = (keep.astype(F32) + swap(send, "core").astype(F32)).astype(BF)
    mine = total(exchange(halves.reshape(8, SUB, D), ("xl",) + NEAR))
    tiles = mine.reshape(SUB, 9, 128).transpose(1, 0, 2).reshape(SUB * 9, 128)
    tiles = jnp.pad(tiles, ((0, 768 - SUB * 9), (0, 0))).reshape(32, 24, 128)
    done = total(exchange(tiles, FAR))
    done = spread(done, FAR, 32).reshape(768, 128)[:704]
    done = spread(done, NEAR, 4)[:, : SUB * 9]
    return done.reshape(4, 9, SUB, 128).transpose(0, 2, 1, 3).reshape(SHARD, D).astype(F32)


def with_ids(block, ids):
    row = jnp.pad(ids.astype(BF)[None, :], ((0, 15), (0, D - ROWS)))
    return jnp.concatenate([block, row], 0)


def split_ids(payload):
    return payload[:ROWS], payload[ROWS, :ROWS]


def normalize(rows):
    radius = jnp.sqrt(jnp.sum(rows * rows, -1, keepdims=True) + 1e-06)
    return rows / radius, radius


def on_device(feats, proj_weight, text_embed, row_ids, logit_scale, logit_bias):
    scale = logit_scale[0]
    bias = logit_bias[0]
    payloads = [with_ids(feats, row_ids)]
    payloads.append(shift(payloads[0], -1))
    text_unit = normalize(text_embed.astype(F32))[0].astype(BF)
    text_payload = shift(with_ids(text_unit, row_ids), 1)
    weight = gather_weight(proj_weight)
    payloads.append(shift(payloads[1], -1))
    payloads.append(shift(payloads[2], -1))
    texts = [split_ids(with_ids(text_unit, row_ids)), split_ids(text_payload)]

    def pair(image_unit, ids, text, text_ids):
        logits = (
            scale
            * lax.dot_general(image_unit, text, (((1,), (1,)), ((), ())), preferred_element_type=F32)
            + bias
        )
        sign = jnp.where(ids[:, None] == text_ids[None, :], 1.0, -1.0).astype(F32)
        return (-sign * jax.nn.sigmoid(-sign * logits)).astype(BF)

    text_grad = jnp.zeros((ROWS, D), F32)
    part = jnp.zeros((D, D), F32)
    for offset in range(4):
        columns, ids = split_ids(payloads[offset])
        raw = jnp.dot(columns, weight, preferred_element_type=F32)
        unit, radius = normalize(raw)
        image_unit = unit.astype(BF)
        near = pair(image_unit, ids, *texts[0])
        text_grad = text_grad + scale * lax.dot_general(
            near, image_unit, (((0,), (0,)), ((), ())), preferred_element_type=F32
        )
        if offset < 3:
            back = pair(image_unit, ids, *texts[1])
            image_grad = scale * jnp.dot(back, texts[1][0], preferred_element_type=F32)
            if offset == 0:
                image_grad = image_grad + scale * jnp.dot(near, texts[0][0], preferred_element_type=F32)
            inner = jnp.sum(image_grad * unit, -1, keepdims=True)
            raw_grad = ((image_grad - unit * inner) / radius).astype(BF)
            part = part + lax.dot_general(
                columns, raw_grad, (((0,), (0,)), ((), ())), preferred_element_type=F32
            )
    return (reduce_weight_grad(part.astype(BF)), text_grad)


def solution(mesh):
    fine = Mesh(mesh.devices.reshape((2,) * 9), SPLIT)
    grp = SPLIT[7:]
    return jax.shard_map(
        on_device,
        mesh=fine,
        in_specs=(P(SPLIT, None), P(grp, None), P(SPLIT, None), P(SPLIT), P(), P()),
        out_specs=(P(grp, None), P(SPLIT, None)),
        check_vma=False,
    )
```

time: 926 us -> 220 us (0.24)
  the two profiles are of different devices: /device:TPU:2 before, /device:TPU:1 now
where the time goes in v1:
time: 220 us; the launch traced here: 217 us
  starting transfers between devices  87.9 us (40%)
  matrix products  54.4 us (25%)
  waiting for transfers between devices  46.5 us (21%)
  local copies, waits for them, and re-layouts  15.1 us (7%)
  other arithmetic  10.5 us (5%)
  between operations  2.28 us (1%)
    ppermute x4, starting transfers between devices, shift(): return lax.ppermute(block, BLK, [((i - distance) % n, i) for i in range(n)])  44.3 us
    all_to_all x4, starting transfers between devices, exchange(): return lax.all_to_all(chunks, axes, 0, 0, tiled=True)  33.7 us
    all_to_all x4, waiting for transfers between devices, exchange(): return lax.all_to_all(chunks, axes, 0, 0, tiled=True)  26.2 us
    ppermute x4, waiting for transfers between devices, shift(): return lax.ppermute(block, BLK, [((i - distance) % n, i) for i in range(n)])  17.7 us
    dot_general x3, matrix products, on_device(): lax.dot_general(columns, raw_grad, (((0,), (0,)), ((), ())), preferred_el...  15.3 us
    dot_general x4, matrix products, on_device(): lax.dot_general(near, image_unit, (((0,), (0,)), ((), ())), preferred_ele...  12.1 us
    dot_general x4, matrix products, on_device(): raw = jnp.dot(columns, weight, preferred_element_type=F32)  12.1 us
    dot_general x3, matrix products, on_device(): image_grad = scale * jnp.dot(back, texts[1][0], preferred_element_type=F32)  11.4 us
  transfers between devices with their start and end apart: 11, of which 6 were waited for; matrix products, arithmetic and copies ran while one was open for 13% of the time, Pallas kernels for 0%

profile of v1, /device:TPU:1, one launch (start us, length us, event | category | flops | bytes accessed | tf_op | source)
XLA Modules:
  0.0 216.7 jit_solution(5039456779605943187)
XLA Ops:
  0.6 0.0 copy-start.5
  0.6 4.1 %collective-permute-start.1 = (bf16[288,1152]{1,0:T(8,128)(2,1)}, bf16[288,1152]{1,0:T(8,128)(2,1)S(1)}, u32[]{:S(2)}, u32[]{:S(2)}) collective-permute-start(bf16[288,1152]{1,0:T(8,128)(2,1)} %param.7), channel_id=1, source_target_pairs={{0,2},{2,0},{1,3},{3,1},{4,6},{6,4},{5,7},{7,5},{8,10},{10,8},{9,1... | collective-permute-start | bytes 1990664 | tf_op jit(solution)/shard_map/ppermute | solution.py:24
  4.7 1.3 fusion.5
  6.0 0.7 convert_element_type.90
  6.7 0.5 copy-done.9
  7.2 1.3 fusion.6
  8.5 0.0 copy-start.2
  8.5 1.1 fusion.68
  9.7 15.7 %collective-permute-start.3 = (bf16[272,1152]{1,0:T(8,128)(2,1)}, bf16[272,1152]{1,0:T(8,128)(2,1)}, u32[]{:S(2)}, u32[]{:S(2)}) collective-permute-start(bf16[272,1152]{1,0:T(8,128)(2,1)} %get-tuple-element.6), channel_id=1, source_target_pairs={{4,0},{8,4},{12,8},{16,12},{20,16},{24,20},{28,24},{32,28},{36,32}... | collective-permute-start | bytes 1880072 | tf_op jit(solution)/shard_map/ppermute | solution.py:20
  25.4 0.3 maximum_select_fusion.2
  25.7 3.1 %collective-permute-start.2 = (bf16[2,288,1152]{2,1,0:T(8,128)(2,1)S(1)}, bf16[2,288,1152]{2,1,0:T(8,128)(2,1)}, u32[]{:S(2)}, u32[]{:S(2)}) collective-permute-start(bf16[2,288,1152]{2,1,0:T(8,128)(2,1)S(1)} %maximum_select_fusion.2), channel_id=1, source_target_pairs={{0,1},{1,0},{2,3},{3,2},{4,5},{5,4},{6,7},{7,6},{8,9},{9,8},{10,11... | collective-permute-start | bytes 3981320 | tf_op jit(solution)/shard_map/ppermute | solution.py:24
  28.9 1.9 collective-permute-start
  30.8 7.4 %collective-permute-done.3 = bf16[272,1152]{1,0:T(8,128)(2,1)} collective-permute-done((bf16[272,1152]{1,0:T(8,128)(2,1)}, bf16[272,1152]{1,0:T(8,128)(2,1)}, u32[]{:S(2)}, u32[]{:S(2)}) %collective-permute-start.3) | collective-permute-done | bytes 626720 | tf_op jit(solution)/shard_map/ppermute | solution.py:20
  38.2 16.5 %collective-permute-start.4 = (bf16[272,1152]{1,0:T(8,128)(2,1)}, bf16[272,1152]{1,0:T(8,128)(2,1)}, u32[]{:S(2)}, u32[]{:S(2)}) collective-permute-start(bf16[272,1152]{1,0:T(8,128)(2,1)} %collective-permute-done.3), channel_id=1, source_target_pairs={{4,0},{8,4},{12,8},{16,12},{20,16},{24,20},{28,24},{32,28},{36,32}... | collective-permute-start | bytes 1880072 | tf_op jit(solution)/shard_map/ppermute | solution.py:20
  55.9 1.2 slice_reduce_fusion.2
  57.2 10.3 %collective-permute-done = bf16[272,1152]{1,0:T(8,128)(2,1)} collective-permute-done((bf16[272,1152]{1,0:T(8,128)(2,1)}, bf16[272,1152]{1,0:T(8,128)(2,1)}, u32[]{:S(2)}, u32[]{:S(2)}) %collective-permute-start) | collective-permute-done | bytes 626720 | tf_op jit(solution)/shard_map/ppermute | solution.py:20
  67.5 1.3 slice_reduce_fusion.3
  68.8 0.3 maximum_select_fusion.1
  69.0 0.0 collective-permute-done.4
  69.1 1.2 slice_reduce_fusion.1
  70.3 0.0 collective-permute-done.2
  70.3 2.1 maximum_select_fusion
  72.4 2.0 multiply_reduce_fusion.5
  74.5 2.2 multiply_reduce_fusion.4
  76.6 0.4 copy.21
  77.0 4.0 %multiply_reduce_fusion.2 = (f32[256]{0:T(256)S(1)}, f32[256,1152]{1,0:T(8,128)}) fusion(bf16[1152,1152]{1,0:T(8,128)(2,1)} %bitcast.79, bf16[272,1152]{1,0:T(8,128)(2,1)} %collective-permute-done.4), kind=kOutput, calls=%fused_computation.37 | convolution fusion | flops 680066816 | bytes 4424704 | tf_op jit(solution)/shard_map/dot_general | solution.py:101
  81.0 1.6 copy.23
  82.6 2.1 fusion.61
  84.8 0.7 copy-done.7
  85.4 1.4 fusion.177
  86.8 4.9 %fusion.7 = (f32[256]{0:T(256)}, f32[256,1152]{0,1:T(8,128)}) fusion(f32[1152,256]{1,0:T(8,128)} %get-tuple-element.9, f32[256]{0:T(256)S(1)} %add_sqrt_fusion.3, f32[]{:T(128)} %bitcast.62, f32[256,1152]{0,1:T(8,128)} %fusion.177, bf16[272,1152]{1,0:T(8,128)(2,1)} %collective-permute-done, f32[]{:T(128)} %bitcast.69, ...), kind=kOutput, calls=%fused_computation.29 | convolution fusion | flops 304774912 | bytes 5903872 | tf_op jit(solution)/shard_map/dot_general | solution.py:110
  91.7 4.9 %convolution_bitcast_fusion = f32[1152,1152]{1,0:T(8,128)} fusion(bf16[256,1152]{1,0:T(8,128)(2,1)S(1)} %copy-done.6, f32[256,1152]{0,1:T(8,128)} %get-tuple-element.11, f32[256]{0:T(256)S(1)} %add_sqrt_fusion.3, f32[256]{0:T(256)} %get-tuple-element.10, f32[1152,256]{1,0:T(8,128)} %get-tuple-element.9), kind=kOutput, calls=%fused_computation.2 | convolution fusion | flops 680951808 | bytes 8259584 | tf_op jit(solution)/shard_map/dot_general | solution.py:115
  96.6 3.3 %multiply_reduce_fusion.3 = (f32[256]{0:T(256)S(1)}, f32[256,1152]{0,1:T(8,128)}) fusion(f32[256,1152]{0,1:T(8,128)S(1)} %copy.21, f32[256]{0:T(256)S(1)} %add_sqrt_fusion.2, bf16[272,1152]{1,0:T(8,128)(2,1)} %collective-permute-done, f32[]{:T(128)} %bitcast.74, f32[]{:T(128)} %bitcast.65, bf16[256]{0:T(256)(128)(2,1)} %slice_reduce_fusion.3, ...), kind=kOutput, calls=%fused_computation.39 | convolution fusion | flops 304480000 | bytes 4724224 | tf_op jit(solution)/shard_map/dot_general | solution.py:110
  99.9 6.4 %convolution_add_fusion.1 = f32[1152,1152]{1,0:T(8,128)} fusion(f32[1152,1152]{1,0:T(8,128)} %convolution_bitcast_fusion, f32[256,1152]{0,1:T(8,128)} %get-tuple-element.15, f32[256]{0:T(256)S(1)} %get-tuple-element.14, f32[256]{0:T(256)S(1)} %add_sqrt_fusion.2, bf16[272,1152]{1,0:T(8,128)(2,1)} %collective-permute-done.3, f32[256,1152]{0,1:T(8,128)S(1)} %copy.21), kind=kOutput, calls=%fused_computation.1 | convolution fusion | flops 682278912 | bytes 13568000 | tf_op jit(solution)/shard_map/dot_general | solution.py:115
  106.2 3.3 %multiply_reduce_fusion.1 = (f32[256]{0:T(256)S(1)}, f32[256,1152]{0,1:T(8,128)}) fusion(f32[256,1152]{0,1:T(8,128)S(1)} %copy.23, f32[256]{0:T(256)S(1)} %add_sqrt_fusion.1, bf16[272,1152]{1,0:T(8,128)(2,1)} %collective-permute-done, f32[]{:T(128)} %bitcast.73, f32[]{:T(128)} %bitcast.64, bf16[256]{0:T(256)(128)(2,1)S(1)} %copy-done.13, ...), kind=kOutput, calls=%fused_computation.36 | convolution fusion | flops 304480000 | bytes 4724224 | tf_op jit(solution)/shard_map/dot_general | solution.py:110
  109.5 4.0 %fusion = bf16[1152,1152]{1,0:T(8,128)(2,1)S(1)} fusion(f32[1152,1152]{1,0:T(8,128)} %convolution_add_fusion.1, f32[256,1152]{0,1:T(8,128)} %get-tuple-element.19, f32[256]{0:T(256)S(1)} %get-tuple-element.18, f32[256]{0:T(256)S(1)} %add_sqrt_fusion.1, bf16[272,1152]{1,0:T(8,128)(2,1)} %collective-permute-done.4, f32[256,1152]{0,1:T(8,128)S(1)} %copy.23), kind=kOutput, calls=%fused_computation.3 | convolution fusion | flops 683606016 | bytes 10913792 | tf_op jit(solution)/shard_map/dot_general | solution.py:115
  113.6 0.1 dynamic-slice_bitcast_fusion
  113.7 1.4 copy-done.1
  115.1 2.7 %collective-permute-start.5 = (bf16[2,288,1152]{2,1,0:T(8,128)(2,1)S(1)}, bf16[2,288,1152]{2,1,0:T(8,128)(2,1)}, u32[]{:S(2)}, u32[]{:S(2)}) collective-permute-start(bf16[2,288,1152]{2,1,0:T(8,128)(2,1)S(1)} %dynamic-slice_bitcast_fusion), channel_id=1, source_target_pairs={{0,1},{1,0},{2,3},{3,2},{4,5},{5,4},{6,7},{7,6},{8,9},{9,8},{10,11... | collective-permute-start | bytes 3981320 | tf_op jit(solution)/shard_map/ppermute | solution.py:24
  117.8 2.6 %collective-permute-done.5 = bf16[2,288,1152]{2,1,0:T(8,128)(2,1)} collective-permute-done((bf16[2,288,1152]{2,1,0:T(8,128)(2,1)S(1)}, bf16[2,288,1152]{2,1,0:T(8,128)(2,1)}, u32[]{:S(2)}, u32[]{:S(2)}) %collective-permute-start.5) | collective-permute-done | bytes 1327136 | tf_op jit(solution)/shard_map/ppermute | solution.py:24
  120.4 3.1 %fusion.3 = bf16[2,288,1152]{2,1,0:T(8,128)(2,1)} fusion(bf16[2,288,1152]{2,1,0:T(8,128)(2,1)} %collective-permute-done.5, bf16[2,2,288,1152]{3,2,1,0:T(8,128)(2,1)} %bitcast.82, s32[]{:T(128)S(6)} %select_n.71), kind=kLoop, calls=%fused_computation.14 | loop fusion | flops 2654208 | bytes 3981316 | tf_op jit(solution)/shard_map/convert_element_type | solution.py:52
  123.5 3.6 %all-to-all-start = ((bf16[8,72,1152]{2,1,0:T(8,128)(2,1)}), bf16[8,72,1152]{2,1,0:T(8,128)(2,1)S(1)}, u32[]{:S(2)}, u32[]{:S(2)}) async-start(bf16[8,72,1152]{2,1,0:T(8,128)(2,1)} %bitcast.13), calls=%async_computation | async-start | bytes 2654208 | tf_op jit(solution)/shard_map/all_to_all | solution.py:28
  127.0 10.1 %collective-permute-start.6 = (bf16[272,1152]{1,0:T(8,128)(2,1)}, bf16[272,1152]{1,0:T(8,128)(2,1)}, u32[]{:S(2)}, u32[]{:S(2)}) collective-permute-start(bf16[272,1152]{1,0:T(8,128)(2,1)} %collective-permute-done.4), channel_id=1, source_target_pairs={{4,0},{8,4},{12,8},{16,12},{20,16},{24,20},{28,24},{32,28},{36,32}... | collective-permute-start | bytes 1880072 | tf_op jit(solution)/shard_map/ppermute | solution.py:20
  137.2 7.9 %all-to-all-done = bf16[8,72,1152]{2,1,0:T(8,128)(2,1)S(1)} async-done(((bf16[8,72,1152]{2,1,0:T(8,128)(2,1)}), bf16[8,72,1152]{2,1,0:T(8,128)(2,1)S(1)}, u32[]{:S(2)}, u32[]{:S(2)}) %all-to-all-start) | async-done | bytes 1327136 | tf_op jit(solution)/shard_map/all_to_all | solution.py:28
  145.1 0.2 reduce_sum.103
  145.3 0.1 reshape.137
  145.5 0.7 pad.11
  146.2 13.0 %all-to-all-start.1 = ((bf16[32,24,128]{2,1,0:T(8,128)(2,1)}), bf16[32,24,128]{2,1,0:T(8,128)(2,1)S(1)}, u32[]{:S(2)}, u32[]{:S(2)}) async-start(bf16[32,24,128]{2,1,0:T(8,128)(2,1)} %bitcast.16), calls=%async_computation.1 | async-start | bytes 393216 | tf_op jit(solution)/shard_map/all_to_all | solution.py:28
  159.1 0.7 slice_reduce_fusion
  159.8 2.6 %fusion.154 = f32[256,1152]{0,1:T(8,128)} fusion(bf16[256,256]{1,0:T(8,128)(2,1)S(1)} %copy-done.8, f32[1152,256]{1,0:T(8,128)} %get-tuple-element.9, f32[256]{0:T(256)S(1)} %add_sqrt_fusion.3), kind=kOutput, calls=%fused_computation.195 | convolution fusion | flops 151584768 | bytes 2491392 | tf_op jit(solution)/shard_map/dot_general | solution.py:105
  162.4 11.2 %all-to-all-done.1 = bf16[32,24,128]{2,1,0:T(8,128)(2,1)S(1)} async-done(((bf16[32,24,128]{2,1,0:T(8,128)(2,1)}), bf16[32,24,128]{2,1,0:T(8,128)(2,1)S(1)}, u32[]{:S(2)}, u32[]{:S(2)}) %all-to-all-start.1) | async-done | bytes 196640 | tf_op jit(solution)/shard_map/all_to_all | solution.py:28
  173.6 0.7 broadcast_in_dim.48
  174.3 4.7 %all-to-all-start.2 = ((bf16[32,24,128]{2,1,0:T(8,128)(2,1)}), bf16[32,24,128]{2,1,0:T(8,128)(2,1)S(1)}, u32[]{:S(2)}, u32[]{:S(2)}) async-start(bf16[32,24,128]{2,1,0:T(8,128)(2,1)} %broadcast_in_dim.48), calls=%async_computation.2 | async-start | bytes 393216 | tf_op jit(solution)/shard_map/all_to_all | solution.py:28
  179.0 3.3 %convolution_add_fusion.3 = f32[256,1152]{0,1:T(8,128)} fusion(f32[256,1152]{0,1:T(8,128)} %fusion.154, bf16[256,1152]{1,0:T(8,128)(2,1)S(1)} %fusion.6, f32[]{:T(128)} %bitcast.72, f32[]{:T(128)} %bitcast.68, bf16[256]{0:T(256)(128)(2,1)S(1)} %copy-done.10, bf16[256]{0:T(256)(128)(2,1)S(1)} %copy-done.12, f32[256,1152]{0,1:T(8,128)S(1)} %copy.21, ...), kind=kOutput, calls=%fused_computation.5 | convolution fusion | flops 304185344 | bytes 4130824 | tf_op jit(solution)/shard_map/dot_general | solution.py:105
  182.3 4.0 %multiply_reduce_fusion = (f32[256]{0:T(256)S(1)}, f32[256,1152]{1,0:T(8,128)}) fusion(bf16[1152,1152]{1,0:T(8,128)(2,1)} %bitcast.80, bf16[272,1152]{1,0:T(8,128)(2,1)} %collective-permute-done.6), kind=kOutput, calls=%fused_computation.34 | convolution fusion | flops 680066816 | bytes 4424704 | tf_op jit(solution)/shard_map/dot_general | solution.py:101
  186.2 7.2 %all-to-all-done.2 = bf16[32,24,128]{2,1,0:T(8,128)(2,1)S(1)} async-done(((bf16[32,24,128]{2,1,0:T(8,128)(2,1)}), bf16[32,24,128]{2,1,0:T(8,128)(2,1)S(1)}, u32[]{:S(2)}, u32[]{:S(2)}) %all-to-all-start.2) | async-done | bytes 196640 | tf_op jit(solution)/shard_map/all_to_all | solution.py:28
  193.5 0.9 broadcast_in_dim.49
  194.4 12.5 %all-to-all-start.3 = ((bf16[4,704,128]{2,1,0:T(8,128)(2,1)}), bf16[4,704,128]{2,1,0:T(8,128)(2,1)S(1)}, u32[]{:S(2)}, u32[]{:S(2)}) async-start(bf16[4,704,128]{2,1,0:T(8,128)(2,1)} %broadcast_in_dim.49), calls=%async_computation.3 | async-start | bytes 1441792 | tf_op jit(solution)/shard_map/all_to_all | solution.py:28
  206.9 3.3 %convolution_add_fusion.2 = f32[256,1152]{0,1:T(8,128)} fusion(f32[256,1152]{0,1:T(8,128)} %convolution_add_fusion.3, bf16[256,1152]{1,0:T(8,128)(2,1)S(1)} %fusion.6, f32[]{:T(128)} %bitcast.71, f32[]{:T(128)} %bitcast.67, bf16[256]{0:T(256)(128)(2,1)S(1)} %copy-done.10, bf16[256]{0:T(256)(128)(2,1)S(1)} %copy-done.11, f32[256,1152]{0,1:T(8,128)S(1)} %copy-done.4, ...), kind=kOutput, calls=%fused_computation.4 | convolution fusion | flops 304185344 | bytes 4130824 | tf_op jit(solution)/shard_map/dot_general | solution.py:105
  210.2 3.0 %fusion.2 = f32[256,1152]{0,1:T(8,128)S(1)} fusion(f32[256,1152]{0,1:T(8,128)} %convolution_add_fusion.2, bf16[256,1152]{1,0:T(8,128)(2,1)S(1)} %fusion.6, f32[256,1152]{1,0:T(8,128)} %get-tuple-element.21, f32[256]{0:T(256)S(1)} %add_sqrt_fusion, f32[]{:T(128)} %bitcast.66, f32[]{:T(128)} %bitcast.70, bf16[256]{0:T(256)(128)(2,1)S(1)} %copy-done.10, ...), kind=kOutput, calls=%fused_computation.11 | convolution fusion | flops 304480256 | bytes 4130824 | tf_op jit(solution)/shard_map/dot_general | solution.py:105
  213.2 1.4 copy.31
  214.6 0.1 convert_bitcast_fusion
  214.7 0.4 copy.26
  215.1 1.6 copy.42
  (36 shorter events, 0.2 us)
Async XLA Ops:
  0.6 7.9 %copy-start.5 = (bf16[256,1152]{1,0:T(8,128)(2,1)S(1)}, bf16[256,1152]{1,0:T(8,128)(2,1)}, u32[]{:S(2)}) copy-start(bf16[256,1152]{1,0:T(8,128)(2,1)} %param.6) | copy-start | bytes 1769476
  0.6 24.8 %collective-permute-start.1 = (bf16[288,1152]{1,0:T(8,128)(2,1)}, bf16[288,1152]{1,0:T(8,128)(2,1)S(1)}, u32[]{:S(2)}, u32[]{:S(2)}) collective-permute-start(bf16[288,1152]{1,0:T(8,128)(2,1)} %param.7), channel_id=1, source_target_pairs={{0,2},{2,0},{1,3},{3,1},{4,6},{6,4},{5,7},{7,5},{8,10},{10,8},{9,1... | collective-permute-start | bytes 1990664 | tf_op jit(solution)/shard_map/ppermute | solution.py:24
  6.7 0.5 copy-start.9
  8.5 16.9 %copy-start.2 = (bf16[288,1152]{1,0:T(8,128)(2,1)S(1)}, bf16[288,1152]{1,0:T(8,128)(2,1)}, u32[]{:S(2)}) copy-start(bf16[288,1152]{1,0:T(8,128)(2,1)} %param.7) | copy-start | bytes 1990660
  9.7 28.5 %collective-permute-start.3 = (bf16[272,1152]{1,0:T(8,128)(2,1)}, bf16[272,1152]{1,0:T(8,128)(2,1)}, u32[]{:S(2)}, u32[]{:S(2)}) collective-permute-start(bf16[272,1152]{1,0:T(8,128)(2,1)} %get-tuple-element.6), channel_id=1, source_target_pairs={{4,0},{8,4},{12,8},{16,12},{20,16},{24,20},{28,24},{32,28},{36,32}... | collective-permute-start | bytes 1880072 | tf_op jit(solution)/shard_map/ppermute | solution.py:20
  25.7 44.6 %collective-permute-start.2 = (bf16[2,288,1152]{2,1,0:T(8,128)(2,1)S(1)}, bf16[2,288,1152]{2,1,0:T(8,128)(2,1)}, u32[]{:S(2)}, u32[]{:S(2)}) collective-permute-start(bf16[2,288,1152]{2,1,0:T(8,128)(2,1)S(1)} %maximum_select_fusion.2), channel_id=1, source_target_pairs={{0,1},{1,0},{2,3},{3,2},{4,5},{5,4},{6,7},{7,6},{8,9},{9,8},{10,11... | collective-permute-start | bytes 3981320 | tf_op jit(solution)/shard_map/ppermute | solution.py:24
  28.9 38.6 %collective-permute-start = (bf16[272,1152]{1,0:T(8,128)(2,1)}, bf16[272,1152]{1,0:T(8,128)(2,1)}, u32[]{:S(2)}, u32[]{:S(2)}) collective-permute-start(bf16[272,1152]{1,0:T(8,128)(2,1)} %get-tuple-element.7), channel_id=1, source_target_pairs={{508,0},{0,4},{4,8},{8,12},{12,16},{16,20},{20,24},{24,28},{28,32}... | collective-permute-start | bytes 1880072 | tf_op jit(solution)/shard_map/ppermute | solution.py:20
  38.2 30.9 %collective-permute-start.4 = (bf16[272,1152]{1,0:T(8,128)(2,1)}, bf16[272,1152]{1,0:T(8,128)(2,1)}, u32[]{:S(2)}, u32[]{:S(2)}) collective-permute-start(bf16[272,1152]{1,0:T(8,128)(2,1)} %collective-permute-done.3), channel_id=1, source_target_pairs={{4,0},{8,4},{12,8},{16,12},{20,16},{24,20},{28,24},{32,28},{36,32}... | collective-permute-start | bytes 1880072 | tf_op jit(solution)/shard_map/ppermute | solution.py:20
  70.3 2.1 copy-start.6
  72.4 2.0 copy-start
  82.6 26.9 %copy-start.3 = (f32[256,1152]{0,1:T(8,128)}, f32[256,1152]{0,1:T(8,128)S(1)}, u32[]{:S(2)}) copy-start(f32[256,1152]{0,1:T(8,128)S(1)} %copy.23) | copy-start | bytes 3538948
  84.8 0.7 copy-start.7
  85.4 1.4 copy-start.10
  99.9 6.4 %copy-start.11 = (bf16[256]{0:T(256)(128)(2,1)S(1)}, bf16[256]{0:T(256)(128)(2,1)}, u32[]{:S(2)}) copy-start(bf16[256]{0:T(256)(128)(2,1)} %slice_reduce_fusion.1) | copy-start | bytes 1540
  99.9 6.4 %copy-start.13 = (bf16[256]{0:T(256)(128)(2,1)S(1)}, bf16[256]{0:T(256)(128)(2,1)}, u32[]{:S(2)}) copy-start(bf16[256]{0:T(256)(128)(2,1)} %slice_reduce_fusion.3) | copy-start | bytes 1540
  113.6 1.5 copy-start.1
  115.1 5.3 %collective-permute-start.5 = (bf16[2,288,1152]{2,1,0:T(8,128)(2,1)S(1)}, bf16[2,288,1152]{2,1,0:T(8,128)(2,1)}, u32[]{:S(2)}, u32[]{:S(2)}) collective-permute-start(bf16[2,288,1152]{2,1,0:T(8,128)(2,1)S(1)} %dynamic-slice_bitcast_fusion), channel_id=1, source_target_pairs={{0,1},{1,0},{2,3},{3,2},{4,5},{5,4},{6,7},{7,6},{8,9},{9,8},{10,11... | collective-permute-start | bytes 3981320 | tf_op jit(solution)/shard_map/ppermute | solution.py:24
  123.5 21.6 %all-to-all-start = ((bf16[8,72,1152]{2,1,0:T(8,128)(2,1)}), bf16[8,72,1152]{2,1,0:T(8,128)(2,1)S(1)}, u32[]{:S(2)}, u32[]{:S(2)}) async-start(bf16[8,72,1152]{2,1,0:T(8,128)(2,1)} %bitcast.13), calls=%async_computation | async-start | bytes 2654208 | tf_op jit(solution)/shard_map/all_to_all | solution.py:28
  127.0 32.1 %collective-permute-start.6 = (bf16[272,1152]{1,0:T(8,128)(2,1)}, bf16[272,1152]{1,0:T(8,128)(2,1)}, u32[]{:S(2)}, u32[]{:S(2)}) collective-permute-start(bf16[272,1152]{1,0:T(8,128)(2,1)} %collective-permute-done.4), channel_id=1, source_target_pairs={{4,0},{8,4},{12,8},{16,12},{20,16},{24,20},{28,24},{32,28},{36,32}... | collective-permute-start | bytes 1880072 | tf_op jit(solution)/shard_map/ppermute | solution.py:20
  145.3 14.5 %copy-start.8 = (bf16[256,256]{1,0:T(8,128)(2,1)S(1)}, bf16[256,256]{1,0:T(8,128)(2,1)}, u32[]{:S(2)}) copy-start(bf16[256,256]{1,0:T(8,128)(2,1)} %copy-done.7) | copy-start | bytes 393220
  146.2 27.4 %all-to-all-start.1 = ((bf16[32,24,128]{2,1,0:T(8,128)(2,1)}), bf16[32,24,128]{2,1,0:T(8,128)(2,1)S(1)}, u32[]{:S(2)}, u32[]{:S(2)}) async-start(bf16[32,24,128]{2,1,0:T(8,128)(2,1)} %bitcast.16), calls=%async_computation.1 | async-start | bytes 393216 | tf_op jit(solution)/shard_map/all_to_all | solution.py:28
  159.8 19.2 %copy-start.12 = (bf16[256]{0:T(256)(128)(2,1)S(1)}, bf16[256]{0:T(256)(128)(2,1)}, u32[]{:S(2)}) copy-start(bf16[256]{0:T(256)(128)(2,1)} %slice_reduce_fusion.2) | copy-start | bytes 1540
  174.3 19.1 %all-to-all-start.2 = ((bf16[32,24,128]{2,1,0:T(8,128)(2,1)}), bf16[32,24,128]{2,1,0:T(8,128)(2,1)S(1)}, u32[]{:S(2)}, u32[]{:S(2)}) async-start(bf16[32,24,128]{2,1,0:T(8,128)(2,1)} %broadcast_in_dim.48), calls=%async_computation.2 | async-start | bytes 393216 | tf_op jit(solution)/shard_map/all_to_all | solution.py:28
  193.4 13.5 %copy-start.4 = (f32[256,1152]{0,1:T(8,128)S(1)}, f32[256,1152]{0,1:T(8,128)}, u32[]{:S(2)}) copy-start(f32[256,1152]{0,1:T(8,128)} %copy-done.3) | copy-start | bytes 3538948
  194.4 20.2 %all-to-all-start.3 = ((bf16[4,704,128]{2,1,0:T(8,128)(2,1)}), bf16[4,704,128]{2,1,0:T(8,128)(2,1)S(1)}, u32[]{:S(2)}, u32[]{:S(2)}) async-start(bf16[4,704,128]{2,1,0:T(8,128)(2,1)} %broadcast_in_dim.49), calls=%async_computation.3 | async-start | bytes 1441792 | tf_op jit(solution)/shard_map/all_to_all | solution.py:28

commit v2 on v1

v2 whole, which is shorter than its diff:
```python
import functools

import jax
import jax.numpy as jnp
from jax import lax
from jax.experimental import pallas as pl
from jax.experimental.pallas import tpu as pltpu
from jax.sharding import Mesh, PartitionSpec as P

BF = jnp.bfloat16
F32 = jnp.float32
ROWS = 256
D = 1152
SHARD = D // 4
SUB = SHARD // 4
PACKED = ROWS + 16
SPLIT = ("z2", "z1", "z0", "xh", "y2", "y1", "y0", "xl", "core")
BLK = SPLIT[:7]
NEAR = ("z0", "y0")
FAR = ("z2", "z1", "xh", "y2", "y1")
VMEM = pl.BlockSpec(memory_space=pltpu.VMEM)
SMEM = pl.BlockSpec(memory_space=pltpu.SMEM)


def shift(block, distance):
    n = 128
    return lax.ppermute(block, BLK, [((i - distance) % n, i) for i in range(n)])


def swap(block, axis):
    return lax.ppermute(block, axis, [(0, 1), (1, 0)])


def exchange(chunks, axes):
    return lax.all_to_all(chunks, axes, 0, 0, tiled=True)


def spread(chunk, axes, n):
    return exchange(jnp.broadcast_to(chunk[None], (n,) + chunk.shape), axes)


def total(chunks):
    return jnp.sum(chunks.astype(F32), 0).astype(BF)


def gather_weight(shard, after):
    xl, core = lax.axis_index("xl"), lax.axis_index("core")
    other = swap(shard, "xl")
    pair = jnp.where(xl == 0, jnp.stack([shard, other]), jnp.stack([other, shard]))
    pair = lax.optimization_barrier((pair, after))[0]
    far = swap(pair, "core")
    return jnp.where(core == 0, jnp.stack([pair, far], 1), jnp.stack([far, pair], 1)).reshape(D, D)


def call(kernel, outs, specs, flops, scratch=()):
    def run(*args):
        moved = sum(a.size * a.dtype.itemsize for a in args) + sum(
            o.size * o.dtype.itemsize for o in outs
        )
        return pl.pallas_call(
            kernel,
            out_shape=outs,
            in_specs=specs,
            out_specs=[VMEM] * len(outs),
            scratch_shapes=scratch,
            compiler_params=pltpu.CompilerParams(vmem_limit_bytes=48 * 1024 * 1024),
            cost_estimate=pl.CostEstimate(flops=flops, bytes_accessed=moved, transcendentals=0),
        )(*args)

    return run


def put_ids(ids_ref, out_ref):
    first = lax.broadcasted_iota(jnp.int32, (16, ROWS), 0) == 0
    ids = jnp.broadcast_to(ids_ref[...].astype(F32), (16, ROWS))
    out_ref[ROWS:, :ROWS] = jnp.where(first, ids, 0.0).astype(BF)
    out_ref[ROWS:, ROWS:] = jnp.zeros((16, D - ROWS), BF)


def pack_kernel(feats_ref, ids_ref, out_ref):
    out_ref[:ROWS, :] = feats_ref[...]
    put_ids(ids_ref, out_ref)


def text_kernel(text_ref, ids_ref, out_ref):
    rows = text_ref[...].astype(F32)
    inverse = 1.0 / jnp.sqrt(jnp.sum(rows * rows, -1, keepdims=True) + 1e-06)
    out_ref[:ROWS, :] = (rows * inverse).astype(BF)
    put_ids(ids_ref, out_ref)


def project(image_ref, weight_ref):
    raw = jnp.dot(image_ref[:ROWS, :], weight_ref[...], preferred_element_type=F32)
    inverse = 1.0 / jnp.sqrt(jnp.sum(raw * raw, -1, keepdims=True) + 1e-06)
    unit = raw * inverse
    return unit, unit.astype(BF), inverse


def ids_down(image_ref):
    ones = jnp.ones((16, ROWS), BF)
    return lax.dot_general(
        image_ref[ROWS:, :ROWS], ones, (((0,), (0,)), ((), ())), preferred_element_type=F32
    )


def pair(image_unit, ids, text_ref, scale, bias):
    logits = (
        scale
        * lax.dot_general(
            image_unit, text_ref[:ROWS, :], (((1,), (1,)), ((), ())), preferred_element_type=F32
        )
        + bias
    )
    match = ids == text_ref[ROWS:, :ROWS].astype(F32)[0:1, :]
    weight = 1.0 / (1.0 + jnp.exp(jnp.where(match, logits, -logits)))
    return jnp.where(match, -weight, weight).astype(BF)


def across(left, right):
    return lax.dot_general(left, right, (((0,), (0,)), ((), ())), preferred_element_type=F32)


def back(image_grad, unit, inverse):
    inner = jnp.sum(image_grad * unit, -1, keepdims=True)
    return ((image_grad - unit * inner) * inverse).astype(BF)


def front_kernel(scale_ref, bias_ref, weight_ref, image0_ref, image1_ref, text_ref, text1_ref, part_ref, grad_ref):
    scale, bias = scale_ref[0], bias_ref[0]
    unit, image_unit, inverse = project(image0_ref, weight_ref)
    ids = ids_down(image0_ref)
    near = pair(image_unit, ids, text_ref, scale, bias)
    far = pair(image_unit, ids, text1_ref, scale, bias)
    grad = across(near, image_unit)
    image_grad = scale * (
        jnp.dot(near, text_ref[:ROWS, :], preferred_element_type=F32)
        + jnp.dot(far, text1_ref[:ROWS, :], preferred_element_type=F32)
    )
    part_ref[...] = across(image0_ref[:ROWS, :], back(image_grad, unit, inverse))
    unit, image_unit, inverse = project(image1_ref, weight_ref)
    ids = ids_down(image1_ref)
    near = pair(image_unit, ids, text_ref, scale, bias)
    far = pair(image_unit, ids, text1_ref, scale, bias)
    grad_ref[...] = scale * (grad + across(near, image_unit))
    image_grad = scale * jnp.dot(far, text1_ref[:ROWS, :], preferred_element_type=F32)
    part_ref[...] += across(image1_ref[:ROWS, :], back(image_grad, unit, inverse))


def last_kernel(core_ref, scale_ref, bias_ref, weight_ref, image_ref, text1_ref, part_ref, keep_ref, send_ref, sum_ref, sem):
    scale, bias = scale_ref[0], bias_ref[0]
    load = pltpu.make_async_copy(part_ref, sum_ref, sem)
    load.start()
    unit, image_unit, inverse = project(image_ref, weight_ref)
    far = pair(image_unit, ids_down(image_ref), text1_ref, scale, bias)
    image_grad = scale * jnp.dot(far, text1_ref[:ROWS, :], preferred_element_type=F32)
    raw_grad = back(image_grad, unit, inverse)
    load.wait()
    sum_ref[...] += across(image_ref[:ROWS, :], raw_grad)
    core = core_ref[0]
    for half in range(2):
        for out_ref, quarter in ((keep_ref, core), (send_ref, 1 - core)):
            at = pl.multiple_of((2 * half + quarter) * SHARD, 32)
            out_ref[half * SHARD : (half + 1) * SHARD, :] = sum_ref[pl.ds(at, SHARD), :].astype(BF)


def finish_kernel(scale_ref, bias_ref, weight_ref, image2_ref, image3_ref, text_ref, grad_ref, out_ref):
    scale, bias = scale_ref[0], bias_ref[0]
    grad = None
    for image_ref in (image2_ref, image3_ref):
        _, image_unit, _ = project(image_ref, weight_ref)
        near = pair(image_unit, ids_down(image_ref), text_ref, scale, bias)
        term = across(near, image_unit)
        grad = term if grad is None else grad + term
    out_ref[...] = grad_ref[...] + scale * grad


def shape(rows, columns, dtype):
    return jax.ShapeDtypeStruct((rows, columns), dtype)


def on_device(feats, proj_weight, text_embed, row_ids, logit_scale, logit_bias):
    ids = row_ids.reshape(1, ROWS)
    packed = shape(PACKED, D, BF)
    core = lax.axis_index("core").astype(jnp.int32).reshape(1)
    image0 = call(pack_kernel, [packed], [VMEM] * 2, ROWS)(feats, ids)[0]
    image0, text_embed = lax.optimization_barrier((image0, text_embed))
    image1 = shift(image0, -1)
    text0 = call(text_kernel, [packed], [VMEM] * 2, ROWS)(text_embed, ids)[0]
    proj_weight, text0 = lax.optimization_barrier((proj_weight, text0))
    text1 = shift(text0, 1)
    weight = gather_weight(proj_weight, (image1, text1))
    image2 = shift(image1, -1)
    project_flops = 2 * ROWS * D * D
    part, grad = call(
        front_kernel,
        [shape(D, D, F32), shape(ROWS, D, F32)],
        [SMEM] * 2 + [VMEM] * 5,
        4 * project_flops,
    )(logit_scale, logit_bias, weight, image0, image1, text0, text1)
    keep, send = call(
        last_kernel,
        [shape(2 * SHARD, D, BF)] * 2,
        [SMEM] * 3 + [VMEM] * 3 + [pl.BlockSpec(memory_space=pl.ANY)],
        2 * project_flops,
        [pltpu.VMEM((D, D), F32), pltpu.SemaphoreType.DMA],
    )(core, logit_scale, logit_bias, weight, image2, text1, part)
    halves = (keep.astype(F32) + swap(send, "core").astype(F32)).astype(BF)
    mine = total(exchange(halves.reshape(8, SUB, D), ("xl",) + NEAR))
    mine, image2 = lax.optimization_barrier((mine, image2))
    tiles = mine.reshape(SUB, 9, 128).transpose(1, 0, 2).reshape(SUB * 9, 128)
    tiles = jnp.pad(tiles, ((0, 768 - SUB * 9), (0, 0))).reshape(32, 24, 128)
    done = total(exchange(tiles, FAR))
    image3 = shift(image2, -1)
    done = spread(done, FAR, 32).reshape(768, 128)[:704]
    done, image3 = lax.optimization_barrier((done, image3))
    done = spread(done, NEAR, 4)[:, : SUB * 9]
    weight_grad = done.reshape(4, 9, SUB, 128).transpose(0, 2, 1, 3).reshape(SHARD, D).astype(F32)
    text_grad = call(
        finish_kernel, [shape(ROWS, D, F32)], [SMEM] * 2 + [VMEM] * 5, 2 * project_flops
    )(logit_scale, logit_bias, weight, image2, image3, text0, grad)[0]
    return (weight_grad, text_grad)


def solution(mesh):
    fine = Mesh(mesh.devices.reshape((2,) * 9), SPLIT)
    grp = SPLIT[7:]
    return jax.shard_map(
        on_device,
        mesh=fine,
        in_specs=(P(SPLIT, None), P(grp, None), P(SPLIT, None), P(SPLIT), P(), P()),
        out_specs=(P(grp, None), P(SPLIT, None)),
        check_vma=False,
    )
```

time: 220 us -> 170 us (0.77)
  the two profiles are of different devices: /device:TPU:1 before, /device:TPU:8 now
where the time goes in v2:
time: 170 us
  blocking collectives  53.4 us (31%)
  starting transfers between devices  45.8 us (27%)
  waiting for transfers between devices  25.9 us (15%)
  Pallas kernels  24.3 us (14%)
  local copies, waits for them, and re-layouts  11.7 us (7%)
  other arithmetic  6.3 us (4%)
  between operations  2.12 us (1%)
    all_to_all x2, blocking collectives, exchange(): return lax.all_to_all(chunks, axes, 0, 0, tiled=True)  53.4 us
    pallas_call x5, Pallas kernels, run(): pl.pallas_call(kernel, out_shape=outs, in_specs=specs, out_specs=[VMEM] *...  24.3 us
    ppermute x4, starting transfers between devices, shift(): return lax.ppermute(block, BLK, [((i - distance) % n, i) for i in range(n)])  24.2 us
    all_to_all x2, starting transfers between devices, exchange(): return lax.all_to_all(chunks, axes, 0, 0, tiled=True)  14.1 us
    all_to_all x2, waiting for transfers between devices, exchange(): return lax.all_to_all(chunks, axes, 0, 0, tiled=True)  13.1 us
    ppermute x3, waiting for transfers between devices, swap(): return lax.ppermute(block, axis, [(0, 1), (1, 0)])  9.86 us
    ppermute x3, starting transfers between devices, swap(): return lax.ppermute(block, axis, [(0, 1), (1, 0)])  7.44 us
    unnamed x15, local copies, waits for them, and re-layouts  6.67 us
  transfers between devices with their start and end apart: 9, of which 4 were waited for; matrix products, arithmetic and copies ran while one was open for 4% of the time, Pallas kernels for 10%

profile of v2, /device:TPU:8, one launch (start us, length us, event | category | flops | bytes accessed | tf_op | source)
XLA Modules:
  0.0 169.5 jit_solution(12109334382970864462)
XLA Ops:
  0.6 0.0 copy-start.3
  0.6 1.1 copy-done.3
  1.7 0.0 copy-start.5
  1.7 0.7 copy-done.5
  2.4 0.0 copy-start.4
  2.4 0.0 copy-start.6
  2.4 1.0 copy-done.4
  3.4 0.2 shard_map.78.text_ref
  3.7 0.0 copy-done.6
  3.7 3.4 %collective-permute-start = (bf16[288,1152]{1,0:T(8,128)(2,1)S(1)}, bf16[288,1152]{1,0:T(8,128)(2,1)}, u32[]{:S(2)}, u32[]{:S(2)}) collective-permute-start(bf16[288,1152]{1,0:T(8,128)(2,1)S(1)} %copy-done.6), channel_id=1, source_target_pairs={{0,2},{2,0},{1,3},{3,1},{4,6},{6,4},{5,7},{7,5},{8,10},{10,8},{9,1... | collective-permute-start | bytes 1990664 | tf_op jit(solution)/shard_map/ppermute | solution.py:31
  7.1 3.5 %collective-permute-start.2 = (bf16[272,1152]{1,0:T(8,128)(2,1)S(1)}, bf16[272,1152]{1,0:T(8,128)(2,1)S(1)}, u32[]{:S(2)}, u32[]{:S(2)}) collective-permute-start(bf16[272,1152]{1,0:T(8,128)(2,1)S(1)} %shard_map.78.text_ref), channel_id=1, source_target_pairs={{508,0},{0,4},{4,8},{8,12},{12,16},{16,20},{20,24},{24,28},{28,32}... | collective-permute-start | bytes 1880072 | tf_op jit(solution)/shard_map/ppermute | solution.py:27
  10.6 4.7 %collective-permute-start.1 = (bf16[272,1152]{1,0:T(8,128)(2,1)S(1)}, bf16[272,1152]{1,0:T(8,128)(2,1)S(1)}, u32[]{:S(2)}, u32[]{:S(2)}) collective-permute-start(bf16[272,1152]{1,0:T(8,128)(2,1)S(1)} %shard_map.77.image0_ref), channel_id=1, source_target_pairs={{4,0},{8,4},{12,8},{16,12},{20,16},{24,20},{28,24},{32,28},{36,32}... | collective-permute-start | bytes 1880072 | tf_op jit(solution)/shard_map/ppermute | solution.py:27
  15.3 7.0 %collective-permute-done = bf16[288,1152]{1,0:T(8,128)(2,1)} collective-permute-done((bf16[288,1152]{1,0:T(8,128)(2,1)S(1)}, bf16[288,1152]{1,0:T(8,128)(2,1)}, u32[]{:S(2)}, u32[]{:S(2)}) %collective-permute-start) | collective-permute-done | bytes 663584 | tf_op jit(solution)/shard_map/ppermute | solution.py:31
  22.3 2.6 %maximum_select_fusion.1 = bf16[2,288,1152]{2,1,0:T(8,128)(2,1)} fusion(bf16[1,288,1152]{2,1,0:T(8,128)(2,1)} %bitcast.3, bf16[1,288,1152]{2,1,0:T(8,128)(2,1)S(1)} %bitcast.33, pred[]{:T(512)S(6)} %eq.7), kind=kLoop, calls=%fused_computation.3 | loop fusion | flops 1990656 | bytes 2654209 | tf_op jit(solution)/shard_map/jit(_where)/select_n | solution.py:49
  24.9 0.0 collective-permute-done.2.text1_ref
  24.9 2.9 %collective-permute-done.1.image1_ref = bf16[272,1152]{1,0:T(8,128)(2,1)S(1)} collective-permute-done((bf16[272,1152]{1,0:T(8,128)(2,1)S(1)}, bf16[272,1152]{1,0:T(8,128)(2,1)S(1)}, u32[]{:S(2)}, u32[]{:S(2)}) %collective-permute-start.1) | collective-permute-done | bytes 626720 | tf_op jit(solution)/shard_map/ppermute | solution.py:27
  27.8 1.9 %collective-permute-start.3 = (bf16[2,288,1152]{2,1,0:T(8,128)(2,1)}, bf16[2,288,1152]{2,1,0:T(8,128)(2,1)}, u32[]{:S(2)}, u32[]{:S(2)}) collective-permute-start(bf16[2,288,1152]{2,1,0:T(8,128)(2,1)} %maximum_select_fusion.1), channel_id=1, source_target_pairs={{0,1},{1,0},{2,3},{3,2},{4,5},{5,4},{6,7},{7,6},{8,9},{9,8},{10,11... | collective-permute-start | bytes 3981320 | tf_op jit(solution)/shard_map/ppermute | solution.py:31
  31.0 12.7 %collective-permute-start.4 = (bf16[272,1152]{1,0:T(8,128)(2,1)S(1)}, bf16[272,1152]{1,0:T(8,128)(2,1)}, u32[]{:S(2)}, u32[]{:S(2)}) collective-permute-start(bf16[272,1152]{1,0:T(8,128)(2,1)S(1)} %collective-permute-done.1.image1_ref), channel_id=1, source_target_pairs={{4,0},{8,4},{12,8},{16,12},{20,16},{24,20},{28,24},{32,28},{36,32}... | collective-permute-start | bytes 1880072 | tf_op jit(solution)/shard_map/ppermute | solution.py:27
  43.7 0.0 collective-permute-done.3
  43.7 3.1 %maximum_select_fusion = bf16[2,2,288,1152]{3,2,0,1:T(8,128)(2,1)S(1)} fusion(bf16[2,1,288,1152]{3,2,0,1:T(8,128)(2,1)} %bitcast.5, bf16[2,1,288,1152]{3,2,0,1:T(8,128)(2,1)} %bitcast.4, pred[]{:T(512)S(6)} %eq.6), kind=kLoop, calls=%fused_computation | loop fusion | flops 3981312 | bytes 5308417 | tf_op jit(solution)/shard_map/jit(_where)/select_n | solution.py:52
  46.8 1.7 copy.9
  48.5 10.7 %shard_map.79 = (f32[1152,1152]{1,0:T(8,128)}, f32[256,1152]{1,0:T(8,128)S(1)}) custom-call(f32[1]{0:T(128)S(6)} %copy.15.scale_ref, f32[1]{0:T(128)S(6)} %copy.16.bias_ref, bf16[1152,1152]{1,0:T(8,128)(2,1)} %bitcast.21, bf16[272,1152]{1,0:T(8,128)(2,1)S(1)} %shard_map.77.image0_ref, bf16[272,1152]{1,0:T(8,128)(2,1)S(1)} %collective-permute-done.1.image1_ref, ...), custom_call_target="tpu_custom_call" | custom-call | flops 2717908992 | bytes 11649032 | tf_op jit(solution)/shard_map/pallas_call | solution.py:60
  59.2 0.0 copy-start.1
  59.2 1.0 copy-done.1
  60.2 0.0 collective-permute-done.4.image_ref.image2_ref
  60.2 7.4 %shard_map.80 = (bf16[576,1152]{1,0:T(8,128)(2,1)S(1)}, bf16[576,1152]{1,0:T(8,128)(2,1)S(1)}) custom-call(s32[1]{0:T(128)} %bitcast.core_ref, f32[1]{0:T(128)S(6)} %copy.15.scale_ref, f32[1]{0:T(128)S(6)} %copy.16.bias_ref, bf16[1152,1152]{1,0:T(8,128)(2,1)} %bitcast.22, bf16[272,1152]{1,0:T(8,128)(2,1)} %collective-permute-done.4.image_ref.image2_ref, ...), custom_call_target="tpu_custom_call" | custom-call | flops 1358954496 | bytes 11870220 | tf_op jit(solution)/shard_map/pallas_call | solution.py:60
  67.6 2.1 %collective-permute-start.5 = (bf16[576,1152]{1,0:T(8,128)(2,1)S(1)}, bf16[576,1152]{1,0:T(8,128)(2,1)S(1)}, u32[]{:S(2)}, u32[]{:S(2)}) collective-permute-start(bf16[576,1152]{1,0:T(8,128)(2,1)S(1)} %get-tuple-element.22), channel_id=1, source_target_pairs={{0,1},{1,0},{2,3},{3,2},{4,5},{5,4},{6,7},{7,6},{8,9},{9,8},{10,11... | collective-permute-start | bytes 3981320 | tf_op jit(solution)/shard_map/ppermute | solution.py:31
  69.8 2.8 %collective-permute-done.5 = bf16[576,1152]{1,0:T(8,128)(2,1)S(1)} collective-permute-done((bf16[576,1152]{1,0:T(8,128)(2,1)S(1)}, bf16[576,1152]{1,0:T(8,128)(2,1)S(1)}, u32[]{:S(2)}, u32[]{:S(2)}) %collective-permute-start.5) | collective-permute-done | bytes 1327136 | tf_op jit(solution)/shard_map/ppermute | solution.py:31
  72.6 0.3 add_convert_fusion
  72.9 34.6 %all_to_all.20 = bf16[8,72,1152]{2,1,0:T(8,128)(2,1)S(1)} all-to-all(bf16[8,72,1152]{2,1,0:T(8,128)(2,1)S(1)} %bitcast.27), channel_id=1, replica_groups=mesh['z2'=2,'z1'=2,'z0'=2,'xh'=2,'y2'=2,'y1'=2,'y0'=2,'xl'=2,'core'=2] {..., dimensions={0} | all-to-all | bytes 2654208 | tf_op jit(solution)/shard_map/all_to_all | solution.py:35
  107.5 0.2 reduce_sum.24
  107.7 0.1 reshape.41
  107.9 0.7 pad.4
  108.6 8.7 %all-to-all-start.1 = ((bf16[32,24,128]{2,1,0:T(8,128)(2,1)}), bf16[32,24,128]{2,1,0:T(8,128)(2,1)S(1)}, u32[]{:S(2)}, u32[]{:S(2)}) async-start(bf16[32,24,128]{2,1,0:T(8,128)(2,1)} %bitcast.10), calls=%async_computation.1 | async-start | bytes 393216 | tf_op jit(solution)/shard_map/all_to_all | solution.py:35
  117.3 3.4 %collective-permute-start.6 = (bf16[272,1152]{1,0:T(8,128)(2,1)}, bf16[272,1152]{1,0:T(8,128)(2,1)}, u32[]{:S(2)}, u32[]{:S(2)}) collective-permute-start(bf16[272,1152]{1,0:T(8,128)(2,1)} %collective-permute-done.4.image_ref.image2_ref), channel_id=1, source_target_pairs={{4,0},{8,4},{12,8},{16,12},{20,16},{24,20},{28,24},{32,28},{36,32}... | collective-permute-start | bytes 1880072 | tf_op jit(solution)/shard_map/ppermute | solution.py:27
  120.7 13.1 %all-to-all-done.1 = bf16[32,24,128]{2,1,0:T(8,128)(2,1)S(1)} async-done(((bf16[32,24,128]{2,1,0:T(8,128)(2,1)}), bf16[32,24,128]{2,1,0:T(8,128)(2,1)S(1)}, u32[]{:S(2)}, u32[]{:S(2)}) %all-to-all-start.1) | async-done | bytes 196640 | tf_op jit(solution)/shard_map/all_to_all | solution.py:35
  133.9 18.8 %all_to_all.21 = bf16[32,24,128]{2,1,0:T(8,128)(2,1)S(1)} all-to-all(bf16[32,24,128]{2,1,0:T(8,128)(2,1)S(1)} %broadcast_in_dim.4), channel_id=1, replica_groups=mesh['z2'=2,'z1'=2,'z0'=2,'xh'=2,'y2'=2,'y1'=2,'y0'=2,'xl'=2,'core'=2] {..., dimensions={0} | all-to-all | bytes 393216 | tf_op jit(solution)/shard_map/all_to_all | solution.py:35
  152.7 0.0 copy-start
  152.7 0.0 collective-permute-done.6.image3_ref
  152.7 1.0 broadcast_in_dim.5
  153.7 5.3 %all-to-all-start.3 = ((bf16[4,704,128]{2,1,0:T(8,128)(2,1)}), bf16[4,704,128]{2,1,0:T(8,128)(2,1)}, u32[]{:S(2)}, u32[]{:S(2)}) async-start(bf16[4,704,128]{2,1,0:T(8,128)(2,1)} %broadcast_in_dim.5), calls=%async_computation.3 | async-start | bytes 1441792 | tf_op jit(solution)/shard_map/all_to_all | solution.py:35
  159.0 0.0 copy-done
  159.0 0.0 copy-start.2
  159.0 1.3 copy-done.2
  160.3 5.9 %shard_map.81 = f32[256,1152]{1,0:T(8,128)} custom-call(f32[1]{0:T(128)S(6)} %copy.15.scale_ref, f32[1]{0:T(128)S(6)} %copy.16.bias_ref, bf16[1152,1152]{1,0:T(8,128)(2,1)S(1)} %bitcast.23, bf16[272,1152]{1,0:T(8,128)(2,1)} %collective-permute-done.4.image_ref.image2_ref, bf16[272,1152]{1,0:T(8,128)(2,1)} %collective-permute-done.6.image3_ref, ...), custom_call_target="tpu_custom_call" | custom-call | flops 1358954496 | bytes 6893576 | tf_op jit(solution)/shard_map/pallas_call | solution.py:60
  166.3 0.0 all-to-all-done.3
  166.3 1.1 slice.9
  167.4 0.1 convert_bitcast_fusion
  167.5 0.4 copy.11
  167.9 1.6 copy.14
  (5 shorter events, 0.2 us)
Async XLA Ops:
  0.6 1.1 copy-start.3
  1.7 0.7 copy-start.5
  2.4 1.1 copy-start.4
  2.4 1.3 copy-start.6
  3.7 18.6 %collective-permute-start = (bf16[288,1152]{1,0:T(8,128)(2,1)S(1)}, bf16[288,1152]{1,0:T(8,128)(2,1)}, u32[]{:S(2)}, u32[]{:S(2)}) collective-permute-start(bf16[288,1152]{1,0:T(8,128)(2,1)S(1)} %copy-done.6), channel_id=1, source_target_pairs={{0,2},{2,0},{1,3},{3,1},{4,6},{6,4},{5,7},{7,5},{8,10},{10,8},{9,1... | collective-permute-start | bytes 1990664 | tf_op jit(solution)/shard_map/ppermute | solution.py:31
  7.1 17.8 %collective-permute-start.2 = (bf16[272,1152]{1,0:T(8,128)(2,1)S(1)}, bf16[272,1152]{1,0:T(8,128)(2,1)S(1)}, u32[]{:S(2)}, u32[]{:S(2)}) collective-permute-start(bf16[272,1152]{1,0:T(8,128)(2,1)S(1)} %shard_map.78.text_ref), channel_id=1, source_target_pairs={{508,0},{0,4},{4,8},{8,12},{12,16},{16,20},{20,24},{24,28},{28,32}... | collective-permute-start | bytes 1880072 | tf_op jit(solution)/shard_map/ppermute | solution.py:27
  10.6 17.2 %collective-permute-start.1 = (bf16[272,1152]{1,0:T(8,128)(2,1)S(1)}, bf16[272,1152]{1,0:T(8,128)(2,1)S(1)}, u32[]{:S(2)}, u32[]{:S(2)}) collective-permute-start(bf16[272,1152]{1,0:T(8,128)(2,1)S(1)} %shard_map.77.image0_ref), channel_id=1, source_target_pairs={{4,0},{8,4},{12,8},{16,12},{20,16},{24,20},{28,24},{32,28},{36,32}... | collective-permute-start | bytes 1880072 | tf_op jit(solution)/shard_map/ppermute | solution.py:27
  27.8 15.9 %collective-permute-start.3 = (bf16[2,288,1152]{2,1,0:T(8,128)(2,1)}, bf16[2,288,1152]{2,1,0:T(8,128)(2,1)}, u32[]{:S(2)}, u32[]{:S(2)}) collective-permute-start(bf16[2,288,1152]{2,1,0:T(8,128)(2,1)} %maximum_select_fusion.1), channel_id=1, source_target_pairs={{0,1},{1,0},{2,3},{3,2},{4,5},{5,4},{6,7},{7,6},{8,9},{9,8},{10,11... | collective-permute-start | bytes 3981320 | tf_op jit(solution)/shard_map/ppermute | solution.py:31
  31.0 29.2 %collective-permute-start.4 = (bf16[272,1152]{1,0:T(8,128)(2,1)S(1)}, bf16[272,1152]{1,0:T(8,128)(2,1)}, u32[]{:S(2)}, u32[]{:S(2)}) collective-permute-start(bf16[272,1152]{1,0:T(8,128)(2,1)S(1)} %collective-permute-done.1.image1_ref), channel_id=1, source_target_pairs={{4,0},{8,4},{12,8},{16,12},{20,16},{24,20},{28,24},{32,28},{36,32}... | collective-permute-start | bytes 1880072 | tf_op jit(solution)/shard_map/ppermute | solution.py:27
  59.2 1.0 copy-start.1
  67.6 5.0 %collective-permute-start.5 = (bf16[576,1152]{1,0:T(8,128)(2,1)S(1)}, bf16[576,1152]{1,0:T(8,128)(2,1)S(1)}, u32[]{:S(2)}, u32[]{:S(2)}) collective-permute-start(bf16[576,1152]{1,0:T(8,128)(2,1)S(1)} %get-tuple-element.22), channel_id=1, source_target_pairs={{0,1},{1,0},{2,3},{3,2},{4,5},{5,4},{6,7},{7,6},{8,9},{9,8},{10,11... | collective-permute-start | bytes 3981320 | tf_op jit(solution)/shard_map/ppermute | solution.py:31
  108.6 25.3 %all-to-all-start.1 = ((bf16[32,24,128]{2,1,0:T(8,128)(2,1)}), bf16[32,24,128]{2,1,0:T(8,128)(2,1)S(1)}, u32[]{:S(2)}, u32[]{:S(2)}) async-start(bf16[32,24,128]{2,1,0:T(8,128)(2,1)} %bitcast.10), calls=%async_computation.1 | async-start | bytes 393216 | tf_op jit(solution)/shard_map/all_to_all | solution.py:35
  117.3 35.4 %collective-permute-start.6 = (bf16[272,1152]{1,0:T(8,128)(2,1)}, bf16[272,1152]{1,0:T(8,128)(2,1)}, u32[]{:S(2)}, u32[]{:S(2)}) collective-permute-start(bf16[272,1152]{1,0:T(8,128)(2,1)} %collective-permute-done.4.image_ref.image2_ref), channel_id=1, source_target_pairs={{4,0},{8,4},{12,8},{16,12},{20,16},{24,20},{28,24},{32,28},{36,32}... | collective-permute-start | bytes 1880072 | tf_op jit(solution)/shard_map/ppermute | solution.py:27
  152.7 6.3 %copy-start = (bf16[2,2,288,1152]{3,2,1,0:T(8,128)(2,1)S(1)}, bf16[2,2,288,1152]{3,2,1,0:T(8,128)(2,1)}, u32[]{:S(2)}) copy-start(bf16[2,2,288,1152]{3,2,1,0:T(8,128)(2,1)} %copy.9) | copy-start | bytes 7962628
  153.7 12.6 %all-to-all-start.3 = ((bf16[4,704,128]{2,1,0:T(8,128)(2,1)}), bf16[4,704,128]{2,1,0:T(8,128)(2,1)}, u32[]{:S(2)}, u32[]{:S(2)}) async-start(bf16[4,704,128]{2,1,0:T(8,128)(2,1)} %broadcast_in_dim.5), calls=%async_computation.3 | async-start | bytes 1441792 | tf_op jit(solution)/shard_map/all_to_all | solution.py:35
  159.0 1.3 copy-start.2

commit v3 on v2

v3 whole, which is shorter than its diff:
```python
import jax
import jax.numpy as jnp
from jax import lax
from jax.experimental import pallas as pl
from jax.experimental.pallas import tpu as pltpu
from jax.sharding import PartitionSpec as P

BF = jnp.bfloat16
F32 = jnp.float32
ROWS = 256
D = 1152
SHARD = D // 4
SUB = SHARD // 4
PACKED = ROWS + 16
N = 512
AXIS = ("blk", "grp")
VMEM = pl.BlockSpec(memory_space=pltpu.VMEM)
SMEM = pl.BlockSpec(memory_space=pltpu.SMEM)


def coordinates(device):
    blk, grp = divmod(device, 4)
    return blk // 16, (blk // 8) % 2 * 2 + grp // 2, blk % 8, grp % 2


def device_at(z, x, y, core):
    return ((z % 8 * 2 + x % 4 // 2) * 8 + y % 8) * 4 + x % 2 * 2 + core


def swap_x(flips):
    moves = []
    for device in range(N):
        z, x, y, core = coordinates(device)
        moves.append((device_at(z, x ^ flips[core], y, core), device))
    return moves


def grouped(same, place):
    groups = {}
    for device in range(N):
        z, x, y, core = coordinates(device)
        key = (z + core) % 8, (x + core) % 4, (y + core) % 8, x % 2, core
        groups.setdefault(same(*key), []).append((place(*key), device))
    return [[device for _, device in sorted(group)] for group in groups.values()]


FIRST = grouped(lambda z, x, y, xl, core: (z // 2, x // 2, y // 2, core), lambda z, x, y, xl, core: (xl, z % 2, y % 2))
NEAR = grouped(lambda z, x, y, xl, core: (z // 2, x, y // 2, core), lambda z, x, y, xl, core: (z % 2, y % 2))
FAR = grouped(lambda z, x, y, xl, core: (z % 2, x, y % 2, core), lambda z, x, y, xl, core: (z // 2, y // 2))
CORES = [(i ^ 1, i) for i in range(N)]


def shift(block, distance):
    return lax.ppermute(block, AXIS, [((i - 4 * distance) % N, i) for i in range(N)])


def move(block, moves):
    return lax.ppermute(block, AXIS, moves)


def exchange(chunks, groups):
    return lax.all_to_all(chunks, AXIS, 0, 0, axis_index_groups=groups, tiled=True)


def spread(chunk, groups):
    return exchange(jnp.broadcast_to(chunk[None], (len(groups[0]),) + chunk.shape), groups)


def total(chunks):
    return jnp.sum(chunks.astype(F32), 0).astype(BF)


def call(kernel, outs, specs, flops, scratch=()):
    def run(*args):
        moved = sum(a.size * a.dtype.itemsize for a in args) + sum(
            o.size * o.dtype.itemsize for o in outs
        )
        return pl.pallas_call(
            kernel,
            out_shape=outs,
            in_specs=specs,
            out_specs=[VMEM] * len(outs),
            scratch_shapes=scratch,
            compiler_params=pltpu.CompilerParams(vmem_limit_bytes=48 * 1024 * 1024),
            cost_estimate=pl.CostEstimate(flops=flops, bytes_accessed=moved, transcendentals=0),
        )(*args)

    return run


def put_ids(ids_ref, out_ref):
    first = lax.broadcasted_iota(jnp.int32, (16, ROWS), 0) == 0
    ids = jnp.broadcast_to(ids_ref[...].astype(F32), (16, ROWS))
    out_ref[ROWS:, :ROWS] = jnp.where(first, ids, 0.0).astype(BF)
    out_ref[ROWS:, ROWS:] = jnp.zeros((16, D - ROWS), BF)


def prepare_kernel(feats_ref, text_ref, ids_ref, image_ref, out_ref):
    image_ref[:ROWS, :] = feats_ref[...]
    put_ids(ids_ref, image_ref)
    rows = text_ref[...].astype(F32)
    inverse = 1.0 / jnp.sqrt(jnp.sum(rows * rows, -1, keepdims=True) + 1e-06)
    out_ref[:ROWS, :] = (rows * inverse).astype(BF)
    put_ids(ids_ref, out_ref)


def project(image_ref, weight_ref):
    raw = jnp.dot(image_ref[:ROWS, :], weight_ref[...], preferred_element_type=F32)
    inverse = 1.0 / jnp.sqrt(jnp.sum(raw * raw, -1, keepdims=True) + 1e-06)
    unit = raw * inverse
    return unit, unit.astype(BF), inverse


def ids_down(image_ref):
    ones = jnp.ones((16, ROWS), BF)
    return lax.dot_general(
        image_ref[ROWS:, :ROWS], ones, (((0,), (0,)), ((), ())), preferred_element_type=F32
    )


def pair(image_unit, ids, text_ref, scale, bias):
    logits = (
        scale
        * lax.dot_general(
            image_unit, text_ref[:ROWS, :], (((1,), (1,)), ((), ())), preferred_element_type=F32
        )
        + bias
    )
    match = ids == text_ref[ROWS:, :ROWS].astype(F32)[0:1, :]
    weight = 1.0 / (1.0 + jnp.exp(jnp.where(match, logits, -logits)))
    return jnp.where(match, -weight, weight).astype(BF)


def across(left, right):
    return lax.dot_general(left, right, (((0,), (0,)), ((), ())), preferred_element_type=F32)


def back(image_grad, unit, inverse):
    inner = jnp.sum(image_grad * unit, -1, keepdims=True)
    return ((image_grad - unit * inner) * inverse).astype(BF)


def own_kernel(
    grp_ref, scale_ref, bias_ref, shard0_ref, shard1_ref, shard2_ref, shard3_ref, image_ref, text_ref, weight_ref, raw_grad_ref, grad_ref
):
    grp = grp_ref[0]
    for flip, shard_ref in enumerate((shard0_ref, shard1_ref, shard2_ref, shard3_ref)):
        weight_ref[pl.ds(pl.multiple_of((grp ^ flip) * SHARD, 32), SHARD), :] = shard_ref[...]
    scale, bias = scale_ref[0], bias_ref[0]
    unit, image_unit, inverse = project(image_ref, weight_ref)
    near = pair(image_unit, ids_down(image_ref), text_ref, scale, bias)
    grad_ref[...] = across(near, image_unit)
    image_grad = scale * jnp.dot(near, text_ref[:ROWS, :], preferred_element_type=F32)
    raw_grad_ref[...] = back(image_grad, unit, inverse)


def next_kernel(
    scale_ref, bias_ref, weight_ref, image0_ref, raw_grad0_ref, image1_ref, text_ref, text1_ref, grad0_ref, part_ref, grad_ref
):
    scale, bias = scale_ref[0], bias_ref[0]
    unit, image_unit, inverse = project(image1_ref, weight_ref)
    ids = ids_down(image1_ref)
    near = pair(image_unit, ids, text_ref, scale, bias)
    far = pair(image_unit, ids, text1_ref, scale, bias)
    grad_ref[...] = grad0_ref[...] + across(near, image_unit)
    image_grad = scale * (
        jnp.dot(near, text_ref[:ROWS, :], preferred_element_type=F32)
        + jnp.dot(far, text1_ref[:ROWS, :], preferred_element_type=F32)
    )
    raw_grad = back(image_grad, unit, inverse)
    part_ref[...] = across(image0_ref[:ROWS, :], raw_grad0_ref[...])
    part_ref[...] += across(image1_ref[:ROWS, :], raw_grad)


def load_quarters(core, part_ref, rows_ref, sems):
    loads = []
    for half in range(2):
        at = pl.multiple_of((2 * half + core) * SHARD, 32)
        loads.append(
            pltpu.make_async_copy(
                part_ref.at[pl.ds(at, SHARD), :],
                rows_ref.at[pl.ds(half * SHARD, SHARD), :],
                sems.at[half],
            )
        )
    for load in loads:
        load.start()
    return loads


def add_quarters(core, turned_ref, raw_grad, rows_ref, loads, out_ref):
    for half in range(2):
        at = pl.multiple_of((2 * half + core) * SHARD, 32)
        rows = pl.ds(half * SHARD, SHARD)
        term = jnp.dot(turned_ref[pl.ds(at, SHARD), :], raw_grad, preferred_element_type=F32)
        loads[half].wait()
        out_ref[rows, :] = (rows_ref[rows, :] + term).astype(BF)


def last_kernel(
    grp_ref, scale_ref, bias_ref, weight_ref, image_ref, text1_ref, part_ref, send_ref, turned_ref, raw_grad_ref, rows_ref, sems
):
    core = 1 - grp_ref[0] % 2
    loads = load_quarters(core, part_ref, rows_ref, sems)
    scale, bias = scale_ref[0], bias_ref[0]
    turned_ref[...] = image_ref[:ROWS, :].astype(F32).T.astype(BF)
    unit, image_unit, inverse = project(image_ref, weight_ref)
    far = pair(image_unit, ids_down(image_ref), text1_ref, scale, bias)
    image_grad = scale * jnp.dot(far, text1_ref[:ROWS, :], preferred_element_type=F32)
    raw_grad = back(image_grad, unit, inverse)
    raw_grad_ref[...] = raw_grad
    add_quarters(core, turned_ref, raw_grad, rows_ref, loads, send_ref)


def keep_kernel(grp_ref, turned_ref, raw_grad_ref, part_ref, keep_ref, rows_ref, sems):
    core = grp_ref[0] % 2
    loads = load_quarters(core, part_ref, rows_ref, sems)
    add_quarters(core, turned_ref, raw_grad_ref[...], rows_ref, loads, keep_ref)


def finish_kernel(scale_ref, bias_ref, weight_ref, image2_ref, image3_ref, text_ref, grad_ref, out_ref):
    scale, bias = scale_ref[0], bias_ref[0]
    grad = None
    for image_ref in (image2_ref, image3_ref):
        _, image_unit, _ = project(image_ref, weight_ref)
        near = pair(image_unit, ids_down(image_ref), text_ref, scale, bias)
        term = across(near, image_unit)
        grad = term if grad is None else grad + term
    out_ref[...] = scale * (grad_ref[...] + grad)


def shape(rows, columns, dtype):
    return jax.ShapeDtypeStruct((rows, columns), dtype)


def on_device(feats, proj_weight, text_embed, row_ids, logit_scale, logit_bias):
    packed = shape(PACKED, D, BF)
    grp = lax.axis_index("grp").astype(jnp.int32).reshape(1)
    numbers = (logit_scale, logit_bias)
    flops = 2 * ROWS * D * D
    anywhere = pl.BlockSpec(memory_space=pl.ANY)
    scratch = [pltpu.VMEM((2 * SHARD, D), F32), pltpu.SemaphoreType.DMA((2,))]
    image0, text0 = call(prepare_kernel, [packed] * 2, [VMEM] * 3, ROWS)(
        feats, text_embed, row_ids.reshape(1, ROWS)
    )
    shard1 = move(proj_weight, CORES)
    shard2 = move(proj_weight, swap_x((1, 3)))
    image1 = shift(image0, -1)
    text1 = shift(text0, 1)
    image2 = shift(image1, -1)
    shard2, text1 = lax.optimization_barrier((shard2, text1))
    shard3 = move(shard2, CORES)
    weight, raw_grad0, grad = call(
        own_kernel, [shape(D, D, BF), shape(ROWS, D, BF), shape(ROWS, D, F32)], [SMEM] * 3 + [VMEM] * 6, flops
    )(grp, *numbers, proj_weight, shard1, shard2, shard3, image0, text0)
    part, grad = call(
        next_kernel, [shape(D, D, F32), shape(ROWS, D, F32)], [SMEM] * 2 + [VMEM] * 7, 4 * flops
    )(*numbers, weight, image0, raw_grad0, image1, text0, text1, grad)
    send, turned, raw_grad2 = call(
        last_kernel,
        [shape(2 * SHARD, D, BF), shape(D, ROWS, BF), shape(ROWS, D, BF)],
        [SMEM] * 3 + [VMEM] * 3 + [anywhere],
        2 * flops,
        scratch,
    )(grp, *numbers, weight, image2, text1, part)
    keep = call(
        keep_kernel, [shape(2 * SHARD, D, BF)], [SMEM] + [VMEM] * 2 + [anywhere], flops, scratch
    )(grp, turned, raw_grad2, part)[0]
    halves = (keep.astype(F32) + move(send, CORES).astype(F32)).astype(BF)
    mine = total(exchange(halves.reshape(8, SUB, D), FIRST))
    mine, image2 = lax.optimization_barrier((mine, image2))
    tiles = mine.reshape(SUB, 9, 128).transpose(1, 0, 2).reshape(SUB * 9, 128)
    tiles = jnp.pad(tiles, ((0, 768 - SUB * 9), (0, 0))).reshape(16, 48, 128)
    done = total(exchange(tiles, FAR))
    image3 = shift(image2, -1)
    done = (done.astype(F32) + move(done, swap_x((2, 2))).astype(F32)).astype(BF)
    done = spread(done, FAR).reshape(768, 128)[:704]
    done, image3 = lax.optimization_barrier((done, image3))
    done = spread(done, NEAR)[:, : SUB * 9]
    weight_grad = done.reshape(4, 9, SUB, 128).transpose(0, 2, 1, 3).reshape(SHARD, D).astype(F32)
    text_grad = call(finish_kernel, [shape(ROWS, D, F32)], [SMEM] * 2 + [VMEM] * 5, 2 * flops)(
        *numbers, weight, image2, image3, text0, grad
    )[0]
    return (weight_grad, text_grad)


def solution(mesh):
    return jax.shard_map(
        on_device,
        mesh=mesh,
        in_specs=(P(AXIS, None), P("grp", None), P(AXIS, None), P(AXIS), P(), P()),
        out_specs=(P("grp", None), P(AXIS, None)),
        check_vma=False,
    )
```

time: 170 us -> 159 us (0.935)
  the two profiles are of different devices: /device:TPU:8 before, /device:TPU:1 now
where the time goes in v3:
time: 159 us; the launch traced here: 157 us
  starting transfers between devices  69.4 us (44%)
  blocking collectives  33.9 us (21%)
  Pallas kernels  25.1 us (16%)
  waiting for transfers between devices  13.8 us (9%)
  local copies, waits for them, and re-layouts  11.8 us (7%)
  between operations  2.19 us (1%)
    all_to_all x2, blocking collectives, exchange(): lax.all_to_all(chunks, AXIS, 0, 0, axis_index_groups=groups, tiled=True)  33.9 us
    ppermute x4, starting transfers between devices, shift(): lax.ppermute(block, AXIS, [((i - 4 * distance) % N, i) for i in range(N)])  28.8 us
    pallas_call x6, Pallas kernels, run(): pl.pallas_call(kernel, out_shape=outs, in_specs=specs, out_specs=[VMEM] *...  25.1 us
    ppermute x5, starting transfers between devices, move(): return lax.ppermute(block, AXIS, moves)  21.2 us
    all_to_all x2, starting transfers between devices, exchange(): lax.all_to_all(chunks, AXIS, 0, 0, axis_index_groups=groups, tiled=True)  19.4 us
    unnamed x23, local copies, waits for them, and re-layouts  8.45 us
    ppermute x4, waiting for transfers between devices, shift(): lax.ppermute(block, AXIS, [((i - 4 * distance) % N, i) for i in range(N)])  6.24 us
    all_to_all x2, waiting for transfers between devices, exchange(): lax.all_to_all(chunks, AXIS, 0, 0, axis_index_groups=groups, tiled=True)  4.19 us
  transfers between devices with their start and end apart: 11, of which 4 were waited for; matrix products, arithmetic and copies ran while one was open for 0% of the time, Pallas kernels for 12%

profile of v3, /device:TPU:1, one launch (start us, length us, event | category | flops | bytes accessed | tf_op | source)
XLA Modules:
  0.0 156.8 jit_solution(11582603823266960937)
XLA Ops:
  0.6 0.0 copy-start.3
  0.6 5.3 %collective-permute-start.1 = (bf16[288,1152]{1,0:T(8,128)(2,1)}, bf16[288,1152]{1,0:T(8,128)(2,1)S(1)}, u32[]{:S(2)}, u32[]{:S(2)}) collective-permute-start(bf16[288,1152]{1,0:T(8,128)(2,1)} %shard0_ref.1), channel_id=1, source_target_pairs={{2,0},{35,1},{0,2},{33,3},{6,4},{39,5},{4,6},{37,7},{10,8},{43,9},... | collective-permute-start | bytes 1990664 | tf_op jit(solution)/shard_map/ppermute | solution.py:58
  6.0 0.0 copy-start.8
  6.0 1.1 copy-done.8
  7.1 0.0 copy-start.9
  7.1 1.1 copy-done.9
  8.1 0.0 copy-start.10
  8.1 0.7 copy-done.10
  8.8 0.3 shard_map.77
  9.1 3.2 %collective-permute-start.2 = (bf16[272,1152]{1,0:T(8,128)(2,1)S(1)}, bf16[272,1152]{1,0:T(8,128)(2,1)S(1)}, u32[]{:S(2)}, u32[]{:S(2)}) collective-permute-start(bf16[272,1152]{1,0:T(8,128)(2,1)S(1)} %get-tuple-element.18.text_ref), channel_id=1, source_target_pairs={{508,0},{509,1},{510,2},{511,3},{0,4},{1,5},{2,6},{3,7},{4,8},{5,9... | collective-permute-start | bytes 1880072 | tf_op jit(solution)/shard_map/ppermute | solution.py:54
  12.3 12.5 %collective-permute-start.4 = (bf16[272,1152]{1,0:T(8,128)(2,1)S(1)}, bf16[272,1152]{1,0:T(8,128)(2,1)}, u32[]{:S(2)}, u32[]{:S(2)}) collective-permute-start(bf16[272,1152]{1,0:T(8,128)(2,1)S(1)} %get-tuple-element.20.image_ref.image0_ref), channel_id=1, source_target_pairs={{4,0},{5,1},{6,2},{7,3},{8,4},{9,5},{10,6},{11,7},{12,8},{13,9},{1... | collective-permute-start | bytes 1880072 | tf_op jit(solution)/shard_map/ppermute | solution.py:54
  24.8 0.0 copy-start.4
  24.8 0.8 copy-done.4
  25.6 3.8 %collective-permute-start = (bf16[288,1152]{1,0:T(8,128)(2,1)}, bf16[288,1152]{1,0:T(8,128)(2,1)S(1)}, u32[]{:S(2)}, u32[]{:S(2)}) collective-permute-start(bf16[288,1152]{1,0:T(8,128)(2,1)} %shard0_ref.1), channel_id=1, source_target_pairs={{1,0},{0,1},{3,2},{2,3},{5,4},{4,5},{7,6},{6,7},{9,8},{8,9},{11,10... | collective-permute-start | bytes 1990664 | tf_op jit(solution)/shard_map/ppermute | solution.py:58
  29.5 6.2 %collective-permute-done.2.text1_ref = bf16[272,1152]{1,0:T(8,128)(2,1)S(1)} collective-permute-done((bf16[272,1152]{1,0:T(8,128)(2,1)S(1)}, bf16[272,1152]{1,0:T(8,128)(2,1)S(1)}, u32[]{:S(2)}, u32[]{:S(2)}) %collective-permute-start.2) | collective-permute-done | bytes 626720 | tf_op jit(solution)/shard_map/ppermute | solution.py:54
  35.7 0.0 copy-start.6
  35.7 0.8 copy-done.6
  36.5 0.0 collective-permute-done.1.shard2_ref
  36.5 4.2 %collective-permute-start.3 = (bf16[288,1152]{1,0:T(8,128)(2,1)S(1)}, bf16[288,1152]{1,0:T(8,128)(2,1)S(1)}, u32[]{:S(2)}, u32[]{:S(2)}) collective-permute-start(bf16[288,1152]{1,0:T(8,128)(2,1)S(1)} %collective-permute-done.1.shard2_ref), channel_id=1, source_target_pairs={{1,0},{0,1},{3,2},{2,3},{5,4},{4,5},{7,6},{6,7},{9,8},{8,9},{11,10... | collective-permute-start | bytes 1990664 | tf_op jit(solution)/shard_map/ppermute | solution.py:58
  40.7 0.0 collective-permute-done.4.image1_ref
  40.7 5.8 %collective-permute-start.5 = (bf16[272,1152]{1,0:T(8,128)(2,1)}, bf16[272,1152]{1,0:T(8,128)(2,1)}, u32[]{:S(2)}, u32[]{:S(2)}) collective-permute-start(bf16[272,1152]{1,0:T(8,128)(2,1)} %collective-permute-done.4.image1_ref), channel_id=1, source_target_pairs={{4,0},{5,1},{6,2},{7,3},{8,4},{9,5},{10,6},{11,7},{12,8},{13,9},{1... | collective-permute-start | bytes 1880072 | tf_op jit(solution)/shard_map/ppermute | solution.py:54
  47.8 0.0 collective-permute-done.shard1_ref
  47.8 0.0 collective-permute-done.3.shard3_ref
  47.8 0.0 copy-done.3
  47.9 0.0 copy-start.5
  47.9 1.1 copy-done.5
  48.9 0.0 copy-start.7
  48.9 2.6 %shard_map.78 = (bf16[1152,1152]{1,0:T(8,128)(2,1)}, bf16[256,1152]{1,0:T(8,128)(2,1)S(1)}, f32[256,1152]{1,0:T(8,128)S(1)}) custom-call(s32[1]{0:T(128)} %bitcast.grp_ref, f32[1]{0:T(128)S(6)} %copy.13.scale_ref, f32[1]{0:T(128)S(6)} %copy.14.bias_ref, bf16[288,1152]{1,0:T(8,128)(2,1)S(1)} %copy-done.3, ...), custom_call_target="tpu_custom_call" | custom-call | flops 679477248 | bytes 8331276 | tf_op jit(solution)/shard_map/pallas_call | solution.py:78
  51.5 0.0 copy-done.7
  51.5 8.2 %shard_map.79 = (f32[1152,1152]{1,0:T(8,128)}, f32[256,1152]{1,0:T(8,128)S(1)}) custom-call(f32[1]{0:T(128)S(6)} %copy.13.scale_ref, f32[1]{0:T(128)S(6)} %copy.14.bias_ref, bf16[1152,1152]{1,0:T(8,128)(2,1)} %get-tuple-element.21.weight_ref, bf16[272,1152]{1,0:T(8,128)(2,1)S(1)} %copy-done.5, bf16[256,1152]{1,0:T(8,128)(2,1)S(1)} %get-tuple-element.23.raw_grad0_ref, ...), custom_call_target="tpu_custom_call" | custom-call | flops 2717908992 | bytes 13418504 | tf_op jit(solution)/shard_map/pallas_call | solution.py:78
  59.7 0.0 copy-start.1
  59.7 0.0 collective-permute-done.5.image_ref.image2_ref
  59.7 6.0 %shard_map.80 = (bf16[576,1152]{1,0:T(8,128)(2,1)S(1)}, bf16[1152,256]{1,0:T(8,128)(2,1)S(1)}, bf16[256,1152]{1,0:T(8,128)(2,1)S(1)}) custom-call(s32[1]{0:T(128)} %bitcast.grp_ref, f32[1]{0:T(128)S(6)} %copy.13.scale_ref, f32[1]{0:T(128)S(6)} %copy.14.bias_ref, bf16[1152,1152]{1,0:T(8,128)(2,1)} %get-tuple-element.21.weight_ref, ...), custom_call_target="tpu_custom_call" | custom-call | flops 1358954496 | bytes 11722764 | tf_op jit(solution)/shard_map/pallas_call | solution.py:78
  65.7 0.0 copy-done.1
  65.8 4.7 %collective-permute-start.6 = (bf16[576,1152]{1,0:T(8,128)(2,1)S(1)}, bf16[576,1152]{1,0:T(8,128)(2,1)S(1)}, u32[]{:S(2)}, u32[]{:S(2)}) collective-permute-start(bf16[576,1152]{1,0:T(8,128)(2,1)S(1)} %get-tuple-element.28), channel_id=1, source_target_pairs={{1,0},{0,1},{3,2},{2,3},{5,4},{4,5},{7,6},{6,7},{9,8},{8,9},{11,10... | collective-permute-start | bytes 3981320 | tf_op jit(solution)/shard_map/ppermute | solution.py:58
  70.5 2.1 %shard_map.81 = bf16[576,1152]{1,0:T(8,128)(2,1)S(1)} custom-call(s32[1]{0:T(128)} %bitcast.grp_ref, bf16[1152,256]{1,0:T(8,128)(2,1)S(1)} %get-tuple-element.26.turned_ref, bf16[256,1152]{1,0:T(8,128)(2,1)S(1)} %get-tuple-element.27.raw_grad_ref, f32[1152,1152]{1,0:T(8,128)} %get-tuple-element.25.part_ref), custom_call_target="tpu_custom_call" | custom-call | flops 679477248 | bytes 7815172 | tf_op jit(solution)/shard_map/pallas_call | solution.py:78
  72.6 0.5 collective-permute-done.6
  73.2 0.3 add_convert_fusion
  73.5 18.1 %all_to_all.20 = bf16[8,72,1152]{2,1,0:T(8,128)(2,1)S(1)} all-to-all(bf16[8,72,1152]{2,1,0:T(8,128)(2,1)S(1)} %bitcast.18), channel_id=1, replica_groups={{0,4,64,68,2,6,66,70},{477,449,29,1,511,483,63,35},{509,481,61,33,479,4..., dimensions={0} | all-to-all | bytes 2654208 | tf_op jit(solution)/shard_map/all_to_all | solution.py:62
  91.6 0.2 reduce_sum.24
  91.8 0.1 reshape.36
  91.9 0.7 pad.4
  92.6 6.2 %all-to-all-start.1 = ((bf16[16,48,128]{2,1,0:T(8,128)(2,1)}), bf16[16,48,128]{2,1,0:T(8,128)(2,1)S(1)}, u32[]{:S(2)}, u32[]{:S(2)}) async-start(bf16[16,48,128]{2,1,0:T(8,128)(2,1)} %bitcast.5), calls=%async_computation.1 | async-start | bytes 393216 | tf_op jit(solution)/shard_map/all_to_all | solution.py:62
  98.8 7.3 %collective-permute-start.8 = (bf16[272,1152]{1,0:T(8,128)(2,1)}, bf16[272,1152]{1,0:T(8,128)(2,1)}, u32[]{:S(2)}, u32[]{:S(2)}) collective-permute-start(bf16[272,1152]{1,0:T(8,128)(2,1)} %collective-permute-done.5.image_ref.image2_ref), channel_id=1, source_target_pairs={{4,0},{5,1},{6,2},{7,3},{8,4},{9,5},{10,6},{11,7},{12,8},{13,9},{1... | collective-permute-start | bytes 1880072 | tf_op jit(solution)/shard_map/ppermute | solution.py:54
  106.1 4.2 %all-to-all-done.1 = bf16[16,48,128]{2,1,0:T(8,128)(2,1)S(1)} async-done(((bf16[16,48,128]{2,1,0:T(8,128)(2,1)}), bf16[16,48,128]{2,1,0:T(8,128)(2,1)S(1)}, u32[]{:S(2)}, u32[]{:S(2)}) %all-to-all-start.1) | async-done | bytes 196640 | tf_op jit(solution)/shard_map/all_to_all | solution.py:62
  110.3 3.1 %collective-permute-start.7 = (bf16[48,128]{1,0:T(8,128)(2,1)S(1)}, bf16[48,128]{1,0:T(8,128)(2,1)S(1)}, u32[]{:S(2)}, u32[]{:S(2)}) collective-permute-start(bf16[48,128]{1,0:T(8,128)(2,1)S(1)} %reduce_sum.25), channel_id=1, source_target_pairs={{32,0},{33,1},{34,2},{35,3},{36,4},{37,5},{38,6},{39,7},{40,8},{41... | collective-permute-start | bytes 36872 | tf_op jit(solution)/shard_map/ppermute | solution.py:58
  113.5 2.8 %collective-permute-done.7 = bf16[48,128]{1,0:T(8,128)(2,1)S(1)} collective-permute-done((bf16[48,128]{1,0:T(8,128)(2,1)S(1)}, bf16[48,128]{1,0:T(8,128)(2,1)S(1)}, u32[]{:S(2)}, u32[]{:S(2)}) %collective-permute-start.7) | collective-permute-done | bytes 12320 | tf_op jit(solution)/shard_map/ppermute | solution.py:58
  116.3 15.8 %all_to_all.21 = bf16[16,48,128]{2,1,0:T(8,128)(2,1)S(1)} all-to-all(bf16[16,48,128]{2,1,0:T(8,128)(2,1)S(1)} %broadcast_in_dim.4), channel_id=1, replica_groups={{0,8,16,24,128,136,144,152,256,264,272,280,384,392,400,408},{1,9,17,25,..., dimensions={0} | all-to-all | bytes 393216 | tf_op jit(solution)/shard_map/all_to_all | solution.py:62
  132.1 0.0 copy-start
  132.1 0.0 collective-permute-done.8.image3_ref
  132.1 1.0 broadcast_in_dim.5
  133.1 13.1 %all-to-all-start.3 = ((bf16[4,704,128]{2,1,0:T(8,128)(2,1)}), bf16[4,704,128]{2,1,0:T(8,128)(2,1)}, u32[]{:S(2)}, u32[]{:S(2)}) async-start(bf16[4,704,128]{2,1,0:T(8,128)(2,1)} %broadcast_in_dim.5), calls=%async_computation.3 | async-start | bytes 1441792 | tf_op jit(solution)/shard_map/all_to_all | solution.py:62
  146.2 0.0 copy-done
  146.2 0.0 copy-start.2
  146.2 1.3 copy-done.2
  147.5 6.0 %shard_map.82 = f32[256,1152]{1,0:T(8,128)} custom-call(f32[1]{0:T(128)S(6)} %copy.13.scale_ref, f32[1]{0:T(128)S(6)} %copy.14.bias_ref, bf16[1152,1152]{1,0:T(8,128)(2,1)S(1)} %copy-done, bf16[272,1152]{1,0:T(8,128)(2,1)} %collective-permute-done.5.image_ref.image2_ref, bf16[272,1152]{1,0:T(8,128)(2,1)} %collective-permute-done.8.image3_ref, ...), custom_call_target="tpu_custom_call" | custom-call | flops 1358954496 | bytes 6893576 | tf_op jit(solution)/shard_map/pallas_call | solution.py:78
  153.5 0.0 all-to-all-done.3
  153.5 1.1 slice.9
  154.6 0.1 convert_bitcast_fusion
  154.7 0.4 copy.9
  155.1 1.6 %copy.12 = f32[36,8,9,128]{3,1,2,0:T(8,128)} copy(f32[36,8,9,128]{3,2,1,0:T(8,128)S(1)} %bitcast.17) | data formatting | bytes 2654208
  (5 shorter events, 0.1 us)
Async XLA Ops:
  0.6 47.2 %copy-start.3 = (bf16[288,1152]{1,0:T(8,128)(2,1)S(1)}, bf16[288,1152]{1,0:T(8,128)(2,1)}, u32[]{:S(2)}) copy-start(bf16[288,1152]{1,0:T(8,128)(2,1)} %shard0_ref.1) | copy-start | bytes 1990660
  0.6 35.9 %collective-permute-start.1 = (bf16[288,1152]{1,0:T(8,128)(2,1)}, bf16[288,1152]{1,0:T(8,128)(2,1)S(1)}, u32[]{:S(2)}, u32[]{:S(2)}) collective-permute-start(bf16[288,1152]{1,0:T(8,128)(2,1)} %shard0_ref.1), channel_id=1, source_target_pairs={{2,0},{35,1},{0,2},{33,3},{6,4},{39,5},{4,6},{37,7},{10,8},{43,9},... | collective-permute-start | bytes 1990664 | tf_op jit(solution)/shard_map/ppermute | solution.py:58
  6.0 1.1 copy-start.8
  7.1 1.1 copy-start.9
  8.1 0.7 copy-start.10
  9.1 26.6 %collective-permute-start.2 = (bf16[272,1152]{1,0:T(8,128)(2,1)S(1)}, bf16[272,1152]{1,0:T(8,128)(2,1)S(1)}, u32[]{:S(2)}, u32[]{:S(2)}) collective-permute-start(bf16[272,1152]{1,0:T(8,128)(2,1)S(1)} %get-tuple-element.18.text_ref), channel_id=1, source_target_pairs={{508,0},{509,1},{510,2},{511,3},{0,4},{1,5},{2,6},{3,7},{4,8},{5,9... | collective-permute-start | bytes 1880072 | tf_op jit(solution)/shard_map/ppermute | solution.py:54
  12.3 28.4 %collective-permute-start.4 = (bf16[272,1152]{1,0:T(8,128)(2,1)S(1)}, bf16[272,1152]{1,0:T(8,128)(2,1)}, u32[]{:S(2)}, u32[]{:S(2)}) collective-permute-start(bf16[272,1152]{1,0:T(8,128)(2,1)S(1)} %get-tuple-element.20.image_ref.image0_ref), channel_id=1, source_target_pairs={{4,0},{5,1},{6,2},{7,3},{8,4},{9,5},{10,6},{11,7},{12,8},{13,9},{1... | collective-permute-start | bytes 1880072 | tf_op jit(solution)/shard_map/ppermute | solution.py:54
  24.8 0.8 copy-start.4
  25.6 22.2 %collective-permute-start = (bf16[288,1152]{1,0:T(8,128)(2,1)}, bf16[288,1152]{1,0:T(8,128)(2,1)S(1)}, u32[]{:S(2)}, u32[]{:S(2)}) collective-permute-start(bf16[288,1152]{1,0:T(8,128)(2,1)} %shard0_ref.1), channel_id=1, source_target_pairs={{1,0},{0,1},{3,2},{2,3},{5,4},{4,5},{7,6},{6,7},{9,8},{8,9},{11,10... | collective-permute-start | bytes 1990664 | tf_op jit(solution)/shard_map/ppermute | solution.py:58
  35.7 0.8 copy-start.6
  36.5 11.3 %collective-permute-start.3 = (bf16[288,1152]{1,0:T(8,128)(2,1)S(1)}, bf16[288,1152]{1,0:T(8,128)(2,1)S(1)}, u32[]{:S(2)}, u32[]{:S(2)}) collective-permute-start(bf16[288,1152]{1,0:T(8,128)(2,1)S(1)} %collective-permute-done.1.shard2_ref), channel_id=1, source_target_pairs={{1,0},{0,1},{3,2},{2,3},{5,4},{4,5},{7,6},{6,7},{9,8},{8,9},{11,10... | collective-permute-start | bytes 1990664 | tf_op jit(solution)/shard_map/ppermute | solution.py:58
  40.7 19.0 %collective-permute-start.5 = (bf16[272,1152]{1,0:T(8,128)(2,1)}, bf16[272,1152]{1,0:T(8,128)(2,1)}, u32[]{:S(2)}, u32[]{:S(2)}) collective-permute-start(bf16[272,1152]{1,0:T(8,128)(2,1)} %collective-permute-done.4.image1_ref), channel_id=1, source_target_pairs={{4,0},{5,1},{6,2},{7,3},{8,4},{9,5},{10,6},{11,7},{12,8},{13,9},{1... | collective-permute-start | bytes 1880072 | tf_op jit(solution)/shard_map/ppermute | solution.py:54
  47.9 1.1 copy-start.5
  48.9 2.6 %copy-start.7 = (bf16[272,1152]{1,0:T(8,128)(2,1)S(1)}, bf16[272,1152]{1,0:T(8,128)(2,1)}, u32[]{:S(2)}) copy-start(bf16[272,1152]{1,0:T(8,128)(2,1)} %copy-done.6) | copy-start | bytes 1880068
  59.7 6.0 %copy-start.1 = (f32[256,1152]{1,0:T(8,128)}, f32[256,1152]{1,0:T(8,128)S(1)}, u32[]{:S(2)}) copy-start(f32[256,1152]{1,0:T(8,128)S(1)} %get-tuple-element.33.grad_ref) | copy-start | bytes 3538948
  65.8 7.4 %collective-permute-start.6 = (bf16[576,1152]{1,0:T(8,128)(2,1)S(1)}, bf16[576,1152]{1,0:T(8,128)(2,1)S(1)}, u32[]{:S(2)}, u32[]{:S(2)}) collective-permute-start(bf16[576,1152]{1,0:T(8,128)(2,1)S(1)} %get-tuple-element.28), channel_id=1, source_target_pairs={{1,0},{0,1},{3,2},{2,3},{5,4},{4,5},{7,6},{6,7},{9,8},{8,9},{11,10... | collective-permute-start | bytes 3981320 | tf_op jit(solution)/shard_map/ppermute | solution.py:58
  92.6 17.7 %all-to-all-start.1 = ((bf16[16,48,128]{2,1,0:T(8,128)(2,1)}), bf16[16,48,128]{2,1,0:T(8,128)(2,1)S(1)}, u32[]{:S(2)}, u32[]{:S(2)}) async-start(bf16[16,48,128]{2,1,0:T(8,128)(2,1)} %bitcast.5), calls=%async_computation.1 | async-start | bytes 393216 | tf_op jit(solution)/shard_map/all_to_all | solution.py:62
  98.8 33.3 %collective-permute-start.8 = (bf16[272,1152]{1,0:T(8,128)(2,1)}, bf16[272,1152]{1,0:T(8,128)(2,1)}, u32[]{:S(2)}, u32[]{:S(2)}) collective-permute-start(bf16[272,1152]{1,0:T(8,128)(2,1)} %collective-permute-done.5.image_ref.image2_ref), channel_id=1, source_target_pairs={{4,0},{5,1},{6,2},{7,3},{8,4},{9,5},{10,6},{11,7},{12,8},{13,9},{1... | collective-permute-start | bytes 1880072 | tf_op jit(solution)/shard_map/ppermute | solution.py:54
  110.3 5.9 %collective-permute-start.7 = (bf16[48,128]{1,0:T(8,128)(2,1)S(1)}, bf16[48,128]{1,0:T(8,128)(2,1)S(1)}, u32[]{:S(2)}, u32[]{:S(2)}) collective-permute-start(bf16[48,128]{1,0:T(8,128)(2,1)S(1)} %reduce_sum.25), channel_id=1, source_target_pairs={{32,0},{33,1},{34,2},{35,3},{36,4},{37,5},{38,6},{39,7},{40,8},{41... | collective-permute-start | bytes 36872 | tf_op jit(solution)/shard_map/ppermute | solution.py:58
  132.1 14.1 %copy-start = (bf16[1152,1152]{1,0:T(8,128)(2,1)S(1)}, bf16[1152,1152]{1,0:T(8,128)(2,1)}, u32[]{:S(2)}) copy-start(bf16[1152,1152]{1,0:T(8,128)(2,1)} %get-tuple-element.21.weight_ref) | copy-start | bytes 7962628
  133.1 20.4 %all-to-all-start.3 = ((bf16[4,704,128]{2,1,0:T(8,128)(2,1)}), bf16[4,704,128]{2,1,0:T(8,128)(2,1)}, u32[]{:S(2)}, u32[]{:S(2)}) async-start(bf16[4,704,128]{2,1,0:T(8,128)(2,1)} %broadcast_in_dim.5), calls=%async_computation.3 | async-start | bytes 1441792 | tf_op jit(solution)/shard_map/all_to_all | solution.py:62
  146.2 1.3 copy-start.2

commit v4 on v3

--- a/solution.py
+++ b/solution.py
@@ -81,41 +81,40 @@
             in_specs=specs,
             out_specs=[VMEM] * len(outs),
             scratch_shapes=scratch,
-            compiler_params=pltpu.CompilerParams(vmem_limit_bytes=48 * 1024 * 1024),
+            compiler_params=pltpu.CompilerParams(vmem_limit_bytes=20 * 1024 * 1024),
             cost_estimate=pl.CostEstimate(flops=flops, bytes_accessed=moved, transcendentals=0),
         )(*args)
 
     return run
 
 
-def put_ids(ids_ref, out_ref):
+def top_row(ids_ref):
     first = lax.broadcasted_iota(jnp.int32, (16, ROWS), 0) == 0
     ids = jnp.broadcast_to(ids_ref[...].astype(F32), (16, ROWS))
-    out_ref[ROWS:, :ROWS] = jnp.where(first, ids, 0.0).astype(BF)
-    out_ref[ROWS:, ROWS:] = jnp.zeros((16, D - ROWS), BF)
-
-
-def prepare_kernel(feats_ref, text_ref, ids_ref, image_ref, out_ref):
-    image_ref[:ROWS, :] = feats_ref[...]
-    put_ids(ids_ref, image_ref)
+    return jnp.where(first, ids, 0.0).astype(BF)
+
+
+def prepare_kernel(text_ref, ids_ref, out_ref):
     rows = text_ref[...].astype(F32)
     inverse = 1.0 / jnp.sqrt(jnp.sum(rows * rows, -1, keepdims=True) + 1e-06)
     out_ref[:ROWS, :] = (rows * inverse).astype(BF)
-    put_ids(ids_ref, out_ref)
+    out_ref[ROWS:, :ROWS] = top_row(ids_ref)
+    out_ref[ROWS:, ROWS:] = jnp.zeros((16, D - ROWS), BF)
 
 
 def project(image_ref, weight_ref):
-    raw = jnp.dot(image_ref[:ROWS, :], weight_ref[...], preferred_element_type=F32)
+    raw = jnp.dot(image_ref[...], weight_ref[...], preferred_element_type=F32)
     inverse = 1.0 / jnp.sqrt(jnp.sum(raw * raw, -1, keepdims=True) + 1e-06)
     unit = raw * inverse
     return unit, unit.astype(BF), inverse
 
 
-def ids_down(image_ref):
-    ones = jnp.ones((16, ROWS), BF)
-    return lax.dot_general(
-        image_ref[ROWS:, :ROWS], ones, (((0,), (0,)), ((), ())), preferred_element_type=F32
-    )
+def ids_down(ids_ref):
+    return across(top_row(ids_ref), jnp.ones((16, ROWS), BF))
+
+
+def turn(image_ref):
+    return image_ref[...].astype(F32).T.astype(BF)
 
 
 def pair(image_unit, ids, text_ref, scale, bias):
@@ -141,25 +140,34 @@
 
 
 def own_kernel(
-    grp_ref, scale_ref, bias_ref, shard0_ref, shard1_ref, shard2_ref, shard3_ref, image_ref, text_ref, weight_ref, raw_grad_ref, grad_ref
+    grp_ref, scale_ref, bias_ref, shard0_ref, shard1_ref, shard2_ref, shard3_ref, image_ref, ids_ref, text_ref, weight_ref, raw_grad_ref, grad_ref, sems
 ):
     grp = grp_ref[0]
+    loads = []
     for flip, shard_ref in enumerate((shard0_ref, shard1_ref, shard2_ref, shard3_ref)):
-        weight_ref[pl.ds(pl.multiple_of((grp ^ flip) * SHARD, 32), SHARD), :] = shard_ref[...]
+        rows = pl.ds(pl.multiple_of((grp ^ flip) * SHARD, 32), SHARD)
+        loads.append(pltpu.make_async_copy(shard_ref, weight_ref.at[rows, :], sems.at[flip]))
+        loads[-1].start()
+    for load in loads:
+        load.wait()
     scale, bias = scale_ref[0], bias_ref[0]
     unit, image_unit, inverse = project(image_ref, weight_ref)
-    near = pair(image_unit, ids_down(image_ref), text_ref, scale, bias)
+    near = pair(image_unit, ids_down(ids_ref), text_ref, scale, bias)
     grad_ref[...] = across(near, image_unit)
     image_grad = scale * jnp.dot(near, text_ref[:ROWS, :], preferred_element_type=F32)
     raw_grad_ref[...] = back(image_grad, unit, inverse)
 
 
 def next_kernel(
-    scale_ref, bias_ref, weight_ref, image0_ref, raw_grad0_ref, image1_ref, text_ref, text1_ref, grad0_ref, part_ref, grad_ref
+    scale_ref, bias_ref, weight_ref, image0_ref, raw_grad0_ref, image1_ref, ids_ref, text_ref, text1_ref, grad0_ref, part_ref, grad_ref,
+    turned_ref, raw_grads_ref
 ):
+    turned_ref[:, :ROWS] = turn(image0_ref)
+    turned_ref[:, ROWS:] = turn(image1_ref)
+    raw_grads_ref[:ROWS, :] = raw_grad0_ref[...]
     scale, bias = scale_ref[0], bias_ref[0]
     unit, image_unit, inverse = project(image1_ref, weight_ref)
-    ids = ids_down(image1_ref)
+    ids = ids_down(ids_ref)
     near = pair(image_unit, ids, text_ref, scale, bias)
     far = pair(image_unit, ids, text1_ref, scale, bias)
     grad_ref[...] = grad0_ref[...] + across(near, image_unit)
@@ -167,9 +175,8 @@
         jnp.dot(near, text_ref[:ROWS, :], preferred_element_type=F32)
         + jnp.dot(far, text1_ref[:ROWS, :], preferred_element_type=F32)
     )
-    raw_grad = back(image_grad, unit, inverse)
-    part_ref[...] = across(image0_ref[:ROWS, :], raw_grad0_ref[...])
-    part_ref[...] += across(image1_ref[:ROWS, :], raw_grad)
+    raw_grads_ref[ROWS:, :] = back(image_grad, unit, inverse)
+    part_ref[...] = jnp.dot(turned_ref[...], raw_grads_ref[...], preferred_element_type=F32)
 
 
 def load_quarters(core, part_ref, rows_ref, sems):
@@ -198,35 +205,34 @@
 
 
 def last_kernel(
-    grp_ref, scale_ref, bias_ref, weight_ref, image_ref, text1_ref, part_ref, send_ref, turned_ref, raw_grad_ref, rows_ref, sems
+    grp_ref, scale_ref, bias_ref, weight_ref, image_ref, ids_ref, text1_ref, part_ref,
+    send_ref, turned_ref, raw_grad_ref, image_unit_ref, far_ref, rows_ref, sems
 ):
     core = 1 - grp_ref[0] % 2
     loads = load_quarters(core, part_ref, rows_ref, sems)
     scale, bias = scale_ref[0], bias_ref[0]
-    turned_ref[...] = image_ref[:ROWS, :].astype(F32).T.astype(BF)
+    turned_ref[...] = turn(image_ref)
     unit, image_unit, inverse = project(image_ref, weight_ref)
-    far = pair(image_unit, ids_down(image_ref), text1_ref, scale, bias)
+    image_unit_ref[...] = image_unit
+    far = pair(image_unit, ids_down(ids_ref), text1_ref, scale, bias)
+    far_ref[...] = far
     image_grad = scale * jnp.dot(far, text1_ref[:ROWS, :], preferred_element_type=F32)
     raw_grad = back(image_grad, unit, inverse)
     raw_grad_ref[...] = raw_grad
     add_quarters(core, turned_ref, raw_grad, rows_ref, loads, send_ref)
 
 
-def keep_kernel(grp_ref, turned_ref, raw_grad_ref, part_ref, keep_ref, rows_ref, sems):
+def keep_kernel(grp_ref, turned_ref, raw_grad_ref, image_unit_ref, far_ref, part_ref, keep_ref, back_ref, rows_ref, sems):
     core = grp_ref[0] % 2
     loads = load_quarters(core, part_ref, rows_ref, sems)
     add_quarters(core, turned_ref, raw_grad_ref[...], rows_ref, loads, keep_ref)
-
-
-def finish_kernel(scale_ref, bias_ref, weight_ref, image2_ref, image3_ref, text_ref, grad_ref, out_ref):
-    scale, bias = scale_ref[0], bias_ref[0]
-    grad = None
-    for image_ref in (image2_ref, image3_ref):
-        _, image_unit, _ = project(image_ref, weight_ref)
-        near = pair(image_unit, ids_down(image_ref), text_ref, scale, bias)
-        term = across(near, image_unit)
-        grad = term if grad is None else grad + term
-    out_ref[...] = scale * (grad_ref[...] + grad)
+    back_ref[...] = across(far_ref[...], image_unit_ref[...]).astype(BF)
+
+
+def finish_kernel(scale_ref, bias_ref, image_unit2_ref, ids2_ref, text_ref, grad_ref, back_ref, out_ref):
+    image_unit2 = image_unit2_ref[...]
+    near2 = pair(image_unit2, ids_down(ids2_ref), text_ref, scale_ref[0], bias_ref[0])
+    out_ref[...] = scale_ref[0] * (grad_ref[...] + across(near2, image_unit2) + back_ref[...].astype(F32))
 
 
 def shape(rows, columns, dtype):
@@ -240,46 +246,55 @@
     flops = 2 * ROWS * D * D
     anywhere = pl.BlockSpec(memory_space=pl.ANY)
     scratch = [pltpu.VMEM((2 * SHARD, D), F32), pltpu.SemaphoreType.DMA((2,))]
-    image0, text0 = call(prepare_kernel, [packed] * 2, [VMEM] * 3, ROWS)(
-        feats, text_embed, row_ids.reshape(1, ROWS)
-    )
+    ids = [row_ids.reshape(1, ROWS)]
+    text0 = call(prepare_kernel, [packed], [VMEM] * 2, ROWS)(text_embed, ids[0])[0]
     shard1 = move(proj_weight, CORES)
     shard2 = move(proj_weight, swap_x((1, 3)))
-    image1 = shift(image0, -1)
+    image1 = shift(feats, -1)
     text1 = shift(text0, 1)
     image2 = shift(image1, -1)
+    late_ids = lax.optimization_barrier((row_ids, shard2))[0]
+    ids += [shift(late_ids, -distance).reshape(1, ROWS) for distance in (1, 2)]
     shard2, text1 = lax.optimization_barrier((shard2, text1))
     shard3 = move(shard2, CORES)
     weight, raw_grad0, grad = call(
-        own_kernel, [shape(D, D, BF), shape(ROWS, D, BF), shape(ROWS, D, F32)], [SMEM] * 3 + [VMEM] * 6, flops
-    )(grp, *numbers, proj_weight, shard1, shard2, shard3, image0, text0)
+        own_kernel, [shape(D, D, BF), shape(ROWS, D, BF), shape(ROWS, D, F32)], [SMEM] * 3 + [anywhere] * 4 + [VMEM] * 3, flops,
+        [pltpu.SemaphoreType.DMA((4,))],
+    )(grp, *numbers, proj_weight, shard1, shard2, shard3, feats, ids[0], text0)
     part, grad = call(
-        next_kernel, [shape(D, D, F32), shape(ROWS, D, F32)], [SMEM] * 2 + [VMEM] * 7, 4 * flops
-    )(*numbers, weight, image0, raw_grad0, image1, text0, text1, grad)
-    send, turned, raw_grad2 = call(
+        next_kernel,
+        [shape(D, D, F32), shape(ROWS, D, F32)],
+        [SMEM] * 2 + [VMEM] * 8,
+        4 * flops,
+        [pltpu.VMEM((D, 2 * ROWS), BF), pltpu.VMEM((2 * ROWS, D), BF)],
+    )(*numbers, weight, feats, raw_grad0, image1, ids[1], text0, text1, grad)
+    send, turned, raw_grad2, image_unit2, far = call(
         last_kernel,
-        [shape(2 * SHARD, D, BF), shape(D, ROWS, BF), shape(ROWS, D, BF)],
-        [SMEM] * 3 + [VMEM] * 3 + [anywhere],
+        [shape(2 * SHARD, D, BF), shape(D, ROWS, BF), shape(ROWS, D, BF), shape(ROWS, D, BF), shape(ROWS, ROWS, BF)],
+        [SMEM] * 3 + [VMEM] * 4 + [anywhere],
         2 * flops,
         scratch,
-    )(grp, *numbers, weight, image2, text1, part)
-    keep = call(
-        keep_kernel, [shape(2 * SHARD, D, BF)], [SMEM] + [VMEM] * 2 + [anywhere], flops, scratch
-    )(grp, turned, raw_grad2, part)[0]
+    )(grp, *numbers, weight, image2, ids[2], text1, part)
+    keep, term = call(
+        keep_kernel,
+        [shape(2 * SHARD, D, BF), shape(ROWS, D, BF)],
+        [SMEM] + [VMEM] * 4 + [anywhere],
+        flops,
+        scratch,
+    )(grp, turned, raw_grad2, image_unit2, far, part)
+    term = shift(term, -1)
     halves = (keep.astype(F32) + move(send, CORES).astype(F32)).astype(BF)
     mine = total(exchange(halves.reshape(8, SUB, D), FIRST))
-    mine, image2 = lax.optimization_barrier((mine, image2))
+    mine, term = lax.optimization_barrier((mine, term))
     tiles = mine.reshape(SUB, 9, 128).transpose(1, 0, 2).reshape(SUB * 9, 128)
     tiles = jnp.pad(tiles, ((0, 768 - SUB * 9), (0, 0))).reshape(16, 48, 128)
     done = total(exchange(tiles, FAR))
-    image3 = shift(image2, -1)
     done = (done.astype(F32) + move(done, swap_x((2, 2))).astype(F32)).astype(BF)
     done = spread(done, FAR).reshape(768, 128)[:704]
-    done, image3 = lax.optimization_barrier((done, image3))
     done = spread(done, NEAR)[:, : SUB * 9]
     weight_grad = done.reshape(4, 9, SUB, 128).transpose(0, 2, 1, 3).reshape(SHARD, D).astype(F32)
-    text_grad = call(finish_kernel, [shape(ROWS, D, F32)], [SMEM] * 2 + [VMEM] * 5, 2 * flops)(
-        *numbers, weight, image2, image3, text0, grad
+    text_grad = call(finish_kernel, [shape(ROWS, D, F32)], [SMEM] * 2 + [VMEM] * 5, flops)(
+        *numbers, image_unit2, ids[2], text0, grad, term
     )[0]
     return (weight_grad, text_grad)
 

time: 159 us -> 166 us (1.044)
  waiting for transfers between devices: 13.8 us -> 30.9 us
  Pallas kernels: 25.1 us -> 17.1 us
  local copies, waits for them, and re-layouts: 11.8 us -> 8.6 us
  other arithmetic: 0.65 us -> 3.07 us
    ppermute x4 -> x6, waiting for transfers between devices: 6.24 us -> 16.3 us  [shift(): lax.ppermute(block, AXIS, [((i - 4 * distance) % N, i) for i in range(N)])]
    pallas_call x6, Pallas kernels: 25.1 us -> 17.1 us  [run(): pl.pallas_call(kernel, out_shape=outs, in_specs=specs, out_specs=[VMEM] *...]
    all_to_all x2, waiting for transfers between devices: 4.19 us -> 9.55 us  [exchange(): lax.all_to_all(chunks, AXIS, 0, 0, axis_index_groups=groups, tiled=True)]
    ppermute x4 -> x6, starting transfers between devices: 28.8 us -> 31.9 us  [shift(): lax.ppermute(block, AXIS, [((i - 4 * distance) % N, i) for i in range(N)])]
    ppermute x5, starting transfers between devices: 21.2 us -> 18.5 us  [move(): return lax.ppermute(block, AXIS, moves)]
    unnamed x23 -> x17, local copies, waits for them, and re-layouts: 8.45 us -> 5.95 us
    ppermute x5, waiting for transfers between devices: 3.34 us -> 5.01 us  [move(): return lax.ppermute(block, AXIS, moves)]
  transfers between devices with their start and end apart: 11 -> 13, of which waited for: 4 -> 6; matrix products, arithmetic and copies ran while one was open for 0% -> 1% of each run, Pallas kernels for 12% -> 8%
where the time goes in v4:
time: 166 us; the launch traced here: 165 us
  starting transfers between devices  68.6 us (41%)
  blocking collectives  34.3 us (21%)
  waiting for transfers between devices  30.9 us (19%)
  Pallas kernels  17.1 us (10%)
  local copies, waits for them, and re-layouts  8.6 us (5%)
  other arithmetic  3.07 us (2%)
  between operations  2.21 us (1%)
    all_to_all x2, blocking collectives, exchange(): lax.all_to_all(chunks, AXIS, 0, 0, axis_index_groups=groups, tiled=True)  34.3 us
    ppermute x6, starting transfers between devices, shift(): lax.ppermute(block, AXIS, [((i - 4 * distance) % N, i) for i in range(N)])  31.9 us
    ppermute x5, starting transfers between devices, move(): return lax.ppermute(block, AXIS, moves)  18.5 us
    all_to_all x2, starting transfers between devices, exchange(): lax.all_to_all(chunks, AXIS, 0, 0, axis_index_groups=groups, tiled=True)  18.2 us
    pallas_call x6, Pallas kernels, run(): pl.pallas_call(kernel, out_shape=outs, in_specs=specs, out_specs=[VMEM] *...  17.1 us
    ppermute x6, waiting for transfers between devices, shift(): lax.ppermute(block, AXIS, [((i - 4 * distance) % N, i) for i in range(N)])  16.3 us
    all_to_all x2, waiting for transfers between devices, exchange(): lax.all_to_all(chunks, AXIS, 0, 0, axis_index_groups=groups, tiled=True)  9.55 us
    unnamed x17, local copies, waits for them, and re-layouts  5.95 us
  transfers between devices with their start and end apart: 13, of which 6 were waited for; matrix products, arithmetic and copies ran while one was open for 1% of the time, Pallas kernels for 8%

profile of v4, /device:TPU:1, one launch (start us, length us, event | category | flops | bytes accessed | tf_op | source)
XLA Modules:
  0.0 164.8 jit_solution(4358544880312187497)
XLA Ops:
  0.6 0.0 copy-start
  0.6 5.3 %collective-permute-start.1 = (bf16[288,1152]{1,0:T(8,128)(2,1)}, bf16[288,1152]{1,0:T(8,128)(2,1)S(1)}, u32[]{:S(2)}, u32[]{:S(2)}) collective-permute-start(bf16[288,1152]{1,0:T(8,128)(2,1)} %shard0_ref.1), channel_id=1, source_target_pairs={{2,0},{35,1},{0,2},{33,3},{6,4},{39,5},{4,6},{37,7},{10,8},{43,9},... | collective-permute-start | bytes 1990664 | tf_op jit(solution)/shard_map/ppermute | solution.py:58
  6.0 0.0 copy-start.3
  6.0 1.1 copy-done.3
  7.1 0.0 copy-start.5
  7.1 0.7 copy-done.5
  7.7 0.2 shard_map.77.text_ref
  8.0 3.2 %collective-permute-start.2 = (bf16[272,1152]{1,0:T(8,128)(2,1)S(1)}, bf16[272,1152]{1,0:T(8,128)(2,1)S(1)}, u32[]{:S(2)}, u32[]{:S(2)}) collective-permute-start(bf16[272,1152]{1,0:T(8,128)(2,1)S(1)} %shard_map.77.text_ref), channel_id=1, source_target_pairs={{508,0},{509,1},{510,2},{511,3},{0,4},{1,5},{2,6},{3,7},{4,8},{5,9... | collective-permute-start | bytes 1880072 | tf_op jit(solution)/shard_map/ppermute | solution.py:54
  11.2 12.5 %collective-permute-start.4 = (bf16[256,1152]{1,0:T(8,128)(2,1)}, bf16[256,1152]{1,0:T(8,128)(2,1)}, u32[]{:S(2)}, u32[]{:S(2)}) collective-permute-start(bf16[256,1152]{1,0:T(8,128)(2,1)} %image0_ref.1), channel_id=1, source_target_pairs={{4,0},{5,1},{6,2},{7,3},{8,4},{9,5},{10,6},{11,7},{12,8},{13,9},{1... | collective-permute-start | bytes 1769480 | tf_op jit(solution)/shard_map/ppermute | solution.py:54
  23.7 3.8 %collective-permute-start = (bf16[288,1152]{1,0:T(8,128)(2,1)}, bf16[288,1152]{1,0:T(8,128)(2,1)S(1)}, u32[]{:S(2)}, u32[]{:S(2)}) collective-permute-start(bf16[288,1152]{1,0:T(8,128)(2,1)} %shard0_ref.1), channel_id=1, source_target_pairs={{1,0},{0,1},{3,2},{2,3},{5,4},{4,5},{7,6},{6,7},{9,8},{8,9},{11,10... | collective-permute-start | bytes 1990664 | tf_op jit(solution)/shard_map/ppermute | solution.py:58
  27.5 7.0 %collective-permute-done.2.text1_ref = bf16[272,1152]{1,0:T(8,128)(2,1)S(1)} collective-permute-done((bf16[272,1152]{1,0:T(8,128)(2,1)S(1)}, bf16[272,1152]{1,0:T(8,128)(2,1)S(1)}, u32[]{:S(2)}, u32[]{:S(2)}) %collective-permute-start.2) | collective-permute-done | bytes 626720 | tf_op jit(solution)/shard_map/ppermute | solution.py:54
  34.6 0.0 copy-start.1
  34.6 0.8 copy-done.1
  35.4 0.0 collective-permute-done.1.shard2_ref
  35.4 4.2 %collective-permute-start.3 = (bf16[288,1152]{1,0:T(8,128)(2,1)S(1)}, bf16[288,1152]{1,0:T(8,128)(2,1)S(1)}, u32[]{:S(2)}, u32[]{:S(2)}) collective-permute-start(bf16[288,1152]{1,0:T(8,128)(2,1)S(1)} %collective-permute-done.1.shard2_ref), channel_id=1, source_target_pairs={{1,0},{0,1},{3,2},{2,3},{5,4},{4,5},{7,6},{6,7},{9,8},{8,9},{11,10... | collective-permute-start | bytes 1990664 | tf_op jit(solution)/shard_map/ppermute | solution.py:58
  39.6 0.0 collective-permute-done.4.image1_ref
  39.6 5.2 %collective-permute-start.5 = (bf16[256,1152]{1,0:T(8,128)(2,1)}, bf16[256,1152]{1,0:T(8,128)(2,1)}, u32[]{:S(2)}, u32[]{:S(2)}) collective-permute-start(bf16[256,1152]{1,0:T(8,128)(2,1)} %collective-permute-done.4.image1_ref), channel_id=1, source_target_pairs={{4,0},{5,1},{6,2},{7,3},{8,4},{9,5},{10,6},{11,7},{12,8},{13,9},{1... | collective-permute-start | bytes 1769480 | tf_op jit(solution)/shard_map/ppermute | solution.py:54
  46.2 1.9 %collective-permute-start.7 = (s32[256]{0:T(256)}, s32[256]{0:T(256)S(1)}, u32[]{:S(2)}, u32[]{:S(2)}) collective-permute-start(s32[256]{0:T(256)} %param.9), channel_id=1, source_target_pairs={{4,0},{5,1},{6,2},{7,3},{8,4},{9,5},{10,6},{11,7},{12,8},{13,9},{1... | collective-permute-start | bytes 3080 | tf_op jit(solution)/shard_map/ppermute | solution.py:54
  48.1 4.1 %collective-permute-start.6 = (s32[256]{0:T(256)}, s32[256]{0:T(256)S(1)}, u32[]{:S(2)}, u32[]{:S(2)}) collective-permute-start(s32[256]{0:T(256)} %param.9), channel_id=1, source_target_pairs={{8,0},{9,1},{10,2},{11,3},{12,4},{13,5},{14,6},{15,7},{16,8},{17,9... | collective-permute-start | bytes 3080 | tf_op jit(solution)/shard_map/ppermute | solution.py:54
  52.2 0.0 collective-permute-done.shard1_ref
  52.2 0.0 collective-permute-done.3.shard3_ref
  52.3 0.0 copy-done
  52.3 0.0 copy-start.4
  52.3 1.1 copy-done.4
  53.3 0.0 copy-start.6
  53.3 0.7 copy-done.6
  54.0 0.0 copy-start.2
  54.0 3.3 %shard_map.78 = (bf16[1152,1152]{1,0:T(8,128)(2,1)S(1)}, bf16[256,1152]{1,0:T(8,128)(2,1)S(1)}, f32[256,1152]{1,0:T(8,128)S(1)}) custom-call(s32[1]{0:T(128)} %bitcast.grp_ref, f32[1]{0:T(128)S(6)} %copy.13.scale_ref, f32[1]{0:T(128)S(6)} %copy.14.bias_ref, bf16[288,1152]{1,0:T(8,128)(2,1)S(1)} %copy-done, ...), custom_call_target="tpu_custom_call" | custom-call | flops 679477248 | bytes 8295436 | tf_op jit(solution)/shard_map/pallas_call | solution.py:78
  57.3 0.0 collective-permute-done.7
  57.3 0.0 copy-done.2
  57.3 5.3 %shard_map.79 = (f32[1152,1152]{1,0:T(8,128)S(1)}, f32[256,1152]{1,0:T(8,128)S(1)}) custom-call(f32[1]{0:T(128)S(6)} %copy.13.scale_ref, f32[1]{0:T(128)S(6)} %copy.14.bias_ref, bf16[1152,1152]{1,0:T(8,128)(2,1)S(1)} %get-tuple-element.20.weight_ref, bf16[256,1152]{1,0:T(8,128)(2,1)S(1)} %copy-done.4, bf16[256,1152]{1,0:T(8,128)(2,1)S(1)} %get-tuple-element.23.raw_grad0_ref, ...), custom_call_target="tpu_custom_call" | custom-call | flops 2717908992 | bytes 13345800 | tf_op jit(solution)/shard_map/pallas_call | solution.py:78
  62.7 0.0 collective-permute-done.6
  62.7 0.0 collective-permute-done.5.image_ref
  62.7 4.5 %shard_map.80 = (bf16[576,1152]{1,0:T(8,128)(2,1)S(1)}, bf16[1152,256]{1,0:T(8,128)(2,1)S(1)}, bf16[256,1152]{1,0:T(8,128)(2,1)S(1)}, bf16[256,1152]{1,0:T(8,128)(2,1)S(1)}, bf16[256,256]{1,0:T(8,128)(2,1)S(1)}) custom-call(s32[1]{0:T(128)} %bitcast.grp_ref, f32[1]{0:T(128)S(6)} %copy.13.scale_ref, f32[1]{0:T(128)S(6)} %copy.14.bias_ref, ...), custom_call_target="tpu_custom_call" | custom-call | flops 1358954496 | bytes 12407820 | tf_op jit(solution)/shard_map/pallas_call | solution.py:78
  67.2 3.3 %collective-permute-start.8 = (bf16[576,1152]{1,0:T(8,128)(2,1)S(1)}, bf16[576,1152]{1,0:T(8,128)(2,1)S(1)}, u32[]{:S(2)}, u32[]{:S(2)}) collective-permute-start(bf16[576,1152]{1,0:T(8,128)(2,1)S(1)} %get-tuple-element.31), channel_id=1, source_target_pairs={{1,0},{0,1},{3,2},{2,3},{5,4},{4,5},{7,6},{6,7},{9,8},{8,9},{11,10... | collective-permute-start | bytes 3981320 | tf_op jit(solution)/shard_map/ppermute | solution.py:58
  70.5 1.7 %shard_map.81 = (bf16[576,1152]{1,0:T(8,128)(2,1)S(1)}, bf16[256,1152]{1,0:T(8,128)(2,1)S(1)}) custom-call(s32[1]{0:T(128)} %bitcast.grp_ref, bf16[1152,256]{1,0:T(8,128)(2,1)S(1)} %get-tuple-element.26.turned_ref, bf16[256,1152]{1,0:T(8,128)(2,1)S(1)} %get-tuple-element.27.raw_grad_ref, ...), custom_call_target="tpu_custom_call" | custom-call | flops 679477248 | bytes 9125892 | tf_op jit(solution)/shard_map/pallas_call | solution.py:78
  72.2 0.0 copy-start.7
  72.2 1.0 collective-permute-done.8
  73.2 1.4 add_convert_fusion
  74.6 0.0 copy-done.7
  74.6 9.5 %all-to-all-start = ((bf16[8,72,1152]{2,1,0:T(8,128)(2,1)}), bf16[8,72,1152]{2,1,0:T(8,128)(2,1)}, u32[]{:S(2)}, u32[]{:S(2)}) async-start(bf16[8,72,1152]{2,1,0:T(8,128)(2,1)} %bitcast.24), calls=%async_computation | async-start | bytes 2654208 | tf_op jit(solution)/shard_map/all_to_all | solution.py:62
  84.1 4.8 %collective-permute-start.9 = (bf16[256,1152]{1,0:T(8,128)(2,1)}, bf16[256,1152]{1,0:T(8,128)(2,1)S(1)}, u32[]{:S(2)}, u32[]{:S(2)}) collective-permute-start(bf16[256,1152]{1,0:T(8,128)(2,1)} %copy-done.7), channel_id=1, source_target_pairs={{4,0},{5,1},{6,2},{7,3},{8,4},{9,5},{10,6},{11,7},{12,8},{13,9},{1... | collective-permute-start | bytes 1769480 | tf_op jit(solution)/shard_map/ppermute | solution.py:54
  88.9 6.2 %all-to-all-done = bf16[8,72,1152]{2,1,0:T(8,128)(2,1)} async-done(((bf16[8,72,1152]{2,1,0:T(8,128)(2,1)}), bf16[8,72,1152]{2,1,0:T(8,128)(2,1)}, u32[]{:S(2)}, u32[]{:S(2)}) %all-to-all-start) | async-done | bytes 1327136 | tf_op jit(solution)/shard_map/all_to_all | solution.py:62
  95.2 1.5 reduce_sum.24
  96.7 9.3 %collective-permute-done.9.back_ref = bf16[256,1152]{1,0:T(8,128)(2,1)S(1)} collective-permute-done((bf16[256,1152]{1,0:T(8,128)(2,1)}, bf16[256,1152]{1,0:T(8,128)(2,1)S(1)}, u32[]{:S(2)}, u32[]{:S(2)}) %collective-permute-start.9) | collective-permute-done | bytes 589856 | tf_op jit(solution)/shard_map/ppermute | solution.py:54
  105.9 0.1 reshape.44
  106.1 19.0 %all_to_all.20 = bf16[16,48,128]{2,1,0:T(8,128)(2,1)S(1)} all-to-all(bf16[16,48,128]{2,1,0:T(8,128)(2,1)S(1)} %bitcast.28), channel_id=1, replica_groups={{0,8,16,24,128,136,144,152,256,264,272,280,384,392,400,408},{1,9,17,25,..., dimensions={0} | all-to-all | bytes 393216 | tf_op jit(solution)/shard_map/all_to_all | solution.py:62
  125.2 1.9 %collective-permute-start.10 = (bf16[48,128]{1,0:T(8,128)(2,1)S(1)}, bf16[48,128]{1,0:T(8,128)(2,1)S(1)}, u32[]{:S(2)}, u32[]{:S(2)}) collective-permute-start(bf16[48,128]{1,0:T(8,128)(2,1)S(1)} %reduce_sum.25), channel_id=1, source_target_pairs={{32,0},{33,1},{34,2},{35,3},{36,4},{37,5},{38,6},{39,7},{40,8},{41... | collective-permute-start | bytes 36872 | tf_op jit(solution)/shard_map/ppermute | solution.py:58
  127.1 4.0 %collective-permute-done.10 = bf16[48,128]{1,0:T(8,128)(2,1)S(1)} collective-permute-done((bf16[48,128]{1,0:T(8,128)(2,1)S(1)}, bf16[48,128]{1,0:T(8,128)(2,1)S(1)}, u32[]{:S(2)}, u32[]{:S(2)}) %collective-permute-start.10) | collective-permute-done | bytes 12320 | tf_op jit(solution)/shard_map/ppermute | solution.py:58
  131.2 15.3 %all_to_all.21 = bf16[16,48,128]{2,1,0:T(8,128)(2,1)S(1)} all-to-all(bf16[16,48,128]{2,1,0:T(8,128)(2,1)S(1)} %broadcast_in_dim.4), channel_id=1, replica_groups={{0,8,16,24,128,136,144,152,256,264,272,280,384,392,400,408},{1,9,17,25,..., dimensions={0} | all-to-all | bytes 393216 | tf_op jit(solution)/shard_map/all_to_all | solution.py:62
  146.4 1.0 broadcast_in_dim.5
  147.4 8.7 %all-to-all-start.3 = ((bf16[4,704,128]{2,1,0:T(8,128)(2,1)}), bf16[4,704,128]{2,1,0:T(8,128)(2,1)}, u32[]{:S(2)}, u32[]{:S(2)}) async-start(bf16[4,704,128]{2,1,0:T(8,128)(2,1)} %broadcast_in_dim.5), calls=%async_computation.3 | async-start | bytes 1441792 | tf_op jit(solution)/shard_map/all_to_all | solution.py:62
  156.1 2.1 %shard_map.82 = f32[256,1152]{1,0:T(8,128)} custom-call(f32[1]{0:T(128)S(6)} %copy.13.scale_ref, f32[1]{0:T(128)S(6)} %copy.14.bias_ref, bf16[256,1152]{1,0:T(8,128)(2,1)S(1)} %get-tuple-element.28.image_unit_ref.image_unit2_ref, s32[1,256]{1,0:T(1,128)S(1)} %bitcast.19, bf16[272,1152]{1,0:T(8,128)(2,1)S(1)} %shard_map.77.text_ref, ...), custom_call_target="tpu_custom_call" | custom-call | flops 679477248 | bytes 4166664 | tf_op jit(solution)/shard_map/pallas_call | solution.py:78
  158.2 3.3 %all-to-all-done.3 = bf16[4,704,128]{2,1,0:T(8,128)(2,1)} async-done(((bf16[4,704,128]{2,1,0:T(8,128)(2,1)}), bf16[4,704,128]{2,1,0:T(8,128)(2,1)}, u32[]{:S(2)}, u32[]{:S(2)}) %all-to-all-start.3) | async-done | bytes 720928 | tf_op jit(solution)/shard_map/all_to_all | solution.py:62
  161.5 1.1 slice.9
  162.7 0.1 convert_bitcast_fusion
  162.8 0.4 copy.9
  163.1 1.6 copy.12
  (6 shorter events, 0.1 us)
Async XLA Ops:
  0.6 51.6 %copy-start = (bf16[288,1152]{1,0:T(8,128)(2,1)S(1)}, bf16[288,1152]{1,0:T(8,128)(2,1)}, u32[]{:S(2)}) copy-start(bf16[288,1152]{1,0:T(8,128)(2,1)} %shard0_ref.1) | copy-start | bytes 1990660
  0.6 34.8 %collective-permute-start.1 = (bf16[288,1152]{1,0:T(8,128)(2,1)}, bf16[288,1152]{1,0:T(8,128)(2,1)S(1)}, u32[]{:S(2)}, u32[]{:S(2)}) collective-permute-start(bf16[288,1152]{1,0:T(8,128)(2,1)} %shard0_ref.1), channel_id=1, source_target_pairs={{2,0},{35,1},{0,2},{33,3},{6,4},{39,5},{4,6},{37,7},{10,8},{43,9},... | collective-permute-start | bytes 1990664 | tf_op jit(solution)/shard_map/ppermute | solution.py:58
  6.0 1.1 copy-start.3
  7.1 0.7 copy-start.5
  8.0 26.6 %collective-permute-start.2 = (bf16[272,1152]{1,0:T(8,128)(2,1)S(1)}, bf16[272,1152]{1,0:T(8,128)(2,1)S(1)}, u32[]{:S(2)}, u32[]{:S(2)}) collective-permute-start(bf16[272,1152]{1,0:T(8,128)(2,1)S(1)} %shard_map.77.text_ref), channel_id=1, source_target_pairs={{508,0},{509,1},{510,2},{511,3},{0,4},{1,5},{2,6},{3,7},{4,8},{5,9... | collective-permute-start | bytes 1880072 | tf_op jit(solution)/shard_map/ppermute | solution.py:54
  11.2 28.4 %collective-permute-start.4 = (bf16[256,1152]{1,0:T(8,128)(2,1)}, bf16[256,1152]{1,0:T(8,128)(2,1)}, u32[]{:S(2)}, u32[]{:S(2)}) collective-permute-start(bf16[256,1152]{1,0:T(8,128)(2,1)} %image0_ref.1), channel_id=1, source_target_pairs={{4,0},{5,1},{6,2},{7,3},{8,4},{9,5},{10,6},{11,7},{12,8},{13,9},{1... | collective-permute-start | bytes 1769480 | tf_op jit(solution)/shard_map/ppermute | solution.py:54
  23.7 28.5 %collective-permute-start = (bf16[288,1152]{1,0:T(8,128)(2,1)}, bf16[288,1152]{1,0:T(8,128)(2,1)S(1)}, u32[]{:S(2)}, u32[]{:S(2)}) collective-permute-start(bf16[288,1152]{1,0:T(8,128)(2,1)} %shard0_ref.1), channel_id=1, source_target_pairs={{1,0},{0,1},{3,2},{2,3},{5,4},{4,5},{7,6},{6,7},{9,8},{8,9},{11,10... | collective-permute-start | bytes 1990664 | tf_op jit(solution)/shard_map/ppermute | solution.py:58
  34.6 0.8 copy-start.1
  35.4 16.8 %collective-permute-start.3 = (bf16[288,1152]{1,0:T(8,128)(2,1)S(1)}, bf16[288,1152]{1,0:T(8,128)(2,1)S(1)}, u32[]{:S(2)}, u32[]{:S(2)}) collective-permute-start(bf16[288,1152]{1,0:T(8,128)(2,1)S(1)} %collective-permute-done.1.shard2_ref), channel_id=1, source_target_pairs={{1,0},{0,1},{3,2},{2,3},{5,4},{4,5},{7,6},{6,7},{9,8},{8,9},{11,10... | collective-permute-start | bytes 1990664 | tf_op jit(solution)/shard_map/ppermute | solution.py:58
  39.6 23.1 %collective-permute-start.5 = (bf16[256,1152]{1,0:T(8,128)(2,1)}, bf16[256,1152]{1,0:T(8,128)(2,1)}, u32[]{:S(2)}, u32[]{:S(2)}) collective-permute-start(bf16[256,1152]{1,0:T(8,128)(2,1)} %collective-permute-done.4.image1_ref), channel_id=1, source_target_pairs={{4,0},{5,1},{6,2},{7,3},{8,4},{9,5},{10,6},{11,7},{12,8},{13,9},{1... | collective-permute-start | bytes 1769480 | tf_op jit(solution)/shard_map/ppermute | solution.py:54
  46.2 11.2 %collective-permute-start.7 = (s32[256]{0:T(256)}, s32[256]{0:T(256)S(1)}, u32[]{:S(2)}, u32[]{:S(2)}) collective-permute-start(s32[256]{0:T(256)} %param.9), channel_id=1, source_target_pairs={{4,0},{5,1},{6,2},{7,3},{8,4},{9,5},{10,6},{11,7},{12,8},{13,9},{1... | collective-permute-start | bytes 3080 | tf_op jit(solution)/shard_map/ppermute | solution.py:54
  48.1 14.6 %collective-permute-start.6 = (s32[256]{0:T(256)}, s32[256]{0:T(256)S(1)}, u32[]{:S(2)}, u32[]{:S(2)}) collective-permute-start(s32[256]{0:T(256)} %param.9), channel_id=1, source_target_pairs={{8,0},{9,1},{10,2},{11,3},{12,4},{13,5},{14,6},{15,7},{16,8},{17,9... | collective-permute-start | bytes 3080 | tf_op jit(solution)/shard_map/ppermute | solution.py:54
  52.3 1.1 copy-start.4
  53.3 0.7 copy-start.6
  54.0 3.3 %copy-start.2 = (bf16[272,1152]{1,0:T(8,128)(2,1)S(1)}, bf16[272,1152]{1,0:T(8,128)(2,1)}, u32[]{:S(2)}) copy-start(bf16[272,1152]{1,0:T(8,128)(2,1)} %copy-done.1) | copy-start | bytes 1880068
  67.2 6.0 %collective-permute-start.8 = (bf16[576,1152]{1,0:T(8,128)(2,1)S(1)}, bf16[576,1152]{1,0:T(8,128)(2,1)S(1)}, u32[]{:S(2)}, u32[]{:S(2)}) collective-permute-start(bf16[576,1152]{1,0:T(8,128)(2,1)S(1)} %get-tuple-element.31), channel_id=1, source_target_pairs={{1,0},{0,1},{3,2},{2,3},{5,4},{4,5},{7,6},{6,7},{9,8},{8,9},{11,10... | collective-permute-start | bytes 3981320 | tf_op jit(solution)/shard_map/ppermute | solution.py:58
  72.2 2.4 %copy-start.7 = (bf16[256,1152]{1,0:T(8,128)(2,1)}, bf16[256,1152]{1,0:T(8,128)(2,1)S(1)}, u32[]{:S(2)}) copy-start(bf16[256,1152]{1,0:T(8,128)(2,1)S(1)} %get-tuple-element.32) | copy-start | bytes 1769476
  74.6 20.5 %all-to-all-start = ((bf16[8,72,1152]{2,1,0:T(8,128)(2,1)}), bf16[8,72,1152]{2,1,0:T(8,128)(2,1)}, u32[]{:S(2)}, u32[]{:S(2)}) async-start(bf16[8,72,1152]{2,1,0:T(8,128)(2,1)} %bitcast.24), calls=%async_computation | async-start | bytes 2654208 | tf_op jit(solution)/shard_map/all_to_all | solution.py:62
  84.1 21.8 %collective-permute-start.9 = (bf16[256,1152]{1,0:T(8,128)(2,1)}, bf16[256,1152]{1,0:T(8,128)(2,1)S(1)}, u32[]{:S(2)}, u32[]{:S(2)}) collective-permute-start(bf16[256,1152]{1,0:T(8,128)(2,1)} %copy-done.7), channel_id=1, source_target_pairs={{4,0},{5,1},{6,2},{7,3},{8,4},{9,5},{10,6},{11,7},{12,8},{13,9},{1... | collective-permute-start | bytes 1769480 | tf_op jit(solution)/shard_map/ppermute | solution.py:54
  125.2 5.9 %collective-permute-start.10 = (bf16[48,128]{1,0:T(8,128)(2,1)S(1)}, bf16[48,128]{1,0:T(8,128)(2,1)S(1)}, u32[]{:S(2)}, u32[]{:S(2)}) collective-permute-start(bf16[48,128]{1,0:T(8,128)(2,1)S(1)} %reduce_sum.25), channel_id=1, source_target_pairs={{32,0},{33,1},{34,2},{35,3},{36,4},{37,5},{38,6},{39,7},{40,8},{41... | collective-permute-start | bytes 36872 | tf_op jit(solution)/shard_map/ppermute | solution.py:58
  147.4 14.1 %all-to-all-start.3 = ((bf16[4,704,128]{2,1,0:T(8,128)(2,1)}), bf16[4,704,128]{2,1,0:T(8,128)(2,1)}, u32[]{:S(2)}, u32[]{:S(2)}) async-start(bf16[4,704,128]{2,1,0:T(8,128)(2,1)} %broadcast_in_dim.5), calls=%async_computation.3 | async-start | bytes 1441792 | tf_op jit(solution)/shard_map/all_to_all | solution.py:62

commit v5 on v4

--- a/solution.py
+++ b/solution.py
@@ -47,6 +47,9 @@
 FIRST = grouped(lambda z, x, y, xl, core: (z // 2, x // 2, y // 2, core), lambda z, x, y, xl, core: (xl, z % 2, y % 2))
 NEAR = grouped(lambda z, x, y, xl, core: (z // 2, x, y // 2, core), lambda z, x, y, xl, core: (z % 2, y % 2))
 FAR = grouped(lambda z, x, y, xl, core: (z % 2, x, y % 2, core), lambda z, x, y, xl, core: (z // 2, y // 2))
+EVEN, ODD = (
+    [[blk * 4 + grp, (blk + 1) * 4 % N + grp] for blk in range(first, 128, 2) for grp in range(4)] for first in range(2)
+)
 CORES = [(i ^ 1, i) for i in range(N)]
 
 
@@ -94,27 +97,36 @@
     return jnp.where(first, ids, 0.0).astype(BF)
 
 
-def prepare_kernel(text_ref, ids_ref, out_ref):
+def put_ids(ids_ref, out_ref):
+    out_ref[ROWS:, :ROWS] = top_row(ids_ref)
+    out_ref[ROWS:, ROWS:] = jnp.zeros((16, D - ROWS), BF)
+
+
+def pack_kernel(feats_ref, ids_ref, out_ref):
+    out_ref[:ROWS, :] = feats_ref[...]
+    put_ids(ids_ref, out_ref)
+
+
+def text_kernel(text_ref, ids_ref, out_ref):
     rows = text_ref[...].astype(F32)
     inverse = 1.0 / jnp.sqrt(jnp.sum(rows * rows, -1, keepdims=True) + 1e-06)
     out_ref[:ROWS, :] = (rows * inverse).astype(BF)
-    out_ref[ROWS:, :ROWS] = top_row(ids_ref)
-    out_ref[ROWS:, ROWS:] = jnp.zeros((16, D - ROWS), BF)
+    put_ids(ids_ref, out_ref)
 
 
 def project(image_ref, weight_ref):
-    raw = jnp.dot(image_ref[...], weight_ref[...], preferred_element_type=F32)
+    raw = jnp.dot(image_ref[:ROWS, :], weight_ref[...], preferred_element_type=F32)
     inverse = 1.0 / jnp.sqrt(jnp.sum(raw * raw, -1, keepdims=True) + 1e-06)
     unit = raw * inverse
     return unit, unit.astype(BF), inverse
 
 
-def ids_down(ids_ref):
-    return across(top_row(ids_ref), jnp.ones((16, ROWS), BF))
+def ids_down(packed_ref):
+    return across(packed_ref[ROWS:, :ROWS], jnp.ones((16, ROWS), BF))
 
 
 def turn(image_ref):
-    return image_ref[...].astype(F32).T.astype(BF)
+    return image_ref[:ROWS, :].astype(F32).T.astype(BF)
 
 
 def pair(image_unit, ids, text_ref, scale, bias):
@@ -140,7 +152,7 @@
 
 
 def own_kernel(
-    grp_ref, scale_ref, bias_ref, shard0_ref, shard1_ref, shard2_ref, shard3_ref, image_ref, ids_ref, text_ref, weight_ref, raw_grad_ref, grad_ref, sems
+    grp_ref, scale_ref, bias_ref, shard0_ref, shard1_ref, shard2_ref, shard3_ref, image_ref, text_ref, weight_ref, raw_grad_ref, grad_ref, sems
 ):
     grp = grp_ref[0]
     loads = []
@@ -152,14 +164,14 @@
         load.wait()
     scale, bias = scale_ref[0], bias_ref[0]
     unit, image_unit, inverse = project(image_ref, weight_ref)
-    near = pair(image_unit, ids_down(ids_ref), text_ref, scale, bias)
+    near = pair(image_unit, ids_down(image_ref), text_ref, scale, bias)
     grad_ref[...] = across(near, image_unit)
     image_grad = scale * jnp.dot(near, text_ref[:ROWS, :], preferred_element_type=F32)
     raw_grad_ref[...] = back(image_grad, unit, inverse)
 
 
 def next_kernel(
-    scale_ref, bias_ref, weight_ref, image0_ref, raw_grad0_ref, image1_ref, ids_ref, text_ref, text1_ref, grad0_ref, part_ref, grad_ref,
+    scale_ref, bias_ref, weight_ref, image0_ref, raw_grad0_ref, image1_ref, text_ref, text1_ref, grad0_ref, part_ref, grad_ref,
     turned_ref, raw_grads_ref
 ):
     turned_ref[:, :ROWS] = turn(image0_ref)
@@ -167,7 +179,7 @@
     raw_grads_ref[:ROWS, :] = raw_grad0_ref[...]
     scale, bias = scale_ref[0], bias_ref[0]
     unit, image_unit, inverse = project(image1_ref, weight_ref)
-    ids = ids_down(ids_ref)
+    ids = ids_down(image1_ref)
     near = pair(image_unit, ids, text_ref, scale, bias)
     far = pair(image_unit, ids, text1_ref, scale, bias)
     grad_ref[...] = grad0_ref[...] + across(near, image_unit)
@@ -205,7 +217,7 @@
 
 
 def last_kernel(
-    grp_ref, scale_ref, bias_ref, weight_ref, image_ref, ids_ref, text1_ref, part_ref,
+    grp_ref, scale_ref, bias_ref, weight_ref, image_ref, text1_ref, part_ref,
     send_ref, turned_ref, raw_grad_ref, image_unit_ref, far_ref, rows_ref, sems
 ):
     core = 1 - grp_ref[0] % 2
@@ -214,7 +226,7 @@
     turned_ref[...] = turn(image_ref)
     unit, image_unit, inverse = project(image_ref, weight_ref)
     image_unit_ref[...] = image_unit
-    far = pair(image_unit, ids_down(ids_ref), text1_ref, scale, bias)
+    far = pair(image_unit, ids_down(image_ref), text1_ref, scale, bias)
     far_ref[...] = far
     image_grad = scale * jnp.dot(far, text1_ref[:ROWS, :], preferred_element_type=F32)
     raw_grad = back(image_grad, unit, inverse)
@@ -229,10 +241,11 @@
     back_ref[...] = across(far_ref[...], image_unit_ref[...]).astype(BF)
 
 
-def finish_kernel(scale_ref, bias_ref, image_unit2_ref, ids2_ref, text_ref, grad_ref, back_ref, out_ref):
+def finish_kernel(odd_ref, scale_ref, bias_ref, image_unit2_ref, image2_ref, text_ref, grad_ref, even_back_ref, odd_back_ref, out_ref):
     image_unit2 = image_unit2_ref[...]
-    near2 = pair(image_unit2, ids_down(ids2_ref), text_ref, scale_ref[0], bias_ref[0])
-    out_ref[...] = scale_ref[0] * (grad_ref[...] + across(near2, image_unit2) + back_ref[...].astype(F32))
+    back = jnp.where(odd_ref[0] == 1, odd_back_ref[1], even_back_ref[1]).astype(F32)
+    near2 = pair(image_unit2, ids_down(image2_ref), text_ref, scale_ref[0], bias_ref[0])
+    out_ref[...] = scale_ref[0] * (grad_ref[...] + across(near2, image_unit2) + back)
 
 
 def shape(rows, columns, dtype):
@@ -246,35 +259,35 @@
     flops = 2 * ROWS * D * D
     anywhere = pl.BlockSpec(memory_space=pl.ANY)
     scratch = [pltpu.VMEM((2 * SHARD, D), F32), pltpu.SemaphoreType.DMA((2,))]
-    ids = [row_ids.reshape(1, ROWS)]
-    text0 = call(prepare_kernel, [packed], [VMEM] * 2, ROWS)(text_embed, ids[0])[0]
+    ids = row_ids.reshape(1, ROWS)
+    image0 = call(pack_kernel, [packed], [VMEM] * 2, ROWS)(feats, ids)[0]
+    image0, text_embed = lax.optimization_barrier((image0, text_embed))
+    text0 = call(text_kernel, [packed], [VMEM] * 2, ROWS)(text_embed, ids)[0]
     shard1 = move(proj_weight, CORES)
     shard2 = move(proj_weight, swap_x((1, 3)))
-    image1 = shift(feats, -1)
+    image1 = shift(image0, -1)
+    shard2, text0 = lax.optimization_barrier((shard2, text0))
+    shard3 = move(shard2, CORES)
     text1 = shift(text0, 1)
     image2 = shift(image1, -1)
-    late_ids = lax.optimization_barrier((row_ids, shard2))[0]
-    ids += [shift(late_ids, -distance).reshape(1, ROWS) for distance in (1, 2)]
-    shard2, text1 = lax.optimization_barrier((shard2, text1))
-    shard3 = move(shard2, CORES)
     weight, raw_grad0, grad = call(
-        own_kernel, [shape(D, D, BF), shape(ROWS, D, BF), shape(ROWS, D, F32)], [SMEM] * 3 + [anywhere] * 4 + [VMEM] * 3, flops,
+        own_kernel, [shape(D, D, BF), shape(ROWS, D, BF), shape(ROWS, D, F32)], [SMEM] * 3 + [anywhere] * 4 + [VMEM] * 2, flops,
         [pltpu.SemaphoreType.DMA((4,))],
-    )(grp, *numbers, proj_weight, shard1, shard2, shard3, feats, ids[0], text0)
+    )(grp, *numbers, proj_weight, shard1, shard2, shard3, image0, text0)
     part, grad = call(
         next_kernel,
         [shape(D, D, F32), shape(ROWS, D, F32)],
-        [SMEM] * 2 + [VMEM] * 8,
+        [SMEM] * 2 + [VMEM] * 7,
         4 * flops,
         [pltpu.VMEM((D, 2 * ROWS), BF), pltpu.VMEM((2 * ROWS, D), BF)],
-    )(*numbers, weight, feats, raw_grad0, image1, ids[1], text0, text1, grad)
+    )(*numbers, weight, image0, raw_grad0, image1, text0, text1, grad)
     send, turned, raw_grad2, image_unit2, far = call(
         last_kernel,
         [shape(2 * SHARD, D, BF), shape(D, ROWS, BF), shape(ROWS, D, BF), shape(ROWS, D, BF), shape(ROWS, ROWS, BF)],
-        [SMEM] * 3 + [VMEM] * 4 + [anywhere],
+        [SMEM] * 3 + [VMEM] * 3 + [anywhere],
         2 * flops,
         scratch,
-    )(grp, *numbers, weight, image2, ids[2], text1, part)
+    )(grp, *numbers, weight, image2, text1, part)
     keep, term = call(
         keep_kernel,
         [shape(2 * SHARD, D, BF), shape(ROWS, D, BF)],
@@ -282,10 +295,10 @@
         flops,
         scratch,
     )(grp, turned, raw_grad2, image_unit2, far, part)
-    term = shift(term, -1)
+    even = lax.all_gather(term, AXIS, axis_index_groups=EVEN)
+    odd = lax.all_gather(term, AXIS, axis_index_groups=ODD)
     halves = (keep.astype(F32) + move(send, CORES).astype(F32)).astype(BF)
     mine = total(exchange(halves.reshape(8, SUB, D), FIRST))
-    mine, term = lax.optimization_barrier((mine, term))
     tiles = mine.reshape(SUB, 9, 128).transpose(1, 0, 2).reshape(SUB * 9, 128)
     tiles = jnp.pad(tiles, ((0, 768 - SUB * 9), (0, 0))).reshape(16, 48, 128)
     done = total(exchange(tiles, FAR))
@@ -293,8 +306,8 @@
     done = spread(done, FAR).reshape(768, 128)[:704]
     done = spread(done, NEAR)[:, : SUB * 9]
     weight_grad = done.reshape(4, 9, SUB, 128).transpose(0, 2, 1, 3).reshape(SHARD, D).astype(F32)
-    text_grad = call(finish_kernel, [shape(ROWS, D, F32)], [SMEM] * 2 + [VMEM] * 5, flops)(
-        *numbers, image_unit2, ids[2], text0, grad, term
+    text_grad = call(finish_kernel, [shape(ROWS, D, F32)], [SMEM] * 3 + [VMEM] * 6, flops)(
+        (lax.axis_index("blk") % 2).astype(jnp.int32).reshape(1), *numbers, image_unit2, image2, text0, grad, even, odd
     )[0]
     return (weight_grad, text_grad)
 

time: 166 us -> 186 us (1.12)
  waiting for transfers between devices: 30.9 us -> 58 us
  blocking collectives: 34.3 us -> 14.4 us
  between operations: 2.21 us -> 15.6 us
  starting transfers between devices: 68.6 us -> 63.8 us
  local copies, waits for them, and re-layouts: 8.6 us -> 11 us
  Pallas kernels: 17.1 us -> 19 us
    all_to_all x2 -> x1, blocking collectives: 34.3 us -> 14.4 us  [exchange(): lax.all_to_all(chunks, AXIS, 0, 0, axis_index_groups=groups, tiled=True)]
    all_gather x0 -> x2, waiting for transfers between devices: none -> 18.9 us  [the longest x1 18.9 us: on_device(): even = lax.all_gather(term, AXIS, axis_index_groups=EVEN)]
    all_to_all x2 -> x3, waiting for transfers between devices: 9.55 us -> 21.2 us  [exchange(): lax.all_to_all(chunks, AXIS, 0, 0, axis_index_groups=groups, tiled=True)]
    ppermute x6 -> x3, waiting for transfers between devices: 16.3 us -> 9.4 us  [shift(): lax.ppermute(block, AXIS, [((i - 4 * distance) % N, i) for i in range(N)])]
    ppermute x5, waiting for transfers between devices: 5.01 us -> 7.03 us  [move(): return lax.ppermute(block, AXIS, moves)]
    ppermute x5, starting transfers between devices: 18.5 us -> 16.6 us  [move(): return lax.ppermute(block, AXIS, moves)]
    pallas_call x6 -> x7, Pallas kernels: 17.1 us -> 19 us  [run(): pl.pallas_call(kernel, out_shape=outs, in_specs=specs, out_specs=[VMEM] *...]
    all_to_all x2 -> x3, starting transfers between devices: 18.2 us -> 16.5 us  [exchange(): lax.all_to_all(chunks, AXIS, 0, 0, axis_index_groups=groups, tiled=True)]
  transfers between devices with their start and end apart: 13 -> 13, of which waited for: 6 -> 7; matrix products, arithmetic and copies ran while one was open for 1% -> 2% of each run, Pallas kernels for 8% -> 8%
where the time goes in v5:
time: 186 us; the launch traced here: 185 us
  starting transfers between devices  63.8 us (34%)
  waiting for transfers between devices  58 us (31%)
  Pallas kernels  19 us (10%)
  between operations  15.6 us (8%)
  blocking collectives  14.4 us (8%)
  local copies, waits for them, and re-layouts  11 us (6%)
  other arithmetic  3.03 us (2%)
    ppermute x3, starting transfers between devices, shift(): lax.ppermute(block, AXIS, [((i - 4 * distance) % N, i) for i in range(N)])  30.7 us
    all_to_all x3, waiting for transfers between devices, exchange(): lax.all_to_all(chunks, AXIS, 0, 0, axis_index_groups=groups, tiled=True)  21.2 us
    pallas_call x7, Pallas kernels, run(): pl.pallas_call(kernel, out_shape=outs, in_specs=specs, out_specs=[VMEM] *...  19 us
    all_gather x1, waiting for transfers between devices, on_device(): even = lax.all_gather(term, AXIS, axis_index_groups=EVEN)  18.9 us
    ppermute x5, starting transfers between devices, move(): return lax.ppermute(block, AXIS, moves)  16.6 us
    all_to_all x3, starting transfers between devices, exchange(): lax.all_to_all(chunks, AXIS, 0, 0, axis_index_groups=groups, tiled=True)  16.5 us
    all_to_all x1, blocking collectives, exchange(): lax.all_to_all(chunks, AXIS, 0, 0, axis_index_groups=groups, tiled=True)  14.4 us
    ppermute x3, waiting for transfers between devices, shift(): lax.ppermute(block, AXIS, [((i - 4 * distance) % N, i) for i in range(N)])  9.4 us
  transfers between devices with their start and end apart: 13, of which 7 were waited for; matrix products, arithmetic and copies ran while one was open for 2% of the time, Pallas kernels for 8%

profile of v5, /device:TPU:1, one launch (start us, length us, event | category | flops | bytes accessed | tf_op | source)
XLA Modules:
  0.0 184.8 jit_solution(14101742459212659321)
XLA Ops:
  7.2 0.0 copy-start.2
  7.2 5.3 %collective-permute-start.1 = (bf16[288,1152]{1,0:T(8,128)(2,1)}, bf16[288,1152]{1,0:T(8,128)(2,1)S(1)}, u32[]{:S(2)}, u32[]{:S(2)}) collective-permute-start(bf16[288,1152]{1,0:T(8,128)(2,1)} %shard0_ref.1), channel_id=1, source_target_pairs={{2,0},{35,1},{0,2},{33,3},{6,4},{39,5},{4,6},{37,7},{10,8},{43,9},... | collective-permute-start | bytes 1990664 | tf_op jit(solution)/shard_map/ppermute | solution.py:61
  12.5 0.0 copy-start.3
  12.5 1.1 copy-done.3
  13.6 0.0 copy-start.5
  13.6 0.7 copy-done.5
  14.3 13.8 %collective-permute-start.3 = (bf16[272,1152]{1,0:T(8,128)(2,1)S(1)}, bf16[272,1152]{1,0:T(8,128)(2,1)}, u32[]{:S(2)}, u32[]{:S(2)}) collective-permute-start(bf16[272,1152]{1,0:T(8,128)(2,1)S(1)} %shard_map.77.image_ref.image0_ref), channel_id=1, source_target_pairs={{4,0},{5,1},{6,2},{7,3},{8,4},{9,5},{10,6},{11,7},{12,8},{13,9},{1... | collective-permute-start | bytes 1880072 | tf_op jit(solution)/shard_map/ppermute | solution.py:57
  28.1 3.8 %collective-permute-start = (bf16[288,1152]{1,0:T(8,128)(2,1)}, bf16[288,1152]{1,0:T(8,128)(2,1)}, u32[]{:S(2)}, u32[]{:S(2)}) collective-permute-start(bf16[288,1152]{1,0:T(8,128)(2,1)} %shard0_ref.1), channel_id=1, source_target_pairs={{1,0},{0,1},{3,2},{2,3},{5,4},{4,5},{7,6},{6,7},{9,8},{8,9},{11,10... | collective-permute-start | bytes 1990664 | tf_op jit(solution)/shard_map/ppermute | solution.py:61
  32.0 0.0 copy-start.4
  32.0 1.1 copy-done.4
  33.0 0.0 copy-start.6
  33.0 0.7 copy-done.6
  33.7 0.2 shard_map.78.text_ref
  33.9 0.0 collective-permute-done.1.shard2_ref
  34.0 1.9 %collective-permute-start.2 = (bf16[288,1152]{1,0:T(8,128)(2,1)S(1)}, bf16[288,1152]{1,0:T(8,128)(2,1)}, u32[]{:S(2)}, u32[]{:S(2)}) collective-permute-start(bf16[288,1152]{1,0:T(8,128)(2,1)S(1)} %collective-permute-done.1.shard2_ref), channel_id=1, source_target_pairs={{1,0},{0,1},{3,2},{2,3},{5,4},{4,5},{7,6},{6,7},{9,8},{8,9},{11,10... | collective-permute-start | bytes 1990664 | tf_op jit(solution)/shard_map/ppermute | solution.py:61
  35.9 1.9 %collective-permute-start.5 = (bf16[272,1152]{1,0:T(8,128)(2,1)S(1)}, bf16[272,1152]{1,0:T(8,128)(2,1)}, u32[]{:S(2)}, u32[]{:S(2)}) collective-permute-start(bf16[272,1152]{1,0:T(8,128)(2,1)S(1)} %shard_map.78.text_ref), channel_id=1, source_target_pairs={{508,0},{509,1},{510,2},{511,3},{0,4},{1,5},{2,6},{3,7},{4,8},{5,9... | collective-permute-start | bytes 1880072 | tf_op jit(solution)/shard_map/ppermute | solution.py:57
  37.8 2.1 %collective-permute-done.3.image1_ref = bf16[272,1152]{1,0:T(8,128)(2,1)} collective-permute-done((bf16[272,1152]{1,0:T(8,128)(2,1)S(1)}, bf16[272,1152]{1,0:T(8,128)(2,1)}, u32[]{:S(2)}, u32[]{:S(2)}) %collective-permute-start.3) | collective-permute-done | bytes 626720 | tf_op jit(solution)/shard_map/ppermute | solution.py:57
  39.9 15.0 %collective-permute-start.4 = (bf16[272,1152]{1,0:T(8,128)(2,1)}, bf16[272,1152]{1,0:T(8,128)(2,1)S(1)}, u32[]{:S(2)}, u32[]{:S(2)}) collective-permute-start(bf16[272,1152]{1,0:T(8,128)(2,1)} %collective-permute-done.3.image1_ref), channel_id=1, source_target_pairs={{4,0},{5,1},{6,2},{7,3},{8,4},{9,5},{10,6},{11,7},{12,8},{13,9},{1... | collective-permute-start | bytes 1880072 | tf_op jit(solution)/shard_map/ppermute | solution.py:57
  56.2 0.0 collective-permute-done.shard1_ref
  56.2 0.0 collective-permute-done.2.shard3_ref
  56.2 0.0 copy-done.2
  56.2 4.0 %shard_map.79 = (bf16[1152,1152]{1,0:T(8,128)(2,1)S(1)}, bf16[256,1152]{1,0:T(8,128)(2,1)S(1)}, f32[256,1152]{1,0:T(8,128)S(1)}) custom-call(s32[1]{0:T(128)} %bitcast.grp_ref, f32[1]{0:T(128)S(6)} %copy.13.scale_ref, f32[1]{0:T(128)S(6)} %copy.14.bias_ref, bf16[288,1152]{1,0:T(8,128)(2,1)S(1)} %copy-done.2, ...), custom_call_target="tpu_custom_call" | custom-call | flops 679477248 | bytes 8331276 | tf_op jit(solution)/shard_map/pallas_call | solution.py:81
  60.2 7.3 %collective-permute-done.5.text1_ref = bf16[272,1152]{1,0:T(8,128)(2,1)} collective-permute-done((bf16[272,1152]{1,0:T(8,128)(2,1)S(1)}, bf16[272,1152]{1,0:T(8,128)(2,1)}, u32[]{:S(2)}, u32[]{:S(2)}) %collective-permute-start.5) | collective-permute-done | bytes 626720 | tf_op jit(solution)/shard_map/ppermute | solution.py:57
  67.5 5.6 %shard_map.80 = (f32[1152,1152]{1,0:T(8,128)S(1)}, f32[256,1152]{1,0:T(8,128)S(1)}) custom-call(f32[1]{0:T(128)S(6)} %copy.13.scale_ref, f32[1]{0:T(128)S(6)} %copy.14.bias_ref, bf16[1152,1152]{1,0:T(8,128)(2,1)S(1)} %get-tuple-element.22.weight_ref, bf16[272,1152]{1,0:T(8,128)(2,1)S(1)} %shard_map.77.image_ref.image0_ref, ...), custom_call_target="tpu_custom_call" | custom-call | flops 2717908992 | bytes 13418504 | tf_op jit(solution)/shard_map/pallas_call | solution.py:81
  73.1 0.0 collective-permute-done.4.image_ref.image2_ref
  73.1 4.5 %shard_map.81 = (bf16[576,1152]{1,0:T(8,128)(2,1)S(1)}, bf16[1152,256]{1,0:T(8,128)(2,1)S(1)}, bf16[256,1152]{1,0:T(8,128)(2,1)S(1)}, bf16[256,1152]{1,0:T(8,128)(2,1)S(1)}, bf16[256,256]{1,0:T(8,128)(2,1)S(1)}) custom-call(s32[1]{0:T(128)} %bitcast.grp_ref, f32[1]{0:T(128)S(6)} %copy.13.scale_ref, f32[1]{0:T(128)S(6)} %copy.14.bias_ref, ...), custom_call_target="tpu_custom_call" | custom-call | flops 1358954496 | bytes 12443660 | tf_op jit(solution)/shard_map/pallas_call | solution.py:81
  77.7 2.5 %collective-permute-start.6 = (bf16[576,1152]{1,0:T(8,128)(2,1)S(1)}, bf16[576,1152]{1,0:T(8,128)(2,1)S(1)}, u32[]{:S(2)}, u32[]{:S(2)}) collective-permute-start(bf16[576,1152]{1,0:T(8,128)(2,1)S(1)} %get-tuple-element.31), channel_id=1, source_target_pairs={{1,0},{0,1},{3,2},{2,3},{5,4},{4,5},{7,6},{6,7},{9,8},{8,9},{11,10... | collective-permute-start | bytes 3981320 | tf_op jit(solution)/shard_map/ppermute | solution.py:61
  80.2 2.5 %shard_map.82 = (bf16[576,1152]{1,0:T(8,128)(2,1)S(1)}, bf16[256,1152]{1,0:T(8,128)(2,1)}) custom-call(s32[1]{0:T(128)} %bitcast.grp_ref, bf16[1152,256]{1,0:T(8,128)(2,1)S(1)} %get-tuple-element.26.turned_ref, bf16[256,1152]{1,0:T(8,128)(2,1)S(1)} %get-tuple-element.27.raw_grad_ref, bf16[256,1152]{1,0:T(8,128)(2,1)S(1)} %get-tuple-element.28.image_unit_ref.image_unit2_ref, ...), custom_call_target="tpu_custom_call" | custom-call | flops 679477248 | bytes 9125892 | tf_op jit(solution)/shard_map/pallas_call | solution.py:81
  82.6 0.2 collective-permute-done.6
  82.8 1.4 add_convert_fusion
  84.2 6.1 %all-to-all-start = ((bf16[8,72,1152]{2,1,0:T(8,128)(2,1)}), bf16[8,72,1152]{2,1,0:T(8,128)(2,1)}, u32[]{:S(2)}, u32[]{:S(2)}) async-start(bf16[8,72,1152]{2,1,0:T(8,128)(2,1)} %bitcast.24), calls=%async_computation | async-start | bytes 2654208 | tf_op jit(solution)/shard_map/all_to_all | solution.py:65
  90.3 0.0 all-gather.7.cloned.1.call-start
  90.3 0.7 all-gather.7.cloned.1.call-update
  91.0 10.0 %all-to-all-done = bf16[8,72,1152]{2,1,0:T(8,128)(2,1)} async-done(((bf16[8,72,1152]{2,1,0:T(8,128)(2,1)}), bf16[8,72,1152]{2,1,0:T(8,128)(2,1)}, u32[]{:S(2)}, u32[]{:S(2)}) %all-to-all-start) | async-done | bytes 1327136 | tf_op jit(solution)/shard_map/all_to_all | solution.py:65
  101.0 1.5 reduce_sum.24
  102.6 0.1 reshape.39
  102.7 14.4 %all_to_all.20 = bf16[16,48,128]{2,1,0:T(8,128)(2,1)S(1)} all-to-all(bf16[16,48,128]{2,1,0:T(8,128)(2,1)S(1)} %bitcast.28), channel_id=1, replica_groups={{0,8,16,24,128,136,144,152,256,264,272,280,384,392,400,408},{1,9,17,25,..., dimensions={0} | all-to-all | bytes 393216 | tf_op jit(solution)/shard_map/all_to_all | solution.py:65
  117.2 3.1 %collective-permute-start.7 = (bf16[48,128]{1,0:T(8,128)(2,1)S(1)}, bf16[48,128]{1,0:T(8,128)(2,1)S(1)}, u32[]{:S(2)}, u32[]{:S(2)}) collective-permute-start(bf16[48,128]{1,0:T(8,128)(2,1)S(1)} %reduce_sum.25), channel_id=1, source_target_pairs={{32,0},{33,1},{34,2},{35,3},{36,4},{37,5},{38,6},{39,7},{40,8},{41... | collective-permute-start | bytes 36872 | tf_op jit(solution)/shard_map/ppermute | solution.py:61
  120.3 6.8 %collective-permute-done.7 = bf16[48,128]{1,0:T(8,128)(2,1)S(1)} collective-permute-done((bf16[48,128]{1,0:T(8,128)(2,1)S(1)}, bf16[48,128]{1,0:T(8,128)(2,1)S(1)}, u32[]{:S(2)}, u32[]{:S(2)}) %collective-permute-start.7) | collective-permute-done | bytes 12320 | tf_op jit(solution)/shard_map/ppermute | solution.py:61
  127.1 0.7 broadcast_in_dim.4
  127.8 3.5 %all-to-all-start.2 = ((bf16[16,48,128]{2,1,0:T(8,128)(2,1)}), bf16[16,48,128]{2,1,0:T(8,128)(2,1)S(1)}, u32[]{:S(2)}, u32[]{:S(2)}) async-start(bf16[16,48,128]{2,1,0:T(8,128)(2,1)} %broadcast_in_dim.4), calls=%async_computation.2 | async-start | bytes 393216 | tf_op jit(solution)/shard_map/all_to_all | solution.py:65
  131.4 0.0 all-gather.5.cloned.1.call-start
  131.4 0.7 all-gather.5.cloned.1.call-update
  132.1 11.2 %all-to-all-done.2 = bf16[16,48,128]{2,1,0:T(8,128)(2,1)S(1)} async-done(((bf16[16,48,128]{2,1,0:T(8,128)(2,1)}), bf16[16,48,128]{2,1,0:T(8,128)(2,1)S(1)}, u32[]{:S(2)}, u32[]{:S(2)}) %all-to-all-start.2) | async-done | bytes 196640 | tf_op jit(solution)/shard_map/all_to_all | solution.py:65
  143.3 1.0 broadcast_in_dim.5
  144.3 6.9 %all-to-all-start.3 = ((bf16[4,704,128]{2,1,0:T(8,128)(2,1)}), bf16[4,704,128]{2,1,0:T(8,128)(2,1)}, u32[]{:S(2)}, u32[]{:S(2)}) async-start(bf16[4,704,128]{2,1,0:T(8,128)(2,1)} %broadcast_in_dim.5), calls=%async_computation.3 | async-start | bytes 1441792 | tf_op jit(solution)/shard_map/all_to_all | solution.py:65
  151.1 0.0 all-gather.7.cloned.1.call-done
  151.1 18.9 %all-gather.5.cloned.1.call-done = bf16[512,1152]{1,0:T(8,128)(2,1)} async-done(((bf16[256,1152]{1,0:T(8,128)(2,1)}), bf16[512,1152]{1,0:T(8,128)(2,1)}) %all-gather.5.cloned.1.call-update) | async-done | bytes 1179664 | tf_op jit(solution)/shard_map/all_gather | solution.py:298
  170.1 0.0 copy-start
  170.1 1.3 copy-done
  171.3 0.0 copy-start.1
  171.3 1.3 copy-done.1
  172.6 2.1 %shard_map.83 = f32[256,1152]{1,0:T(8,128)} custom-call(s32[1]{0:T(128)} %bitcast.9.odd_ref, f32[1]{0:T(128)S(6)} %copy.13.scale_ref, f32[1]{0:T(128)S(6)} %copy.14.bias_ref, bf16[256,1152]{1,0:T(8,128)(2,1)S(1)} %get-tuple-element.28.image_unit_ref.image_unit2_ref, bf16[272,1152]{1,0:T(8,128)(2,1)S(1)} %collective-permute-done.4.image_ref.image2_ref, ...), custom_call_target="tpu_custom_call" | custom-call | flops 679477248 | bytes 6561804 | tf_op jit(solution)/shard_map/pallas_call | solution.py:81
  174.7 0.0 all-to-all-done.3
  174.7 1.1 slice.9
  175.9 0.1 convert_bitcast_fusion
  176.0 0.4 copy.9
  176.3 1.6 copy.12
  (6 shorter events, 0.2 us)
Async XLA Ops:
  7.2 49.1 %copy-start.2 = (bf16[288,1152]{1,0:T(8,128)(2,1)S(1)}, bf16[288,1152]{1,0:T(8,128)(2,1)}, u32[]{:S(2)}) copy-start(bf16[288,1152]{1,0:T(8,128)(2,1)} %shard0_ref.1) | copy-start | bytes 1990660
  7.2 26.8 %collective-permute-start.1 = (bf16[288,1152]{1,0:T(8,128)(2,1)}, bf16[288,1152]{1,0:T(8,128)(2,1)S(1)}, u32[]{:S(2)}, u32[]{:S(2)}) collective-permute-start(bf16[288,1152]{1,0:T(8,128)(2,1)} %shard0_ref.1), channel_id=1, source_target_pairs={{2,0},{35,1},{0,2},{33,3},{6,4},{39,5},{4,6},{37,7},{10,8},{43,9},... | collective-permute-start | bytes 1990664 | tf_op jit(solution)/shard_map/ppermute | solution.py:61
  12.5 1.1 copy-start.3
  13.6 0.7 copy-start.5
  14.3 25.6 %collective-permute-start.3 = (bf16[272,1152]{1,0:T(8,128)(2,1)S(1)}, bf16[272,1152]{1,0:T(8,128)(2,1)}, u32[]{:S(2)}, u32[]{:S(2)}) collective-permute-start(bf16[272,1152]{1,0:T(8,128)(2,1)S(1)} %shard_map.77.image_ref.image0_ref), channel_id=1, source_target_pairs={{4,0},{5,1},{6,2},{7,3},{8,4},{9,5},{10,6},{11,7},{12,8},{13,9},{1... | collective-permute-start | bytes 1880072 | tf_op jit(solution)/shard_map/ppermute | solution.py:57
  28.1 28.1 %collective-permute-start = (bf16[288,1152]{1,0:T(8,128)(2,1)}, bf16[288,1152]{1,0:T(8,128)(2,1)}, u32[]{:S(2)}, u32[]{:S(2)}) collective-permute-start(bf16[288,1152]{1,0:T(8,128)(2,1)} %shard0_ref.1), channel_id=1, source_target_pairs={{1,0},{0,1},{3,2},{2,3},{5,4},{4,5},{7,6},{6,7},{9,8},{8,9},{11,10... | collective-permute-start | bytes 1990664 | tf_op jit(solution)/shard_map/ppermute | solution.py:61
  32.0 1.1 copy-start.4
  33.0 0.7 copy-start.6
  34.0 22.3 %collective-permute-start.2 = (bf16[288,1152]{1,0:T(8,128)(2,1)S(1)}, bf16[288,1152]{1,0:T(8,128)(2,1)}, u32[]{:S(2)}, u32[]{:S(2)}) collective-permute-start(bf16[288,1152]{1,0:T(8,128)(2,1)S(1)} %collective-permute-done.1.shard2_ref), channel_id=1, source_target_pairs={{1,0},{0,1},{3,2},{2,3},{5,4},{4,5},{7,6},{6,7},{9,8},{8,9},{11,10... | collective-permute-start | bytes 1990664 | tf_op jit(solution)/shard_map/ppermute | solution.py:61
  35.9 31.7 %collective-permute-start.5 = (bf16[272,1152]{1,0:T(8,128)(2,1)S(1)}, bf16[272,1152]{1,0:T(8,128)(2,1)}, u32[]{:S(2)}, u32[]{:S(2)}) collective-permute-start(bf16[272,1152]{1,0:T(8,128)(2,1)S(1)} %shard_map.78.text_ref), channel_id=1, source_target_pairs={{508,0},{509,1},{510,2},{511,3},{0,4},{1,5},{2,6},{3,7},{4,8},{5,9... | collective-permute-start | bytes 1880072 | tf_op jit(solution)/shard_map/ppermute | solution.py:57
  39.9 33.2 %collective-permute-start.4 = (bf16[272,1152]{1,0:T(8,128)(2,1)}, bf16[272,1152]{1,0:T(8,128)(2,1)S(1)}, u32[]{:S(2)}, u32[]{:S(2)}) collective-permute-start(bf16[272,1152]{1,0:T(8,128)(2,1)} %collective-permute-done.3.image1_ref), channel_id=1, source_target_pairs={{4,0},{5,1},{6,2},{7,3},{8,4},{9,5},{10,6},{11,7},{12,8},{13,9},{1... | collective-permute-start | bytes 1880072 | tf_op jit(solution)/shard_map/ppermute | solution.py:57
  77.7 5.2 %collective-permute-start.6 = (bf16[576,1152]{1,0:T(8,128)(2,1)S(1)}, bf16[576,1152]{1,0:T(8,128)(2,1)S(1)}, u32[]{:S(2)}, u32[]{:S(2)}) collective-permute-start(bf16[576,1152]{1,0:T(8,128)(2,1)S(1)} %get-tuple-element.31), channel_id=1, source_target_pairs={{1,0},{0,1},{3,2},{2,3},{5,4},{4,5},{7,6},{6,7},{9,8},{8,9},{11,10... | collective-permute-start | bytes 3981320 | tf_op jit(solution)/shard_map/ppermute | solution.py:61
  84.2 16.8 %all-to-all-start = ((bf16[8,72,1152]{2,1,0:T(8,128)(2,1)}), bf16[8,72,1152]{2,1,0:T(8,128)(2,1)}, u32[]{:S(2)}, u32[]{:S(2)}) async-start(bf16[8,72,1152]{2,1,0:T(8,128)(2,1)} %bitcast.24), calls=%async_computation | async-start | bytes 2654208 | tf_op jit(solution)/shard_map/all_to_all | solution.py:65
  90.3 60.9 %all-gather.7.cloned.1.call-start = ((), (), s32[]{:S(2)}) async-start(), calls=%async_computation.5 | async-start | bytes 1769472 | tf_op jit(solution)/shard_map/all_gather | solution.py:299
  117.2 9.9 %collective-permute-start.7 = (bf16[48,128]{1,0:T(8,128)(2,1)S(1)}, bf16[48,128]{1,0:T(8,128)(2,1)S(1)}, u32[]{:S(2)}, u32[]{:S(2)}) collective-permute-start(bf16[48,128]{1,0:T(8,128)(2,1)S(1)} %reduce_sum.25), channel_id=1, source_target_pairs={{32,0},{33,1},{34,2},{35,3},{36,4},{37,5},{38,6},{39,7},{40,8},{41... | collective-permute-start | bytes 36872 | tf_op jit(solution)/shard_map/ppermute | solution.py:61
  127.8 15.5 %all-to-all-start.2 = ((bf16[16,48,128]{2,1,0:T(8,128)(2,1)}), bf16[16,48,128]{2,1,0:T(8,128)(2,1)S(1)}, u32[]{:S(2)}, u32[]{:S(2)}) async-start(bf16[16,48,128]{2,1,0:T(8,128)(2,1)} %broadcast_in_dim.4), calls=%async_computation.2 | async-start | bytes 393216 | tf_op jit(solution)/shard_map/all_to_all | solution.py:65
  131.4 38.7 %all-gather.5.cloned.1.call-start = ((), (), s32[]{:S(2)}) async-start(), calls=%async_computation.4 | async-start | bytes 1769472 | tf_op jit(solution)/shard_map/all_gather | solution.py:298
  144.3 30.5 %all-to-all-start.3 = ((bf16[4,704,128]{2,1,0:T(8,128)(2,1)}), bf16[4,704,128]{2,1,0:T(8,128)(2,1)}, u32[]{:S(2)}, u32[]{:S(2)}) async-start(bf16[4,704,128]{2,1,0:T(8,128)(2,1)} %broadcast_in_dim.5), calls=%async_computation.3 | async-start | bytes 1441792 | tf_op jit(solution)/shard_map/all_to_all | solution.py:65
  170.1 1.3 copy-start
  171.3 1.3 copy-start.1
Sparse Core Ops, SparseCore 0:
  93.8 33.0 all-gather.6
  134.9 35.1 all-gather.4

commit v6 on v5

--- a/solution.py
+++ b/solution.py
@@ -47,9 +47,6 @@
 FIRST = grouped(lambda z, x, y, xl, core: (z // 2, x // 2, y // 2, core), lambda z, x, y, xl, core: (xl, z % 2, y % 2))
 NEAR = grouped(lambda z, x, y, xl, core: (z // 2, x, y // 2, core), lambda z, x, y, xl, core: (z % 2, y % 2))
 FAR = grouped(lambda z, x, y, xl, core: (z % 2, x, y % 2, core), lambda z, x, y, xl, core: (z // 2, y // 2))
-EVEN, ODD = (
-    [[blk * 4 + grp, (blk + 1) * 4 % N + grp] for blk in range(first, 128, 2) for grp in range(4)] for first in range(2)
-)
 CORES = [(i ^ 1, i) for i in range(N)]
 
 
@@ -102,16 +99,20 @@
     out_ref[ROWS:, ROWS:] = jnp.zeros((16, D - ROWS), BF)
 
 
-def pack_kernel(feats_ref, ids_ref, out_ref):
-    out_ref[:ROWS, :] = feats_ref[...]
+def prepare_kernel(feats_ref, text_ref, ids_ref, image_ref, out_ref, rows_ref, sems):
+    loads = [
+        pltpu.make_async_copy(text_ref, rows_ref, sems.at[0]),
+        pltpu.make_async_copy(feats_ref, image_ref.at[pl.ds(0, ROWS), :], sems.at[1]),
+    ]
+    for load in loads:
+        load.start()
+    put_ids(ids_ref, image_ref)
     put_ids(ids_ref, out_ref)
-
-
-def text_kernel(text_ref, ids_ref, out_ref):
-    rows = text_ref[...].astype(F32)
+    loads[0].wait()
+    rows = rows_ref[...].astype(F32)
     inverse = 1.0 / jnp.sqrt(jnp.sum(rows * rows, -1, keepdims=True) + 1e-06)
     out_ref[:ROWS, :] = (rows * inverse).astype(BF)
-    put_ids(ids_ref, out_ref)
+    loads[1].wait()
 
 
 def project(image_ref, weight_ref):
@@ -241,11 +242,10 @@
     back_ref[...] = across(far_ref[...], image_unit_ref[...]).astype(BF)
 
 
-def finish_kernel(odd_ref, scale_ref, bias_ref, image_unit2_ref, image2_ref, text_ref, grad_ref, even_back_ref, odd_back_ref, out_ref):
+def finish_kernel(scale_ref, bias_ref, image_unit2_ref, image2_ref, text_ref, grad_ref, back_ref, out_ref):
     image_unit2 = image_unit2_ref[...]
-    back = jnp.where(odd_ref[0] == 1, odd_back_ref[1], even_back_ref[1]).astype(F32)
     near2 = pair(image_unit2, ids_down(image2_ref), text_ref, scale_ref[0], bias_ref[0])
-    out_ref[...] = scale_ref[0] * (grad_ref[...] + across(near2, image_unit2) + back)
+    out_ref[...] = scale_ref[0] * (grad_ref[...] + across(near2, image_unit2) + back_ref[...].astype(F32))
 
 
 def shape(rows, columns, dtype):
@@ -258,20 +258,25 @@
     numbers = (logit_scale, logit_bias)
     flops = 2 * ROWS * D * D
     anywhere = pl.BlockSpec(memory_space=pl.ANY)
+    hbm = pl.BlockSpec(memory_space=pltpu.HBM)
     scratch = [pltpu.VMEM((2 * SHARD, D), F32), pltpu.SemaphoreType.DMA((2,))]
     ids = row_ids.reshape(1, ROWS)
-    image0 = call(pack_kernel, [packed], [VMEM] * 2, ROWS)(feats, ids)[0]
-    image0, text_embed = lax.optimization_barrier((image0, text_embed))
-    text0 = call(text_kernel, [packed], [VMEM] * 2, ROWS)(text_embed, ids)[0]
+    image0, text0 = call(
+        prepare_kernel,
+        [packed] * 2,
+        [hbm] * 2 + [VMEM],
+        ROWS,
+        [pltpu.VMEM((ROWS, D), BF), pltpu.SemaphoreType.DMA((2,))],
+    )(feats, text_embed, ids)
+    proj_weight, image0, text0 = lax.optimization_barrier((proj_weight, image0, text0))
+    image1 = shift(image0, -1)
+    text1 = shift(text0, 1)
+    shard2 = move(proj_weight, swap_x((1, 3)))
     shard1 = move(proj_weight, CORES)
-    shard2 = move(proj_weight, swap_x((1, 3)))
-    image1 = shift(image0, -1)
-    shard2, text0 = lax.optimization_barrier((shard2, text0))
-    shard3 = move(shard2, CORES)
-    text1 = shift(text0, 1)
+    shard3 = move(lax.optimization_barrier((shard2, text1, image1))[0], CORES)
     image2 = shift(image1, -1)
     weight, raw_grad0, grad = call(
-        own_kernel, [shape(D, D, BF), shape(ROWS, D, BF), shape(ROWS, D, F32)], [SMEM] * 3 + [anywhere] * 4 + [VMEM] * 2, flops,
+        own_kernel, [shape(D, D, BF), shape(ROWS, D, BF), shape(ROWS, D, F32)], [SMEM] * 3 + [hbm] * 4 + [VMEM] * 2, flops,
         [pltpu.SemaphoreType.DMA((4,))],
     )(grp, *numbers, proj_weight, shard1, shard2, shard3, image0, text0)
     part, grad = call(
@@ -295,19 +300,20 @@
         flops,
         scratch,
     )(grp, turned, raw_grad2, image_unit2, far, part)
-    even = lax.all_gather(term, AXIS, axis_index_groups=EVEN)
-    odd = lax.all_gather(term, AXIS, axis_index_groups=ODD)
     halves = (keep.astype(F32) + move(send, CORES).astype(F32)).astype(BF)
     mine = total(exchange(halves.reshape(8, SUB, D), FIRST))
     tiles = mine.reshape(SUB, 9, 128).transpose(1, 0, 2).reshape(SUB * 9, 128)
     tiles = jnp.pad(tiles, ((0, 768 - SUB * 9), (0, 0))).reshape(16, 48, 128)
     done = total(exchange(tiles, FAR))
     done = (done.astype(F32) + move(done, swap_x((2, 2))).astype(F32)).astype(BF)
+    done, term = lax.optimization_barrier((done, term))
+    term = shift(term, -1)
     done = spread(done, FAR).reshape(768, 128)[:704]
+    done, term = lax.optimization_barrier((done, term))
     done = spread(done, NEAR)[:, : SUB * 9]
     weight_grad = done.reshape(4, 9, SUB, 128).transpose(0, 2, 1, 3).reshape(SHARD, D).astype(F32)
-    text_grad = call(finish_kernel, [shape(ROWS, D, F32)], [SMEM] * 3 + [VMEM] * 6, flops)(
-        (lax.axis_index("blk") % 2).astype(jnp.int32).reshape(1), *numbers, image_unit2, image2, text0, grad, even, odd
+    text_grad = call(finish_kernel, [shape(ROWS, D, F32)], [SMEM] * 2 + [VMEM] * 5, flops)(
+        *numbers, image_unit2, image2, text0, grad, term
     )[0]
     return (weight_grad, text_grad)
 

time: 186 us -> 163 us (0.88)
  blocking collectives: 14.4 us -> 48.8 us
  waiting for transfers between devices: 58 us -> 26.8 us
  between operations: 15.6 us -> 2.21 us
  starting transfers between devices: 63.8 us -> 52 us
    all_to_all x1 -> x3, blocking collectives: 14.4 us -> 48.8 us  [exchange(): lax.all_to_all(chunks, AXIS, 0, 0, axis_index_groups=groups, tiled=True)]
    all_to_all x3 -> x1, waiting for transfers between devices: 21.2 us -> 2.24 us  [exchange(): lax.all_to_all(chunks, AXIS, 0, 0, axis_index_groups=groups, tiled=True)]
    all_gather x2 -> x0, waiting for transfers between devices: 18.9 us -> none  [the longest x1 18.9 us: on_device(): even = lax.all_gather(term, AXIS, axis_index_groups=EVEN)]
    ppermute x3 -> x4, waiting for transfers between devices: 9.4 us -> 19.5 us  [shift(): lax.ppermute(block, AXIS, [((i - 4 * distance) % N, i) for i in range(N)])]
    all_to_all x3 -> x1, starting transfers between devices: 16.5 us -> 9.31 us  [exchange(): lax.all_to_all(chunks, AXIS, 0, 0, axis_index_groups=groups, tiled=True)]
    ppermute x3 -> x4, starting transfers between devices: 30.7 us -> 24.3 us  [shift(): lax.ppermute(block, AXIS, [((i - 4 * distance) % N, i) for i in range(N)])]
    ppermute x5, waiting for transfers between devices: 7.03 us -> 5.01 us  [move(): return lax.ppermute(block, AXIS, moves)]
    pallas_call x7 -> x6, Pallas kernels: 19 us -> 17.2 us  [run(): pl.pallas_call(kernel, out_shape=outs, in_specs=specs, out_specs=[VMEM] *...]
  transfers between devices with their start and end apart: 13 -> 10, of which waited for: 7 -> 6; matrix products, arithmetic and copies ran while one was open for 2% -> 0% of each run, Pallas kernels for 8% -> 8%
where the time goes in v6:
time: 163 us; the launch traced here: 161 us
  starting transfers between devices  52 us (32%)
  blocking collectives  48.8 us (30%)
  waiting for transfers between devices  26.8 us (16%)
  Pallas kernels  17.2 us (11%)
  local copies, waits for them, and re-layouts  11.8 us (7%)
  between operations  2.21 us (1%)
  other arithmetic  2.01 us (1%)
    all_to_all x3, blocking collectives, exchange(): lax.all_to_all(chunks, AXIS, 0, 0, axis_index_groups=groups, tiled=True)  48.8 us
    ppermute x4, starting transfers between devices, shift(): lax.ppermute(block, AXIS, [((i - 4 * distance) % N, i) for i in range(N)])  24.3 us
    ppermute x4, waiting for transfers between devices, shift(): lax.ppermute(block, AXIS, [((i - 4 * distance) % N, i) for i in range(N)])  19.5 us
    ppermute x5, starting transfers between devices, move(): return lax.ppermute(block, AXIS, moves)  18.4 us
    pallas_call x6, Pallas kernels, run(): pl.pallas_call(kernel, out_shape=outs, in_specs=specs, out_specs=[VMEM] *...  17.2 us
    all_to_all x1, starting transfers between devices, exchange(): lax.all_to_all(chunks, AXIS, 0, 0, axis_index_groups=groups, tiled=True)  9.31 us
    unnamed x23, local copies, waits for them, and re-layouts  9.11 us
    ppermute x5, waiting for transfers between devices, move(): return lax.ppermute(block, AXIS, moves)  5.01 us
  transfers between devices with their start and end apart: 10, of which 6 were waited for; matrix products, arithmetic and copies ran while one was open for 0% of the time, Pallas kernels for 8%

profile of v6, /device:TPU:1, one launch (start us, length us, event | category | flops | bytes accessed | tf_op | source)
XLA Modules:
  0.0 160.7 jit_solution(18277714448799340106)
XLA Ops:
  0.6 0.0 copy-start
  0.6 0.0 copy-start.5
  0.7 1.1 copy-done.5
  1.8 0.0 copy-start.6
  1.8 1.1 copy-done.6
  2.8 0.0 copy-start.9
  2.8 0.7 copy-done.9
  3.5 0.5 shard_map.77
  4.0 5.2 %collective-permute-start.1 = (bf16[288,1152]{1,0:T(8,128)(2,1)}, bf16[288,1152]{1,0:T(8,128)(2,1)S(1)}, u32[]{:S(2)}, u32[]{:S(2)}) collective-permute-start(bf16[288,1152]{1,0:T(8,128)(2,1)} %shard0_ref), channel_id=1, source_target_pairs={{2,0},{35,1},{0,2},{33,3},{6,4},{39,5},{4,6},{37,7},{10,8},{43,9},... | collective-permute-start | bytes 1990664 | tf_op jit(solution)/shard_map/ppermute | solution.py:58
  9.2 13.8 %collective-permute-start.3 = (bf16[272,1152]{1,0:T(8,128)(2,1)S(1)}, bf16[272,1152]{1,0:T(8,128)(2,1)}, u32[]{:S(2)}, u32[]{:S(2)}) collective-permute-start(bf16[272,1152]{1,0:T(8,128)(2,1)S(1)} %get-tuple-element.28.image_ref.image0_ref), channel_id=1, source_target_pairs={{4,0},{5,1},{6,2},{7,3},{8,4},{9,5},{10,6},{11,7},{12,8},{13,9},{1... | collective-permute-start | bytes 1880072 | tf_op jit(solution)/shard_map/ppermute | solution.py:54
  23.1 0.0 copy-start.1
  23.1 0.8 copy-done.1
  23.9 1.9 %collective-permute-start.2 = (bf16[272,1152]{1,0:T(8,128)(2,1)S(1)}, bf16[272,1152]{1,0:T(8,128)(2,1)S(1)}, u32[]{:S(2)}, u32[]{:S(2)}) collective-permute-start(bf16[272,1152]{1,0:T(8,128)(2,1)S(1)} %get-tuple-element.27.text_ref), channel_id=1, source_target_pairs={{508,0},{509,1},{510,2},{511,3},{0,4},{1,5},{2,6},{3,7},{4,8},{5,9... | collective-permute-start | bytes 1880072 | tf_op jit(solution)/shard_map/ppermute | solution.py:54
  25.8 3.8 %collective-permute-start = (bf16[288,1152]{1,0:T(8,128)(2,1)}, bf16[288,1152]{1,0:T(8,128)(2,1)S(1)}, u32[]{:S(2)}, u32[]{:S(2)}) collective-permute-start(bf16[288,1152]{1,0:T(8,128)(2,1)} %shard0_ref), channel_id=1, source_target_pairs={{1,0},{0,1},{3,2},{2,3},{5,4},{4,5},{7,6},{6,7},{9,8},{8,9},{11,10... | collective-permute-start | bytes 1990664 | tf_op jit(solution)/shard_map/ppermute | solution.py:58
  29.6 5.2 %collective-permute-done.3.image1_ref = bf16[272,1152]{1,0:T(8,128)(2,1)} collective-permute-done((bf16[272,1152]{1,0:T(8,128)(2,1)S(1)}, bf16[272,1152]{1,0:T(8,128)(2,1)}, u32[]{:S(2)}, u32[]{:S(2)}) %collective-permute-start.3) | collective-permute-done | bytes 626720 | tf_op jit(solution)/shard_map/ppermute | solution.py:54
  34.8 10.4 %collective-permute-done.2.text1_ref = bf16[272,1152]{1,0:T(8,128)(2,1)S(1)} collective-permute-done((bf16[272,1152]{1,0:T(8,128)(2,1)S(1)}, bf16[272,1152]{1,0:T(8,128)(2,1)S(1)}, u32[]{:S(2)}, u32[]{:S(2)}) %collective-permute-start.2) | collective-permute-done | bytes 626720 | tf_op jit(solution)/shard_map/ppermute | solution.py:54
  45.2 0.0 copy-start.3
  45.2 0.8 copy-done.3
  46.0 0.0 collective-permute-done.1.shard2_ref
  46.0 4.7 %collective-permute-start.4 = (bf16[288,1152]{1,0:T(8,128)(2,1)S(1)}, bf16[288,1152]{1,0:T(8,128)(2,1)}, u32[]{:S(2)}, u32[]{:S(2)}) collective-permute-start(bf16[288,1152]{1,0:T(8,128)(2,1)S(1)} %collective-permute-done.1.shard2_ref), channel_id=1, source_target_pairs={{1,0},{0,1},{3,2},{2,3},{5,4},{4,5},{7,6},{6,7},{9,8},{8,9},{11,10... | collective-permute-start | bytes 1990664 | tf_op jit(solution)/shard_map/ppermute | solution.py:58
  50.8 1.9 %collective-permute-start.5 = (bf16[272,1152]{1,0:T(8,128)(2,1)}, bf16[272,1152]{1,0:T(8,128)(2,1)S(1)}, u32[]{:S(2)}, u32[]{:S(2)}) collective-permute-start(bf16[272,1152]{1,0:T(8,128)(2,1)} %collective-permute-done.3.image1_ref), channel_id=1, source_target_pairs={{4,0},{5,1},{6,2},{7,3},{8,4},{9,5},{10,6},{11,7},{12,8},{13,9},{1... | collective-permute-start | bytes 1880072 | tf_op jit(solution)/shard_map/ppermute | solution.py:54
  54.0 0.0 collective-permute-done.shard1_ref
  54.0 0.0 collective-permute-done.4.shard3_ref
  54.0 0.0 copy-done
  54.0 0.0 copy-start.2
  54.0 1.1 copy-done.2
  55.1 0.0 copy-start.4
  55.1 4.2 %shard_map.78 = (bf16[1152,1152]{1,0:T(8,128)(2,1)S(1)}, bf16[256,1152]{1,0:T(8,128)(2,1)S(1)}, f32[256,1152]{1,0:T(8,128)S(1)}) custom-call(s32[1]{0:T(128)} %bitcast.grp_ref, f32[1]{0:T(128)S(6)} %copy.13.scale_ref, f32[1]{0:T(128)S(6)} %copy.14.bias_ref, bf16[288,1152]{1,0:T(8,128)(2,1)S(1)} %copy-done, ...), custom_call_target="tpu_custom_call" | custom-call | flops 679477248 | bytes 8331276 | tf_op jit(solution)/shard_map/pallas_call | solution.py:78
  59.3 0.0 copy-done.4
  59.3 5.4 %shard_map.79 = (f32[1152,1152]{1,0:T(8,128)S(1)}, f32[256,1152]{1,0:T(8,128)S(1)}) custom-call(f32[1]{0:T(128)S(6)} %copy.13.scale_ref, f32[1]{0:T(128)S(6)} %copy.14.bias_ref, bf16[1152,1152]{1,0:T(8,128)(2,1)S(1)} %get-tuple-element.30.weight_ref, bf16[272,1152]{1,0:T(8,128)(2,1)S(1)} %copy-done.2, bf16[256,1152]{1,0:T(8,128)(2,1)S(1)} %get-tuple-element.31.raw_grad0_ref, ...), custom_call_target="tpu_custom_call" | custom-call | flops 2717908992 | bytes 13418504 | tf_op jit(solution)/shard_map/pallas_call | solution.py:78
  64.7 3.9 %collective-permute-done.5.image_ref.image2_ref = bf16[272,1152]{1,0:T(8,128)(2,1)S(1)} collective-permute-done((bf16[272,1152]{1,0:T(8,128)(2,1)}, bf16[272,1152]{1,0:T(8,128)(2,1)S(1)}, u32[]{:S(2)}, u32[]{:S(2)}) %collective-permute-start.5) | collective-permute-done | bytes 626720 | tf_op jit(solution)/shard_map/ppermute | solution.py:54
  68.6 3.5 %shard_map.80 = (bf16[576,1152]{1,0:T(8,128)(2,1)S(1)}, bf16[1152,256]{1,0:T(8,128)(2,1)S(1)}, bf16[256,1152]{1,0:T(8,128)(2,1)S(1)}, bf16[256,1152]{1,0:T(8,128)(2,1)S(1)}, bf16[256,256]{1,0:T(8,128)(2,1)S(1)}) custom-call(s32[1]{0:T(128)} %bitcast.grp_ref, f32[1]{0:T(128)S(6)} %copy.13.scale_ref, f32[1]{0:T(128)S(6)} %copy.14.bias_ref, ...), custom_call_target="tpu_custom_call" | custom-call | flops 1358954496 | bytes 12443660 | tf_op jit(solution)/shard_map/pallas_call | solution.py:78
  72.1 2.7 %collective-permute-start.6 = (bf16[576,1152]{1,0:T(8,128)(2,1)S(1)}, bf16[576,1152]{1,0:T(8,128)(2,1)S(1)}, u32[]{:S(2)}, u32[]{:S(2)}) collective-permute-start(bf16[576,1152]{1,0:T(8,128)(2,1)S(1)} %get-tuple-element.39), channel_id=1, source_target_pairs={{1,0},{0,1},{3,2},{2,3},{5,4},{4,5},{7,6},{6,7},{9,8},{8,9},{11,10... | collective-permute-start | bytes 3981320 | tf_op jit(solution)/shard_map/ppermute | solution.py:58
  74.8 1.7 %shard_map.81 = (bf16[576,1152]{1,0:T(8,128)(2,1)S(1)}, bf16[256,1152]{1,0:T(8,128)(2,1)S(1)}) custom-call(s32[1]{0:T(128)} %bitcast.grp_ref, bf16[1152,256]{1,0:T(8,128)(2,1)S(1)} %get-tuple-element.34.turned_ref, bf16[256,1152]{1,0:T(8,128)(2,1)S(1)} %get-tuple-element.35.raw_grad_ref, ...), custom_call_target="tpu_custom_call" | custom-call | flops 679477248 | bytes 9125892 | tf_op jit(solution)/shard_map/pallas_call | solution.py:78
  76.5 0.0 copy-start.10
  76.5 1.0 collective-permute-done.6
  77.5 0.4 add_convert_fusion
  77.8 0.0 copy-done.10
  77.8 17.5 %all_to_all.20 = bf16[8,72,1152]{2,1,0:T(8,128)(2,1)} all-to-all(bf16[8,72,1152]{2,1,0:T(8,128)(2,1)S(1)} %bitcast.18), channel_id=1, replica_groups={{0,4,64,68,2,6,66,70},{477,449,29,1,511,483,63,35},{509,481,61,33,479,4..., dimensions={0} | all-to-all | bytes 2654208 | tf_op jit(solution)/shard_map/all_to_all | solution.py:62
  95.4 1.5 reduce_sum.24
  96.9 0.1 reshape.36
  97.1 15.3 %all_to_all.21 = bf16[16,48,128]{2,1,0:T(8,128)(2,1)S(1)} all-to-all(bf16[16,48,128]{2,1,0:T(8,128)(2,1)S(1)} %bitcast.22), channel_id=1, replica_groups={{0,8,16,24,128,136,144,152,256,264,272,280,384,392,400,408},{1,9,17,25,..., dimensions={0} | all-to-all | bytes 393216 | tf_op jit(solution)/shard_map/all_to_all | solution.py:62
  112.4 1.9 %collective-permute-start.7 = (bf16[48,128]{1,0:T(8,128)(2,1)S(1)}, bf16[48,128]{1,0:T(8,128)(2,1)S(1)}, u32[]{:S(2)}, u32[]{:S(2)}) collective-permute-start(bf16[48,128]{1,0:T(8,128)(2,1)S(1)} %reduce_sum.25), channel_id=1, source_target_pairs={{32,0},{33,1},{34,2},{35,3},{36,4},{37,5},{38,6},{39,7},{40,8},{41... | collective-permute-start | bytes 36872 | tf_op jit(solution)/shard_map/ppermute | solution.py:58
  114.3 4.0 %collective-permute-done.7 = bf16[48,128]{1,0:T(8,128)(2,1)S(1)} collective-permute-done((bf16[48,128]{1,0:T(8,128)(2,1)S(1)}, bf16[48,128]{1,0:T(8,128)(2,1)S(1)}, u32[]{:S(2)}, u32[]{:S(2)}) %collective-permute-start.7) | collective-permute-done | bytes 12320 | tf_op jit(solution)/shard_map/ppermute | solution.py:58
  118.4 6.6 %collective-permute-start.8 = (bf16[256,1152]{1,0:T(8,128)(2,1)}, bf16[256,1152]{1,0:T(8,128)(2,1)S(1)}, u32[]{:S(2)}, u32[]{:S(2)}) collective-permute-start(bf16[256,1152]{1,0:T(8,128)(2,1)} %copy-done.10), channel_id=1, source_target_pairs={{4,0},{5,1},{6,2},{7,3},{8,4},{9,5},{10,6},{11,7},{12,8},{13,9},{1... | collective-permute-start | bytes 1769480 | tf_op jit(solution)/shard_map/ppermute | solution.py:54
  125.0 15.9 %all_to_all.22 = bf16[16,48,128]{2,1,0:T(8,128)(2,1)S(1)} all-to-all(bf16[16,48,128]{2,1,0:T(8,128)(2,1)S(1)} %broadcast_in_dim.4), channel_id=1, replica_groups={{0,8,16,24,128,136,144,152,256,264,272,280,384,392,400,408},{1,9,17,25,..., dimensions={0} | all-to-all | bytes 393216 | tf_op jit(solution)/shard_map/all_to_all | solution.py:62
  141.0 0.0 collective-permute-done.8.back_ref
  141.0 0.0 copy-start.7
  141.0 0.8 copy-done.7
  141.8 1.0 broadcast_in_dim.5
  142.8 9.3 %all-to-all-start.3 = ((bf16[4,704,128]{2,1,0:T(8,128)(2,1)}), bf16[4,704,128]{2,1,0:T(8,128)(2,1)}, u32[]{:S(2)}, u32[]{:S(2)}) async-start(bf16[4,704,128]{2,1,0:T(8,128)(2,1)} %broadcast_in_dim.5), calls=%async_computation.3 | async-start | bytes 1441792 | tf_op jit(solution)/shard_map/all_to_all | solution.py:62
  152.1 0.0 copy-start.8
  152.1 1.1 copy-done.8
  153.1 2.1 %shard_map.82 = f32[256,1152]{1,0:T(8,128)} custom-call(f32[1]{0:T(128)S(6)} %copy.13.scale_ref, f32[1]{0:T(128)S(6)} %copy.14.bias_ref, bf16[256,1152]{1,0:T(8,128)(2,1)S(1)} %get-tuple-element.36.image_unit_ref.image_unit2_ref, bf16[272,1152]{1,0:T(8,128)(2,1)S(1)} %collective-permute-done.5.image_ref.image2_ref, ...), custom_call_target="tpu_custom_call" | custom-call | flops 679477248 | bytes 4792328 | tf_op jit(solution)/shard_map/pallas_call | solution.py:78
  155.2 2.2 %all-to-all-done.3 = bf16[4,704,128]{2,1,0:T(8,128)(2,1)} async-done(((bf16[4,704,128]{2,1,0:T(8,128)(2,1)}), bf16[4,704,128]{2,1,0:T(8,128)(2,1)}, u32[]{:S(2)}, u32[]{:S(2)}) %all-to-all-start.3) | async-done | bytes 720928 | tf_op jit(solution)/shard_map/all_to_all | solution.py:62
  157.5 1.1 slice.9
  158.6 0.1 convert_bitcast_fusion
  158.7 0.4 copy.9
  159.1 1.6 %copy.12 = f32[36,8,9,128]{3,1,2,0:T(8,128)} copy(f32[36,8,9,128]{3,2,1,0:T(8,128)S(1)} %bitcast.17) | data formatting | bytes 2654208
  (6 shorter events, 0.1 us)
Async XLA Ops:
  0.6 53.4 %copy-start = (bf16[288,1152]{1,0:T(8,128)(2,1)S(1)}, bf16[288,1152]{1,0:T(8,128)(2,1)}, u32[]{:S(2)}) copy-start(bf16[288,1152]{1,0:T(8,128)(2,1)} %shard0_ref) | copy-start | bytes 1990660
  0.6 1.1 copy-start.5
  1.8 1.1 copy-start.6
  2.8 0.7 copy-start.9
  4.0 42.0 %collective-permute-start.1 = (bf16[288,1152]{1,0:T(8,128)(2,1)}, bf16[288,1152]{1,0:T(8,128)(2,1)S(1)}, u32[]{:S(2)}, u32[]{:S(2)}) collective-permute-start(bf16[288,1152]{1,0:T(8,128)(2,1)} %shard0_ref), channel_id=1, source_target_pairs={{2,0},{35,1},{0,2},{33,3},{6,4},{39,5},{4,6},{37,7},{10,8},{43,9},... | collective-permute-start | bytes 1990664 | tf_op jit(solution)/shard_map/ppermute | solution.py:58
  9.2 25.6 %collective-permute-start.3 = (bf16[272,1152]{1,0:T(8,128)(2,1)S(1)}, bf16[272,1152]{1,0:T(8,128)(2,1)}, u32[]{:S(2)}, u32[]{:S(2)}) collective-permute-start(bf16[272,1152]{1,0:T(8,128)(2,1)S(1)} %get-tuple-element.28.image_ref.image0_ref), channel_id=1, source_target_pairs={{4,0},{5,1},{6,2},{7,3},{8,4},{9,5},{10,6},{11,7},{12,8},{13,9},{1... | collective-permute-start | bytes 1880072 | tf_op jit(solution)/shard_map/ppermute | solution.py:54
  23.1 0.8 copy-start.1
  23.9 21.3 %collective-permute-start.2 = (bf16[272,1152]{1,0:T(8,128)(2,1)S(1)}, bf16[272,1152]{1,0:T(8,128)(2,1)S(1)}, u32[]{:S(2)}, u32[]{:S(2)}) collective-permute-start(bf16[272,1152]{1,0:T(8,128)(2,1)S(1)} %get-tuple-element.27.text_ref), channel_id=1, source_target_pairs={{508,0},{509,1},{510,2},{511,3},{0,4},{1,5},{2,6},{3,7},{4,8},{5,9... | collective-permute-start | bytes 1880072 | tf_op jit(solution)/shard_map/ppermute | solution.py:54
  25.8 28.2 %collective-permute-start = (bf16[288,1152]{1,0:T(8,128)(2,1)}, bf16[288,1152]{1,0:T(8,128)(2,1)S(1)}, u32[]{:S(2)}, u32[]{:S(2)}) collective-permute-start(bf16[288,1152]{1,0:T(8,128)(2,1)} %shard0_ref), channel_id=1, source_target_pairs={{1,0},{0,1},{3,2},{2,3},{5,4},{4,5},{7,6},{6,7},{9,8},{8,9},{11,10... | collective-permute-start | bytes 1990664 | tf_op jit(solution)/shard_map/ppermute | solution.py:58
  45.2 0.8 copy-start.3
  46.0 8.0 %collective-permute-start.4 = (bf16[288,1152]{1,0:T(8,128)(2,1)S(1)}, bf16[288,1152]{1,0:T(8,128)(2,1)}, u32[]{:S(2)}, u32[]{:S(2)}) collective-permute-start(bf16[288,1152]{1,0:T(8,128)(2,1)S(1)} %collective-permute-done.1.shard2_ref), channel_id=1, source_target_pairs={{1,0},{0,1},{3,2},{2,3},{5,4},{4,5},{7,6},{6,7},{9,8},{8,9},{11,10... | collective-permute-start | bytes 1990664 | tf_op jit(solution)/shard_map/ppermute | solution.py:58
  50.8 17.8 %collective-permute-start.5 = (bf16[272,1152]{1,0:T(8,128)(2,1)}, bf16[272,1152]{1,0:T(8,128)(2,1)S(1)}, u32[]{:S(2)}, u32[]{:S(2)}) collective-permute-start(bf16[272,1152]{1,0:T(8,128)(2,1)} %collective-permute-done.3.image1_ref), channel_id=1, source_target_pairs={{4,0},{5,1},{6,2},{7,3},{8,4},{9,5},{10,6},{11,7},{12,8},{13,9},{1... | collective-permute-start | bytes 1880072 | tf_op jit(solution)/shard_map/ppermute | solution.py:54
  54.0 1.1 copy-start.2
  55.1 4.2 %copy-start.4 = (bf16[272,1152]{1,0:T(8,128)(2,1)S(1)}, bf16[272,1152]{1,0:T(8,128)(2,1)}, u32[]{:S(2)}) copy-start(bf16[272,1152]{1,0:T(8,128)(2,1)} %copy-done.3) | copy-start | bytes 1880068
  72.1 5.4 %collective-permute-start.6 = (bf16[576,1152]{1,0:T(8,128)(2,1)S(1)}, bf16[576,1152]{1,0:T(8,128)(2,1)S(1)}, u32[]{:S(2)}, u32[]{:S(2)}) collective-permute-start(bf16[576,1152]{1,0:T(8,128)(2,1)S(1)} %get-tuple-element.39), channel_id=1, source_target_pairs={{1,0},{0,1},{3,2},{2,3},{5,4},{4,5},{7,6},{6,7},{9,8},{8,9},{11,10... | collective-permute-start | bytes 3981320 | tf_op jit(solution)/shard_map/ppermute | solution.py:58
  76.5 1.4 copy-start.10
  112.4 5.9 %collective-permute-start.7 = (bf16[48,128]{1,0:T(8,128)(2,1)S(1)}, bf16[48,128]{1,0:T(8,128)(2,1)S(1)}, u32[]{:S(2)}, u32[]{:S(2)}) collective-permute-start(bf16[48,128]{1,0:T(8,128)(2,1)S(1)} %reduce_sum.25), channel_id=1, source_target_pairs={{32,0},{33,1},{34,2},{35,3},{36,4},{37,5},{38,6},{39,7},{40,8},{41... | collective-permute-start | bytes 36872 | tf_op jit(solution)/shard_map/ppermute | solution.py:58
  118.4 22.6 %collective-permute-start.8 = (bf16[256,1152]{1,0:T(8,128)(2,1)}, bf16[256,1152]{1,0:T(8,128)(2,1)S(1)}, u32[]{:S(2)}, u32[]{:S(2)}) collective-permute-start(bf16[256,1152]{1,0:T(8,128)(2,1)} %copy-done.10), channel_id=1, source_target_pairs={{4,0},{5,1},{6,2},{7,3},{8,4},{9,5},{10,6},{11,7},{12,8},{13,9},{1... | collective-permute-start | bytes 1769480 | tf_op jit(solution)/shard_map/ppermute | solution.py:54
  141.0 0.8 copy-start.7
  142.8 14.7 %all-to-all-start.3 = ((bf16[4,704,128]{2,1,0:T(8,128)(2,1)}), bf16[4,704,128]{2,1,0:T(8,128)(2,1)}, u32[]{:S(2)}, u32[]{:S(2)}) async-start(bf16[4,704,128]{2,1,0:T(8,128)(2,1)} %broadcast_in_dim.5), calls=%async_computation.3 | async-start | bytes 1441792 | tf_op jit(solution)/shard_map/all_to_all | solution.py:62
  152.1 1.1 copy-start.8

commit v7 on v6

--- a/solution.py
+++ b/solution.py
@@ -12,6 +12,7 @@
 SHARD = D // 4
 SUB = SHARD // 4
 PACKED = ROWS + 16
+BAND = SUB + 8
 N = 512
 AXIS = ("blk", "grp")
 VMEM = pl.BlockSpec(memory_space=pltpu.VMEM)
@@ -248,6 +249,23 @@
     out_ref[...] = scale_ref[0] * (grad_ref[...] + across(near2, image_unit2) + back_ref[...].astype(F32))
 
 
+def pack_kernel(chunks_ref, out_ref):
+    rows = chunks_ref[0].astype(F32)
+    for chunk in range(1, 8):
+        rows = rows + chunks_ref[chunk].astype(F32)
+    for band in range(9):
+        tile = jnp.concatenate([rows[:, band * 128 : (band + 1) * 128], jnp.zeros((8, 128), F32)], 0)
+        out_ref[band * BAND : (band + 1) * BAND, :] = tile.astype(BF)
+    out_ref[9 * BAND :, :] = jnp.zeros((768 - 9 * BAND, 128), BF)
+
+
+def unpack_kernel(tiles_ref, out_ref):
+    for chunk in range(4):
+        for band in range(9):
+            tile = tiles_ref[chunk, band * BAND : (band + 1) * BAND, :].astype(F32)
+            out_ref[chunk * SUB : (chunk + 1) * SUB, band * 128 : (band + 1) * 128] = tile[:SUB]
+
+
 def shape(rows, columns, dtype):
     return jax.ShapeDtypeStruct((rows, columns), dtype)
 
@@ -268,12 +286,11 @@
         ROWS,
         [pltpu.VMEM((ROWS, D), BF), pltpu.SemaphoreType.DMA((2,))],
     )(feats, text_embed, ids)
-    proj_weight, image0, text0 = lax.optimization_barrier((proj_weight, image0, text0))
     image1 = shift(image0, -1)
     text1 = shift(text0, 1)
     shard2 = move(proj_weight, swap_x((1, 3)))
     shard1 = move(proj_weight, CORES)
-    shard3 = move(lax.optimization_barrier((shard2, text1, image1))[0], CORES)
+    shard3 = move(lax.optimization_barrier((shard2, text1))[0], CORES)
     image2 = shift(image1, -1)
     weight, raw_grad0, grad = call(
         own_kernel, [shape(D, D, BF), shape(ROWS, D, BF), shape(ROWS, D, F32)], [SMEM] * 3 + [hbm] * 4 + [VMEM] * 2, flops,
@@ -301,17 +318,17 @@
         scratch,
     )(grp, turned, raw_grad2, image_unit2, far, part)
     halves = (keep.astype(F32) + move(send, CORES).astype(F32)).astype(BF)
-    mine = total(exchange(halves.reshape(8, SUB, D), FIRST))
-    tiles = mine.reshape(SUB, 9, 128).transpose(1, 0, 2).reshape(SUB * 9, 128)
-    tiles = jnp.pad(tiles, ((0, 768 - SUB * 9), (0, 0))).reshape(16, 48, 128)
+    mine = exchange(halves.reshape(8, SUB, D), FIRST)
+    tiles = call(pack_kernel, [shape(768, 128, BF)], [VMEM], ROWS)(mine)[0]
+    tiles, term = lax.optimization_barrier((tiles, term))
+    tiles = tiles.reshape(16, 48, 128)
+    term = shift(term, -1)
     done = total(exchange(tiles, FAR))
     done = (done.astype(F32) + move(done, swap_x((2, 2))).astype(F32)).astype(BF)
+    done = spread(done, FAR).reshape(768, 128)[: 9 * BAND]
     done, term = lax.optimization_barrier((done, term))
-    term = shift(term, -1)
-    done = spread(done, FAR).reshape(768, 128)[:704]
-    done, term = lax.optimization_barrier((done, term))
-    done = spread(done, NEAR)[:, : SUB * 9]
-    weight_grad = done.reshape(4, 9, SUB, 128).transpose(0, 2, 1, 3).reshape(SHARD, D).astype(F32)
+    done = spread(done, NEAR)
+    weight_grad = call(unpack_kernel, [shape(SHARD, D, F32)], [VMEM], ROWS)(done)[0]
     text_grad = call(finish_kernel, [shape(ROWS, D, F32)], [SMEM] * 2 + [VMEM] * 5, flops)(
         *numbers, image_unit2, image2, text0, grad, term
     )[0]

time: 163 us -> 150 us (0.920); the launches traced: 161 us -> 149 us
  waiting for transfers between devices: 26.8 us -> 9.34 us
  starting transfers between devices: 52 us -> 58.9 us
  local copies, waits for them, and re-layouts: 11.8 us -> 7.81 us
  blocking collectives: 48.8 us -> 52.2 us
    ppermute x4, waiting for transfers between devices: 19.5 us -> 6.31 us  [shift(): lax.ppermute(block, AXIS, [((i - 4 * distance) % N, i) for i in range(N)])]
    ppermute x4, starting transfers between devices: 24.3 us -> 29.9 us  [shift(): lax.ppermute(block, AXIS, [((i - 4 * distance) % N, i) for i in range(N)])]
    ppermute x5, waiting for transfers between devices: 5.01 us -> 1.01 us  [move(): return lax.ppermute(block, AXIS, moves)]
    all_to_all x3, blocking collectives: 48.8 us -> 52.2 us  [exchange(): lax.all_to_all(chunks, AXIS, 0, 0, axis_index_groups=groups, tiled=True)]
    ppermute x5, starting transfers between devices: 18.4 us -> 21 us  [move(): return lax.ppermute(block, AXIS, moves)]
    unnamed x23 -> x20, local copies, waits for them, and re-layouts: 9.11 us -> 6.81 us
    pallas_call x6 -> x8, Pallas kernels: 17.2 us -> 18.5 us  [run(): pl.pallas_call(kernel, out_shape=outs, in_specs=specs, out_specs=[VMEM] *...]
  transfers between devices with their start and end apart: 10 -> 10, of which waited for: 6 -> 4; matrix products, arithmetic and copies ran while one was open for 0% -> 0% of each run, Pallas kernels for 8% -> 9%
where the time goes in v7:
time: 150 us; the launch traced here: 149 us
  starting transfers between devices  58.9 us (39%)
  blocking collectives  52.2 us (35%)
  Pallas kernels  18.5 us (12%)
  waiting for transfers between devices  9.34 us (6%)
  local copies, waits for them, and re-layouts  7.81 us (5%)
  between operations  2.18 us (1%)
    all_to_all x3, blocking collectives, exchange(): lax.all_to_all(chunks, AXIS, 0, 0, axis_index_groups=groups, tiled=True)  52.2 us
    ppermute x4, starting transfers between devices, shift(): lax.ppermute(block, AXIS, [((i - 4 * distance) % N, i) for i in range(N)])  29.9 us
    ppermute x5, starting transfers between devices, move(): return lax.ppermute(block, AXIS, moves)  21 us
    pallas_call x8, Pallas kernels, run(): pl.pallas_call(kernel, out_shape=outs, in_specs=specs, out_specs=[VMEM] *...  18.5 us
    all_to_all x1, starting transfers between devices, exchange(): lax.all_to_all(chunks, AXIS, 0, 0, axis_index_groups=groups, tiled=True)  7.96 us
    unnamed x20, local copies, waits for them, and re-layouts  6.81 us
    ppermute x4, waiting for transfers between devices, shift(): lax.ppermute(block, AXIS, [((i - 4 * distance) % N, i) for i in range(N)])  6.31 us
  transfers between devices with their start and end apart: 10, of which 4 were waited for; matrix products, arithmetic and copies ran while one was open for 0% of the time, Pallas kernels for 9%

profile of v7, /device:TPU:1, one launch (start us, length us, event | category | flops | bytes accessed | tf_op | source)
XLA Modules:
  0.0 149.4 jit_solution(15571194110904694865)
XLA Ops:
  0.6 0.0 copy-start.2
  0.6 5.3 %collective-permute-start.1 = (bf16[288,1152]{1,0:T(8,128)(2,1)}, bf16[288,1152]{1,0:T(8,128)(2,1)S(1)}, u32[]{:S(2)}, u32[]{:S(2)}) collective-permute-start(bf16[288,1152]{1,0:T(8,128)(2,1)} %shard0_ref.1), channel_id=1, source_target_pairs={{2,0},{35,1},{0,2},{33,3},{6,4},{39,5},{4,6},{37,7},{10,8},{43,9},... | collective-permute-start | bytes 1990664 | tf_op jit(solution)/shard_map/ppermute | solution.py:59
  6.0 0.0 copy-start.7
  6.0 1.1 copy-done.7
  7.1 0.0 copy-start.8
  7.1 1.1 copy-done.8
  8.1 0.0 copy-start.9
  8.1 0.7 copy-done.9
  8.8 0.5 shard_map.77
  9.3 3.2 %collective-permute-start.2 = (bf16[272,1152]{1,0:T(8,128)(2,1)S(1)}, bf16[272,1152]{1,0:T(8,128)(2,1)S(1)}, u32[]{:S(2)}, u32[]{:S(2)}) collective-permute-start(bf16[272,1152]{1,0:T(8,128)(2,1)S(1)} %get-tuple-element.21.text_ref), channel_id=1, source_target_pairs={{508,0},{509,1},{510,2},{511,3},{0,4},{1,5},{2,6},{3,7},{4,8},{5,9... | collective-permute-start | bytes 1880072 | tf_op jit(solution)/shard_map/ppermute | solution.py:55
  12.5 12.5 %collective-permute-start.4 = (bf16[272,1152]{1,0:T(8,128)(2,1)S(1)}, bf16[272,1152]{1,0:T(8,128)(2,1)}, u32[]{:S(2)}, u32[]{:S(2)}) collective-permute-start(bf16[272,1152]{1,0:T(8,128)(2,1)S(1)} %get-tuple-element.23.image_ref.image0_ref), channel_id=1, source_target_pairs={{4,0},{5,1},{6,2},{7,3},{8,4},{9,5},{10,6},{11,7},{12,8},{13,9},{1... | collective-permute-start | bytes 1880072 | tf_op jit(solution)/shard_map/ppermute | solution.py:55
  25.1 0.0 copy-start.3
  25.1 0.8 copy-done.3
  25.9 3.8 %collective-permute-start = (bf16[288,1152]{1,0:T(8,128)(2,1)}, bf16[288,1152]{1,0:T(8,128)(2,1)S(1)}, u32[]{:S(2)}, u32[]{:S(2)}) collective-permute-start(bf16[288,1152]{1,0:T(8,128)(2,1)} %shard0_ref.1), channel_id=1, source_target_pairs={{1,0},{0,1},{3,2},{2,3},{5,4},{4,5},{7,6},{6,7},{9,8},{8,9},{11,10... | collective-permute-start | bytes 1990664 | tf_op jit(solution)/shard_map/ppermute | solution.py:59
  29.7 6.2 %collective-permute-done.2.text1_ref = bf16[272,1152]{1,0:T(8,128)(2,1)S(1)} collective-permute-done((bf16[272,1152]{1,0:T(8,128)(2,1)S(1)}, bf16[272,1152]{1,0:T(8,128)(2,1)S(1)}, u32[]{:S(2)}, u32[]{:S(2)}) %collective-permute-start.2) | collective-permute-done | bytes 626720 | tf_op jit(solution)/shard_map/ppermute | solution.py:55
  35.9 0.0 copy-start.5
  35.9 0.8 copy-done.5
  36.8 0.0 collective-permute-done.1.shard2_ref
  36.8 4.2 %collective-permute-start.3 = (bf16[288,1152]{1,0:T(8,128)(2,1)S(1)}, bf16[288,1152]{1,0:T(8,128)(2,1)}, u32[]{:S(2)}, u32[]{:S(2)}) collective-permute-start(bf16[288,1152]{1,0:T(8,128)(2,1)S(1)} %collective-permute-done.1.shard2_ref), channel_id=1, source_target_pairs={{1,0},{0,1},{3,2},{2,3},{5,4},{4,5},{7,6},{6,7},{9,8},{8,9},{11,10... | collective-permute-start | bytes 1990664 | tf_op jit(solution)/shard_map/ppermute | solution.py:59
  40.9 0.0 collective-permute-done.4.image1_ref
  40.9 5.8 %collective-permute-start.5 = (bf16[272,1152]{1,0:T(8,128)(2,1)}, bf16[272,1152]{1,0:T(8,128)(2,1)S(1)}, u32[]{:S(2)}, u32[]{:S(2)}) collective-permute-start(bf16[272,1152]{1,0:T(8,128)(2,1)} %collective-permute-done.4.image1_ref), channel_id=1, source_target_pairs={{4,0},{5,1},{6,2},{7,3},{8,4},{9,5},{10,6},{11,7},{12,8},{13,9},{1... | collective-permute-start | bytes 1880072 | tf_op jit(solution)/shard_map/ppermute | solution.py:55
  48.1 0.0 collective-permute-done.shard1_ref
  48.1 0.0 collective-permute-done.3.shard3_ref
  48.1 0.0 copy-done.2
  48.1 0.0 copy-start.4
  48.1 1.1 copy-done.4
  49.2 0.0 copy-start.6
  49.2 4.1 %shard_map.78 = (bf16[1152,1152]{1,0:T(8,128)(2,1)S(1)}, bf16[256,1152]{1,0:T(8,128)(2,1)S(1)}, f32[256,1152]{1,0:T(8,128)S(1)}) custom-call(s32[1]{0:T(128)} %bitcast.grp_ref, f32[1]{0:T(128)S(6)} %copy.8.scale_ref, f32[1]{0:T(128)S(6)} %copy.9.bias_ref, bf16[288,1152]{1,0:T(8,128)(2,1)S(1)} %copy-done.2, ...), custom_call_target="tpu_custom_call" | custom-call | flops 679477248 | bytes 8331276 | tf_op jit(solution)/shard_map/pallas_call | solution.py:79
  53.3 0.0 copy-done.6
  53.3 5.3 %shard_map.79 = (f32[1152,1152]{1,0:T(8,128)S(1)}, f32[256,1152]{1,0:T(8,128)S(1)}) custom-call(f32[1]{0:T(128)S(6)} %copy.8.scale_ref, f32[1]{0:T(128)S(6)} %copy.9.bias_ref, bf16[1152,1152]{1,0:T(8,128)(2,1)S(1)} %get-tuple-element.24.weight_ref, bf16[272,1152]{1,0:T(8,128)(2,1)S(1)} %copy-done.4, bf16[256,1152]{1,0:T(8,128)(2,1)S(1)} %get-tuple-element.25.raw_grad0_ref, ...), custom_call_target="tpu_custom_call" | custom-call | flops 2717908992 | bytes 13418504 | tf_op jit(solution)/shard_map/pallas_call | solution.py:79
  58.7 0.0 copy-start
  58.7 0.1 collective-permute-done.5.image_ref.image2_ref
  58.8 3.5 %shard_map.80 = (bf16[576,1152]{1,0:T(8,128)(2,1)S(1)}, bf16[1152,256]{1,0:T(8,128)(2,1)S(1)}, bf16[256,1152]{1,0:T(8,128)(2,1)S(1)}, bf16[256,1152]{1,0:T(8,128)(2,1)S(1)}, bf16[256,256]{1,0:T(8,128)(2,1)S(1)}) custom-call(s32[1]{0:T(128)} %bitcast.grp_ref, f32[1]{0:T(128)S(6)} %copy.8.scale_ref, f32[1]{0:T(128)S(6)} %copy.9.bias_ref, ...), custom_call_target="tpu_custom_call" | custom-call | flops 1358954496 | bytes 12443660 | tf_op jit(solution)/shard_map/pallas_call | solution.py:79
  62.2 0.0 copy-done
  62.3 4.7 %collective-permute-start.6 = (bf16[576,1152]{1,0:T(8,128)(2,1)S(1)}, bf16[576,1152]{1,0:T(8,128)(2,1)S(1)}, u32[]{:S(2)}, u32[]{:S(2)}) collective-permute-start(bf16[576,1152]{1,0:T(8,128)(2,1)S(1)} %get-tuple-element.33), channel_id=1, source_target_pairs={{1,0},{0,1},{3,2},{2,3},{5,4},{4,5},{7,6},{6,7},{9,8},{8,9},{11,10... | collective-permute-start | bytes 3981320 | tf_op jit(solution)/shard_map/ppermute | solution.py:59
  67.0 1.7 %shard_map.81 = (bf16[576,1152]{1,0:T(8,128)(2,1)S(1)}, bf16[256,1152]{1,0:T(8,128)(2,1)S(1)}) custom-call(s32[1]{0:T(128)} %bitcast.grp_ref, bf16[1152,256]{1,0:T(8,128)(2,1)S(1)} %get-tuple-element.28.turned_ref, bf16[256,1152]{1,0:T(8,128)(2,1)S(1)} %get-tuple-element.29.raw_grad_ref, ...), custom_call_target="tpu_custom_call" | custom-call | flops 679477248 | bytes 9125892 | tf_op jit(solution)/shard_map/pallas_call | solution.py:79
  68.6 1.0 collective-permute-done.6
  69.6 0.4 add_convert_fusion
  70.0 19.7 %all_to_all.20.chunks_ref = bf16[8,72,1152]{2,1,0:T(8,128)(2,1)S(1)} all-to-all(bf16[8,72,1152]{2,1,0:T(8,128)(2,1)S(1)} %bitcast.7), channel_id=1, replica_groups={{0,4,64,68,2,6,66,70},{477,449,29,1,511,483,63,35},{509,481,61,33,479,4..., dimensions={0} | all-to-all | bytes 2654208 | tf_op jit(solution)/shard_map/all_to_all | solution.py:63
  89.6 0.2 shard_map.82
  89.8 17.6 %all_to_all.21 = bf16[16,48,128]{2,1,0:T(8,128)(2,1)S(1)} all-to-all(bf16[16,48,128]{2,1,0:T(8,128)(2,1)S(1)} %bitcast.5), channel_id=1, replica_groups={{0,8,16,24,128,136,144,152,256,264,272,280,384,392,400,408},{1,9,17,25,..., dimensions={0} | all-to-all | bytes 393216 | tf_op jit(solution)/shard_map/all_to_all | solution.py:63
  107.5 3.0 %collective-permute-start.7 = (bf16[48,128]{1,0:T(8,128)(2,1)S(1)}, bf16[48,128]{1,0:T(8,128)(2,1)S(1)}, u32[]{:S(2)}, u32[]{:S(2)}) collective-permute-start(bf16[48,128]{1,0:T(8,128)(2,1)S(1)} %reduce_sum.12), channel_id=1, source_target_pairs={{32,0},{33,1},{34,2},{35,3},{36,4},{37,5},{38,6},{39,7},{40,8},{41... | collective-permute-start | bytes 36872 | tf_op jit(solution)/shard_map/ppermute | solution.py:59
  110.5 8.4 %collective-permute-start.8 = (bf16[256,1152]{1,0:T(8,128)(2,1)S(1)}, bf16[256,1152]{1,0:T(8,128)(2,1)S(1)}, u32[]{:S(2)}, u32[]{:S(2)}) collective-permute-start(bf16[256,1152]{1,0:T(8,128)(2,1)S(1)} %get-tuple-element.36), channel_id=1, source_target_pairs={{4,0},{5,1},{6,2},{7,3},{8,4},{9,5},{10,6},{11,7},{12,8},{13,9},{1... | collective-permute-start | bytes 1769480 | tf_op jit(solution)/shard_map/ppermute | solution.py:55
  118.8 0.0 collective-permute-done.7
  118.9 15.0 %all_to_all.22 = bf16[16,48,128]{2,1,0:T(8,128)(2,1)S(1)} all-to-all(bf16[16,48,128]{2,1,0:T(8,128)(2,1)S(1)} %broadcast_in_dim.4), channel_id=1, replica_groups={{0,8,16,24,128,136,144,152,256,264,272,280,384,392,400,408},{1,9,17,25,..., dimensions={0} | all-to-all | bytes 393216 | tf_op jit(solution)/shard_map/all_to_all | solution.py:63
  133.9 0.0 collective-permute-done.8.back_ref
  133.9 1.0 broadcast_in_dim.5
  134.9 8.0 %all-to-all-start.3 = ((bf16[4,720,128]{2,1,0:T(8,128)(2,1)}), bf16[4,720,128]{2,1,0:T(8,128)(2,1)S(1)}, u32[]{:S(2)}, u32[]{:S(2)}) async-start(bf16[4,720,128]{2,1,0:T(8,128)(2,1)} %broadcast_in_dim.5), calls=%async_computation.3 | async-start | bytes 1474560 | tf_op jit(solution)/shard_map/all_to_all | solution.py:63
  142.8 0.0 copy-start.1
  142.8 1.3 copy-done.1
  144.1 2.1 %shard_map.84 = f32[256,1152]{1,0:T(8,128)} custom-call(f32[1]{0:T(128)S(6)} %copy.8.scale_ref, f32[1]{0:T(128)S(6)} %copy.9.bias_ref, bf16[256,1152]{1,0:T(8,128)(2,1)S(1)} %get-tuple-element.30.image_unit_ref.image_unit2_ref, bf16[272,1152]{1,0:T(8,128)(2,1)S(1)} %collective-permute-done.5.image_ref.image2_ref, ...), custom_call_target="tpu_custom_call" | custom-call | flops 679477248 | bytes 4792328 | tf_op jit(solution)/shard_map/pallas_call | solution.py:79
  146.2 2.0 %all-to-all-done.3.tiles_ref = bf16[4,720,128]{2,1,0:T(8,128)(2,1)S(1)} async-done(((bf16[4,720,128]{2,1,0:T(8,128)(2,1)}), bf16[4,720,128]{2,1,0:T(8,128)(2,1)S(1)}, u32[]{:S(2)}, u32[]{:S(2)}) %all-to-all-start.3) | async-done | bytes 737312 | tf_op jit(solution)/shard_map/all_to_all | solution.py:63
  148.2 1.1 shard_map.83
  (4 shorter events, 0.1 us)
Async XLA Ops:
  0.6 47.5 %copy-start.2 = (bf16[288,1152]{1,0:T(8,128)(2,1)S(1)}, bf16[288,1152]{1,0:T(8,128)(2,1)}, u32[]{:S(2)}) copy-start(bf16[288,1152]{1,0:T(8,128)(2,1)} %shard0_ref.1) | copy-start | bytes 1990660
  0.6 36.1 %collective-permute-start.1 = (bf16[288,1152]{1,0:T(8,128)(2,1)}, bf16[288,1152]{1,0:T(8,128)(2,1)S(1)}, u32[]{:S(2)}, u32[]{:S(2)}) collective-permute-start(bf16[288,1152]{1,0:T(8,128)(2,1)} %shard0_ref.1), channel_id=1, source_target_pairs={{2,0},{35,1},{0,2},{33,3},{6,4},{39,5},{4,6},{37,7},{10,8},{43,9},... | collective-permute-start | bytes 1990664 | tf_op jit(solution)/shard_map/ppermute | solution.py:59
  6.0 1.1 copy-start.7
  7.1 1.1 copy-start.8
  8.1 0.7 copy-start.9
  9.3 26.6 %collective-permute-start.2 = (bf16[272,1152]{1,0:T(8,128)(2,1)S(1)}, bf16[272,1152]{1,0:T(8,128)(2,1)S(1)}, u32[]{:S(2)}, u32[]{:S(2)}) collective-permute-start(bf16[272,1152]{1,0:T(8,128)(2,1)S(1)} %get-tuple-element.21.text_ref), channel_id=1, source_target_pairs={{508,0},{509,1},{510,2},{511,3},{0,4},{1,5},{2,6},{3,7},{4,8},{5,9... | collective-permute-start | bytes 1880072 | tf_op jit(solution)/shard_map/ppermute | solution.py:55
  12.5 28.4 %collective-permute-start.4 = (bf16[272,1152]{1,0:T(8,128)(2,1)S(1)}, bf16[272,1152]{1,0:T(8,128)(2,1)}, u32[]{:S(2)}, u32[]{:S(2)}) collective-permute-start(bf16[272,1152]{1,0:T(8,128)(2,1)S(1)} %get-tuple-element.23.image_ref.image0_ref), channel_id=1, source_target_pairs={{4,0},{5,1},{6,2},{7,3},{8,4},{9,5},{10,6},{11,7},{12,8},{13,9},{1... | collective-permute-start | bytes 1880072 | tf_op jit(solution)/shard_map/ppermute | solution.py:55
  25.1 0.8 copy-start.3
  25.9 22.2 %collective-permute-start = (bf16[288,1152]{1,0:T(8,128)(2,1)}, bf16[288,1152]{1,0:T(8,128)(2,1)S(1)}, u32[]{:S(2)}, u32[]{:S(2)}) collective-permute-start(bf16[288,1152]{1,0:T(8,128)(2,1)} %shard0_ref.1), channel_id=1, source_target_pairs={{1,0},{0,1},{3,2},{2,3},{5,4},{4,5},{7,6},{6,7},{9,8},{8,9},{11,10... | collective-permute-start | bytes 1990664 | tf_op jit(solution)/shard_map/ppermute | solution.py:59
  35.9 0.8 copy-start.5
  36.8 11.3 %collective-permute-start.3 = (bf16[288,1152]{1,0:T(8,128)(2,1)S(1)}, bf16[288,1152]{1,0:T(8,128)(2,1)}, u32[]{:S(2)}, u32[]{:S(2)}) collective-permute-start(bf16[288,1152]{1,0:T(8,128)(2,1)S(1)} %collective-permute-done.1.shard2_ref), channel_id=1, source_target_pairs={{1,0},{0,1},{3,2},{2,3},{5,4},{4,5},{7,6},{6,7},{9,8},{8,9},{11,10... | collective-permute-start | bytes 1990664 | tf_op jit(solution)/shard_map/ppermute | solution.py:59
  40.9 17.8 %collective-permute-start.5 = (bf16[272,1152]{1,0:T(8,128)(2,1)}, bf16[272,1152]{1,0:T(8,128)(2,1)S(1)}, u32[]{:S(2)}, u32[]{:S(2)}) collective-permute-start(bf16[272,1152]{1,0:T(8,128)(2,1)} %collective-permute-done.4.image1_ref), channel_id=1, source_target_pairs={{4,0},{5,1},{6,2},{7,3},{8,4},{9,5},{10,6},{11,7},{12,8},{13,9},{1... | collective-permute-start | bytes 1880072 | tf_op jit(solution)/shard_map/ppermute | solution.py:55
  48.1 1.1 copy-start.4
  49.2 4.2 %copy-start.6 = (bf16[272,1152]{1,0:T(8,128)(2,1)S(1)}, bf16[272,1152]{1,0:T(8,128)(2,1)}, u32[]{:S(2)}) copy-start(bf16[272,1152]{1,0:T(8,128)(2,1)} %copy-done.5) | copy-start | bytes 1880068
  58.7 3.6 %copy-start = (f32[256,1152]{1,0:T(8,128)}, f32[256,1152]{1,0:T(8,128)S(1)}, u32[]{:S(2)}) copy-start(f32[256,1152]{1,0:T(8,128)S(1)} %get-tuple-element.38.grad_ref) | copy-start | bytes 3538948
  62.3 7.4 %collective-permute-start.6 = (bf16[576,1152]{1,0:T(8,128)(2,1)S(1)}, bf16[576,1152]{1,0:T(8,128)(2,1)S(1)}, u32[]{:S(2)}, u32[]{:S(2)}) collective-permute-start(bf16[576,1152]{1,0:T(8,128)(2,1)S(1)} %get-tuple-element.33), channel_id=1, source_target_pairs={{1,0},{0,1},{3,2},{2,3},{5,4},{4,5},{7,6},{6,7},{9,8},{8,9},{11,10... | collective-permute-start | bytes 3981320 | tf_op jit(solution)/shard_map/ppermute | solution.py:59
  107.5 11.4 %collective-permute-start.7 = (bf16[48,128]{1,0:T(8,128)(2,1)S(1)}, bf16[48,128]{1,0:T(8,128)(2,1)S(1)}, u32[]{:S(2)}, u32[]{:S(2)}) collective-permute-start(bf16[48,128]{1,0:T(8,128)(2,1)S(1)} %reduce_sum.12), channel_id=1, source_target_pairs={{32,0},{33,1},{34,2},{35,3},{36,4},{37,5},{38,6},{39,7},{40,8},{41... | collective-permute-start | bytes 36872 | tf_op jit(solution)/shard_map/ppermute | solution.py:59
  110.5 23.4 %collective-permute-start.8 = (bf16[256,1152]{1,0:T(8,128)(2,1)S(1)}, bf16[256,1152]{1,0:T(8,128)(2,1)S(1)}, u32[]{:S(2)}, u32[]{:S(2)}) collective-permute-start(bf16[256,1152]{1,0:T(8,128)(2,1)S(1)} %get-tuple-element.36), channel_id=1, source_target_pairs={{4,0},{5,1},{6,2},{7,3},{8,4},{9,5},{10,6},{11,7},{12,8},{13,9},{1... | collective-permute-start | bytes 1769480 | tf_op jit(solution)/shard_map/ppermute | solution.py:55
  134.9 13.3 %all-to-all-start.3 = ((bf16[4,720,128]{2,1,0:T(8,128)(2,1)}), bf16[4,720,128]{2,1,0:T(8,128)(2,1)S(1)}, u32[]{:S(2)}, u32[]{:S(2)}) async-start(bf16[4,720,128]{2,1,0:T(8,128)(2,1)} %broadcast_in_dim.5), calls=%async_computation.3 | async-start | bytes 1474560 | tf_op jit(solution)/shard_map/all_to_all | solution.py:63
  142.8 1.3 copy-start.1

commit v8 on v7

--- a/solution.py
+++ b/solution.py
@@ -320,13 +320,12 @@
     halves = (keep.astype(F32) + move(send, CORES).astype(F32)).astype(BF)
     mine = exchange(halves.reshape(8, SUB, D), FIRST)
     tiles = call(pack_kernel, [shape(768, 128, BF)], [VMEM], ROWS)(mine)[0]
-    tiles, term = lax.optimization_barrier((tiles, term))
     tiles = tiles.reshape(16, 48, 128)
     term = shift(term, -1)
     done = total(exchange(tiles, FAR))
+    done, term = lax.optimization_barrier((done, term))
     done = (done.astype(F32) + move(done, swap_x((2, 2))).astype(F32)).astype(BF)
     done = spread(done, FAR).reshape(768, 128)[: 9 * BAND]
-    done, term = lax.optimization_barrier((done, term))
     done = spread(done, NEAR)
     weight_grad = call(unpack_kernel, [shape(SHARD, D, F32)], [VMEM], ROWS)(done)[0]
     text_grad = call(finish_kernel, [shape(ROWS, D, F32)], [SMEM] * 2 + [VMEM] * 5, flops)(

time: 150 us -> 154 us (1.027)
  the two profiles are of different devices: /device:TPU:1 before, /device:TPU:4 now
where the time goes in v8:
time: 154 us; the launch traced here: 153 us
  blocking collectives  54.2 us (35%)
  starting transfers between devices  44.9 us (29%)
  waiting for transfers between devices  22.8 us (15%)
  Pallas kernels  19.6 us (13%)
  local copies, waits for them, and re-layouts  7.81 us (5%)
  between operations  2.17 us (1%)
    all_to_all x2, blocking collectives, exchange(): lax.all_to_all(chunks, AXIS, 0, 0, axis_index_groups=groups, tiled=True)  54.2 us
    ppermute x4, starting transfers between devices, shift(): lax.ppermute(block, AXIS, [((i - 4 * distance) % N, i) for i in range(N)])  24.6 us
    pallas_call x8, Pallas kernels, run(): pl.pallas_call(kernel, out_shape=outs, in_specs=specs, out_specs=[VMEM] *...  19.6 us
    ppermute x5, starting transfers between devices, move(): return lax.ppermute(block, AXIS, moves)  10.9 us
    all_to_all x2, starting transfers between devices, exchange(): lax.all_to_all(chunks, AXIS, 0, 0, axis_index_groups=groups, tiled=True)  9.37 us
    ppermute x4, waiting for transfers between devices, shift(): lax.ppermute(block, AXIS, [((i - 4 * distance) % N, i) for i in range(N)])  8.81 us
    all_to_all x2, waiting for transfers between devices, exchange(): lax.all_to_all(chunks, AXIS, 0, 0, axis_index_groups=groups, tiled=True)  7.45 us
    unnamed x22, local copies, waits for them, and re-layouts  6.81 us
  transfers between devices with their start and end apart: 11, of which 6 were waited for; matrix products, arithmetic and copies ran while one was open for 0% of the time, Pallas kernels for 10%

profile of v8, /device:TPU:4, one launch (start us, length us, event | category | flops | bytes accessed | tf_op | source)
XLA Modules:
  0.0 153.0 jit_solution(166586043907133860)
XLA Ops:
  0.6 0.0 copy-start.2
  0.6 3.2 %collective-permute-start.1 = (bf16[288,1152]{1,0:T(8,128)(2,1)}, bf16[288,1152]{1,0:T(8,128)(2,1)S(1)}, u32[]{:S(2)}, u32[]{:S(2)}) collective-permute-start(bf16[288,1152]{1,0:T(8,128)(2,1)} %shard0_ref.1), channel_id=1, source_target_pairs={{2,0},{35,1},{0,2},{33,3},{6,4},{39,5},{4,6},{37,7},{10,8},{43,9},... | collective-permute-start | bytes 1990664 | tf_op jit(solution)/shard_map/ppermute | solution.py:59
  3.9 0.0 copy-start.7
  3.9 1.1 copy-done.7
  5.0 0.0 copy-start.8
  5.0 1.1 copy-done.8
  6.0 0.0 copy-start.9
  6.0 0.7 copy-done.9
  6.7 0.5 shard_map.77
  7.2 3.5 %collective-permute-start.2 = (bf16[272,1152]{1,0:T(8,128)(2,1)S(1)}, bf16[272,1152]{1,0:T(8,128)(2,1)S(1)}, u32[]{:S(2)}, u32[]{:S(2)}) collective-permute-start(bf16[272,1152]{1,0:T(8,128)(2,1)S(1)} %get-tuple-element.19.text_ref), channel_id=1, source_target_pairs={{508,0},{509,1},{510,2},{511,3},{0,4},{1,5},{2,6},{3,7},{4,8},{5,9... | collective-permute-start | bytes 1880072 | tf_op jit(solution)/shard_map/ppermute | solution.py:55
  10.7 6.0 %collective-permute-start.4 = (bf16[272,1152]{1,0:T(8,128)(2,1)S(1)}, bf16[272,1152]{1,0:T(8,128)(2,1)}, u32[]{:S(2)}, u32[]{:S(2)}) collective-permute-start(bf16[272,1152]{1,0:T(8,128)(2,1)S(1)} %get-tuple-element.21.image_ref.image0_ref), channel_id=1, source_target_pairs={{4,0},{5,1},{6,2},{7,3},{8,4},{9,5},{10,6},{11,7},{12,8},{13,9},{1... | collective-permute-start | bytes 1880072 | tf_op jit(solution)/shard_map/ppermute | solution.py:55
  16.7 0.0 copy-start.3
  16.7 0.8 copy-done.3
  17.5 1.9 %collective-permute-start = (bf16[288,1152]{1,0:T(8,128)(2,1)}, bf16[288,1152]{1,0:T(8,128)(2,1)S(1)}, u32[]{:S(2)}, u32[]{:S(2)}) collective-permute-start(bf16[288,1152]{1,0:T(8,128)(2,1)} %shard0_ref.1), channel_id=1, source_target_pairs={{1,0},{0,1},{3,2},{2,3},{5,4},{4,5},{7,6},{6,7},{9,8},{8,9},{11,10... | collective-permute-start | bytes 1990664 | tf_op jit(solution)/shard_map/ppermute | solution.py:59
  19.4 8.6 %collective-permute-done.2.text1_ref = bf16[272,1152]{1,0:T(8,128)(2,1)S(1)} collective-permute-done((bf16[272,1152]{1,0:T(8,128)(2,1)S(1)}, bf16[272,1152]{1,0:T(8,128)(2,1)S(1)}, u32[]{:S(2)}, u32[]{:S(2)}) %collective-permute-start.2) | collective-permute-done | bytes 626720 | tf_op jit(solution)/shard_map/ppermute | solution.py:55
  28.0 0.0 copy-start.5
  28.0 0.8 copy-done.5
  28.8 0.0 collective-permute-done.1.shard2_ref
  28.8 1.9 %collective-permute-start.3 = (bf16[288,1152]{1,0:T(8,128)(2,1)S(1)}, bf16[288,1152]{1,0:T(8,128)(2,1)}, u32[]{:S(2)}, u32[]{:S(2)}) collective-permute-start(bf16[288,1152]{1,0:T(8,128)(2,1)S(1)} %collective-permute-done.1.shard2_ref), channel_id=1, source_target_pairs={{1,0},{0,1},{3,2},{2,3},{5,4},{4,5},{7,6},{6,7},{9,8},{8,9},{11,10... | collective-permute-start | bytes 1990664 | tf_op jit(solution)/shard_map/ppermute | solution.py:59
  30.8 0.0 collective-permute-done.4.image1_ref
  30.8 6.4 %collective-permute-start.5 = (bf16[272,1152]{1,0:T(8,128)(2,1)}, bf16[272,1152]{1,0:T(8,128)(2,1)S(1)}, u32[]{:S(2)}, u32[]{:S(2)}) collective-permute-start(bf16[272,1152]{1,0:T(8,128)(2,1)} %collective-permute-done.4.image1_ref), channel_id=1, source_target_pairs={{4,0},{5,1},{6,2},{7,3},{8,4},{9,5},{10,6},{11,7},{12,8},{13,9},{1... | collective-permute-start | bytes 1880072 | tf_op jit(solution)/shard_map/ppermute | solution.py:55
  38.5 0.0 collective-permute-done.shard1_ref
  38.5 0.0 collective-permute-done.3.shard3_ref
  38.5 0.0 copy-done.2
  38.5 0.0 copy-start.4
  38.5 1.1 copy-done.4
  39.6 0.0 copy-start.6
  39.6 4.1 %shard_map.78 = (bf16[1152,1152]{1,0:T(8,128)(2,1)S(1)}, bf16[256,1152]{1,0:T(8,128)(2,1)S(1)}, f32[256,1152]{1,0:T(8,128)S(1)}) custom-call(s32[1]{0:T(128)} %bitcast.grp_ref, f32[1]{0:T(128)S(6)} %copy.8.scale_ref, f32[1]{0:T(128)S(6)} %copy.9.bias_ref, bf16[288,1152]{1,0:T(8,128)(2,1)S(1)} %copy-done.2, ...), custom_call_target="tpu_custom_call" | custom-call | flops 679477248 | bytes 8331276 | tf_op jit(solution)/shard_map/pallas_call | solution.py:79
  43.8 0.0 copy-done.6
  43.8 5.4 %shard_map.79 = (f32[1152,1152]{1,0:T(8,128)S(1)}, f32[256,1152]{1,0:T(8,128)S(1)}) custom-call(f32[1]{0:T(128)S(6)} %copy.8.scale_ref, f32[1]{0:T(128)S(6)} %copy.9.bias_ref, bf16[1152,1152]{1,0:T(8,128)(2,1)S(1)} %get-tuple-element.22.weight_ref, bf16[272,1152]{1,0:T(8,128)(2,1)S(1)} %copy-done.4, bf16[256,1152]{1,0:T(8,128)(2,1)S(1)} %get-tuple-element.23.raw_grad0_ref, ...), custom_call_target="tpu_custom_call" | custom-call | flops 2717908992 | bytes 13418504 | tf_op jit(solution)/shard_map/pallas_call | solution.py:79
  49.2 0.0 copy-start
  49.2 0.2 collective-permute-done.5.image_ref.image2_ref
  49.4 3.5 %shard_map.80 = (bf16[576,1152]{1,0:T(8,128)(2,1)S(1)}, bf16[1152,256]{1,0:T(8,128)(2,1)S(1)}, bf16[256,1152]{1,0:T(8,128)(2,1)S(1)}, bf16[256,1152]{1,0:T(8,128)(2,1)S(1)}, bf16[256,256]{1,0:T(8,128)(2,1)S(1)}) custom-call(s32[1]{0:T(128)} %bitcast.grp_ref, f32[1]{0:T(128)S(6)} %copy.8.scale_ref, f32[1]{0:T(128)S(6)} %copy.9.bias_ref, ...), custom_call_target="tpu_custom_call" | custom-call | flops 1358954496 | bytes 12443660 | tf_op jit(solution)/shard_map/pallas_call | solution.py:79
  52.9 0.0 copy-done
  52.9 1.9 %collective-permute-start.6 = (bf16[576,1152]{1,0:T(8,128)(2,1)S(1)}, bf16[576,1152]{1,0:T(8,128)(2,1)S(1)}, u32[]{:S(2)}, u32[]{:S(2)}) collective-permute-start(bf16[576,1152]{1,0:T(8,128)(2,1)S(1)} %get-tuple-element.31), channel_id=1, source_target_pairs={{1,0},{0,1},{3,2},{2,3},{5,4},{4,5},{7,6},{6,7},{9,8},{8,9},{11,10... | collective-permute-start | bytes 3981320 | tf_op jit(solution)/shard_map/ppermute | solution.py:59
  54.8 1.7 %shard_map.81 = (bf16[576,1152]{1,0:T(8,128)(2,1)S(1)}, bf16[256,1152]{1,0:T(8,128)(2,1)S(1)}) custom-call(s32[1]{0:T(128)} %bitcast.grp_ref, bf16[1152,256]{1,0:T(8,128)(2,1)S(1)} %get-tuple-element.26.turned_ref, bf16[256,1152]{1,0:T(8,128)(2,1)S(1)} %get-tuple-element.27.raw_grad_ref, ...), custom_call_target="tpu_custom_call" | custom-call | flops 679477248 | bytes 9125892 | tf_op jit(solution)/shard_map/pallas_call | solution.py:79
  56.5 0.0 copy-start.10
  56.5 1.4 collective-permute-done.6
  57.8 1.4 add_convert_fusion
  59.3 0.0 copy-done.10
  59.3 3.8 %all-to-all-start = ((bf16[8,72,1152]{2,1,0:T(8,128)(2,1)}), bf16[8,72,1152]{2,1,0:T(8,128)(2,1)S(1)}, u32[]{:S(2)}, u32[]{:S(2)}) async-start(bf16[8,72,1152]{2,1,0:T(8,128)(2,1)} %bitcast.7), calls=%async_computation | async-start | bytes 2654208 | tf_op jit(solution)/shard_map/all_to_all | solution.py:63
  63.1 8.8 %collective-permute-start.7 = (bf16[256,1152]{1,0:T(8,128)(2,1)}, bf16[256,1152]{1,0:T(8,128)(2,1)}, u32[]{:S(2)}, u32[]{:S(2)}) collective-permute-start(bf16[256,1152]{1,0:T(8,128)(2,1)} %copy-done.10), channel_id=1, source_target_pairs={{4,0},{5,1},{6,2},{7,3},{8,4},{9,5},{10,6},{11,7},{12,8},{13,9},{1... | collective-permute-start | bytes 1769480 | tf_op jit(solution)/shard_map/ppermute | solution.py:55
  71.9 3.9 %all-to-all-done.chunks_ref = bf16[8,72,1152]{2,1,0:T(8,128)(2,1)S(1)} async-done(((bf16[8,72,1152]{2,1,0:T(8,128)(2,1)}), bf16[8,72,1152]{2,1,0:T(8,128)(2,1)S(1)}, u32[]{:S(2)}, u32[]{:S(2)}) %all-to-all-start) | async-done | bytes 1327136 | tf_op jit(solution)/shard_map/all_to_all | solution.py:63
  75.8 0.2 shard_map.82
  76.0 38.5 %all_to_all.20 = bf16[16,48,128]{2,1,0:T(8,128)(2,1)S(1)} all-to-all(bf16[16,48,128]{2,1,0:T(8,128)(2,1)S(1)} %bitcast.5), channel_id=1, replica_groups={{0,8,16,24,128,136,144,152,256,264,272,280,384,392,400,408},{1,9,17,25,..., dimensions={0} | all-to-all | bytes 393216 | tf_op jit(solution)/shard_map/all_to_all | solution.py:63
  114.6 0.0 collective-permute-done.7.back_ref
  114.6 1.9 %collective-permute-start.8 = (bf16[48,128]{1,0:T(8,128)(2,1)S(1)}, bf16[48,128]{1,0:T(8,128)(2,1)S(1)}, u32[]{:S(2)}, u32[]{:S(2)}) collective-permute-start(bf16[48,128]{1,0:T(8,128)(2,1)S(1)} %reduce_sum.12), channel_id=1, source_target_pairs={{32,0},{33,1},{34,2},{35,3},{36,4},{37,5},{38,6},{39,7},{40,8},{41... | collective-permute-start | bytes 36872 | tf_op jit(solution)/shard_map/ppermute | solution.py:59
  116.5 5.2 %collective-permute-done.8 = bf16[48,128]{1,0:T(8,128)(2,1)S(1)} collective-permute-done((bf16[48,128]{1,0:T(8,128)(2,1)S(1)}, bf16[48,128]{1,0:T(8,128)(2,1)S(1)}, u32[]{:S(2)}, u32[]{:S(2)}) %collective-permute-start.8) | collective-permute-done | bytes 12320 | tf_op jit(solution)/shard_map/ppermute | solution.py:59
  121.7 15.7 %all_to_all.21 = bf16[16,48,128]{2,1,0:T(8,128)(2,1)S(1)} all-to-all(bf16[16,48,128]{2,1,0:T(8,128)(2,1)S(1)} %broadcast_in_dim.6), channel_id=1, replica_groups={{0,8,16,24,128,136,144,152,256,264,272,280,384,392,400,408},{1,9,17,25,..., dimensions={0} | all-to-all | bytes 393216 | tf_op jit(solution)/shard_map/all_to_all | solution.py:63
  137.4 1.0 broadcast_in_dim.16
  138.4 5.5 %all-to-all-start.3 = ((bf16[4,720,128]{2,1,0:T(8,128)(2,1)}), bf16[4,720,128]{2,1,0:T(8,128)(2,1)S(1)}, u32[]{:S(2)}, u32[]{:S(2)}) async-start(bf16[4,720,128]{2,1,0:T(8,128)(2,1)} %broadcast_in_dim.16), calls=%async_computation.3 | async-start | bytes 1474560 | tf_op jit(solution)/shard_map/all_to_all | solution.py:63
  143.9 0.0 copy-start.1
  143.9 1.3 copy-done.1
  145.2 3.2 %shard_map.84 = f32[256,1152]{1,0:T(8,128)} custom-call(f32[1]{0:T(128)S(6)} %copy.8.scale_ref, f32[1]{0:T(128)S(6)} %copy.9.bias_ref, bf16[256,1152]{1,0:T(8,128)(2,1)S(1)} %get-tuple-element.28.image_unit_ref.image_unit2_ref, bf16[272,1152]{1,0:T(8,128)(2,1)S(1)} %collective-permute-done.5.image_ref.image2_ref, ...), custom_call_target="tpu_custom_call" | custom-call | flops 679477248 | bytes 4792328 | tf_op jit(solution)/shard_map/pallas_call | solution.py:79
  148.4 3.5 %all-to-all-done.3.tiles_ref = bf16[4,720,128]{2,1,0:T(8,128)(2,1)S(1)} async-done(((bf16[4,720,128]{2,1,0:T(8,128)(2,1)}), bf16[4,720,128]{2,1,0:T(8,128)(2,1)S(1)}, u32[]{:S(2)}, u32[]{:S(2)}) %all-to-all-start.3) | async-done | bytes 737312 | tf_op jit(solution)/shard_map/all_to_all | solution.py:63
  151.9 1.1 shard_map.83
  (4 shorter events, 0.1 us)
Async XLA Ops:
  0.6 37.9 %copy-start.2 = (bf16[288,1152]{1,0:T(8,128)(2,1)S(1)}, bf16[288,1152]{1,0:T(8,128)(2,1)}, u32[]{:S(2)}) copy-start(bf16[288,1152]{1,0:T(8,128)(2,1)} %shard0_ref.1) | copy-start | bytes 1990660
  0.6 28.2 %collective-permute-start.1 = (bf16[288,1152]{1,0:T(8,128)(2,1)}, bf16[288,1152]{1,0:T(8,128)(2,1)S(1)}, u32[]{:S(2)}, u32[]{:S(2)}) collective-permute-start(bf16[288,1152]{1,0:T(8,128)(2,1)} %shard0_ref.1), channel_id=1, source_target_pairs={{2,0},{35,1},{0,2},{33,3},{6,4},{39,5},{4,6},{37,7},{10,8},{43,9},... | collective-permute-start | bytes 1990664 | tf_op jit(solution)/shard_map/ppermute | solution.py:59
  3.9 1.1 copy-start.7
  5.0 1.1 copy-start.8
  6.0 0.7 copy-start.9
  7.2 20.8 %collective-permute-start.2 = (bf16[272,1152]{1,0:T(8,128)(2,1)S(1)}, bf16[272,1152]{1,0:T(8,128)(2,1)S(1)}, u32[]{:S(2)}, u32[]{:S(2)}) collective-permute-start(bf16[272,1152]{1,0:T(8,128)(2,1)S(1)} %get-tuple-element.19.text_ref), channel_id=1, source_target_pairs={{508,0},{509,1},{510,2},{511,3},{0,4},{1,5},{2,6},{3,7},{4,8},{5,9... | collective-permute-start | bytes 1880072 | tf_op jit(solution)/shard_map/ppermute | solution.py:55
  10.7 20.1 %collective-permute-start.4 = (bf16[272,1152]{1,0:T(8,128)(2,1)S(1)}, bf16[272,1152]{1,0:T(8,128)(2,1)}, u32[]{:S(2)}, u32[]{:S(2)}) collective-permute-start(bf16[272,1152]{1,0:T(8,128)(2,1)S(1)} %get-tuple-element.21.image_ref.image0_ref), channel_id=1, source_target_pairs={{4,0},{5,1},{6,2},{7,3},{8,4},{9,5},{10,6},{11,7},{12,8},{13,9},{1... | collective-permute-start | bytes 1880072 | tf_op jit(solution)/shard_map/ppermute | solution.py:55
  16.7 0.8 copy-start.3
  17.5 21.0 %collective-permute-start = (bf16[288,1152]{1,0:T(8,128)(2,1)}, bf16[288,1152]{1,0:T(8,128)(2,1)S(1)}, u32[]{:S(2)}, u32[]{:S(2)}) collective-permute-start(bf16[288,1152]{1,0:T(8,128)(2,1)} %shard0_ref.1), channel_id=1, source_target_pairs={{1,0},{0,1},{3,2},{2,3},{5,4},{4,5},{7,6},{6,7},{9,8},{8,9},{11,10... | collective-permute-start | bytes 1990664 | tf_op jit(solution)/shard_map/ppermute | solution.py:59
  28.0 0.8 copy-start.5
  28.8 9.7 %collective-permute-start.3 = (bf16[288,1152]{1,0:T(8,128)(2,1)S(1)}, bf16[288,1152]{1,0:T(8,128)(2,1)}, u32[]{:S(2)}, u32[]{:S(2)}) collective-permute-start(bf16[288,1152]{1,0:T(8,128)(2,1)S(1)} %collective-permute-done.1.shard2_ref), channel_id=1, source_target_pairs={{1,0},{0,1},{3,2},{2,3},{5,4},{4,5},{7,6},{6,7},{9,8},{8,9},{11,10... | collective-permute-start | bytes 1990664 | tf_op jit(solution)/shard_map/ppermute | solution.py:59
  30.8 18.6 %collective-permute-start.5 = (bf16[272,1152]{1,0:T(8,128)(2,1)}, bf16[272,1152]{1,0:T(8,128)(2,1)S(1)}, u32[]{:S(2)}, u32[]{:S(2)}) collective-permute-start(bf16[272,1152]{1,0:T(8,128)(2,1)} %collective-permute-done.4.image1_ref), channel_id=1, source_target_pairs={{4,0},{5,1},{6,2},{7,3},{8,4},{9,5},{10,6},{11,7},{12,8},{13,9},{1... | collective-permute-start | bytes 1880072 | tf_op jit(solution)/shard_map/ppermute | solution.py:55
  38.5 1.1 copy-start.4
  39.6 4.2 %copy-start.6 = (bf16[272,1152]{1,0:T(8,128)(2,1)S(1)}, bf16[272,1152]{1,0:T(8,128)(2,1)}, u32[]{:S(2)}) copy-start(bf16[272,1152]{1,0:T(8,128)(2,1)} %copy-done.5) | copy-start | bytes 1880068
  49.2 3.7 %copy-start = (f32[256,1152]{1,0:T(8,128)}, f32[256,1152]{1,0:T(8,128)S(1)}, u32[]{:S(2)}) copy-start(f32[256,1152]{1,0:T(8,128)S(1)} %get-tuple-element.34.grad_ref) | copy-start | bytes 3538948
  52.9 5.0 %collective-permute-start.6 = (bf16[576,1152]{1,0:T(8,128)(2,1)S(1)}, bf16[576,1152]{1,0:T(8,128)(2,1)S(1)}, u32[]{:S(2)}, u32[]{:S(2)}) collective-permute-start(bf16[576,1152]{1,0:T(8,128)(2,1)S(1)} %get-tuple-element.31), channel_id=1, source_target_pairs={{1,0},{0,1},{3,2},{2,3},{5,4},{4,5},{7,6},{6,7},{9,8},{8,9},{11,10... | collective-permute-start | bytes 3981320 | tf_op jit(solution)/shard_map/ppermute | solution.py:59
  56.5 2.8 %copy-start.10 = (bf16[256,1152]{1,0:T(8,128)(2,1)}, bf16[256,1152]{1,0:T(8,128)(2,1)S(1)}, u32[]{:S(2)}) copy-start(bf16[256,1152]{1,0:T(8,128)(2,1)S(1)} %get-tuple-element.32) | copy-start | bytes 1769476
  59.3 16.6 %all-to-all-start = ((bf16[8,72,1152]{2,1,0:T(8,128)(2,1)}), bf16[8,72,1152]{2,1,0:T(8,128)(2,1)S(1)}, u32[]{:S(2)}, u32[]{:S(2)}) async-start(bf16[8,72,1152]{2,1,0:T(8,128)(2,1)} %bitcast.7), calls=%async_computation | async-start | bytes 2654208 | tf_op jit(solution)/shard_map/all_to_all | solution.py:63
  63.1 51.5 %collective-permute-start.7 = (bf16[256,1152]{1,0:T(8,128)(2,1)}, bf16[256,1152]{1,0:T(8,128)(2,1)}, u32[]{:S(2)}, u32[]{:S(2)}) collective-permute-start(bf16[256,1152]{1,0:T(8,128)(2,1)} %copy-done.10), channel_id=1, source_target_pairs={{4,0},{5,1},{6,2},{7,3},{8,4},{9,5},{10,6},{11,7},{12,8},{13,9},{1... | collective-permute-start | bytes 1769480 | tf_op jit(solution)/shard_map/ppermute | solution.py:55
  114.6 7.1 %collective-permute-start.8 = (bf16[48,128]{1,0:T(8,128)(2,1)S(1)}, bf16[48,128]{1,0:T(8,128)(2,1)S(1)}, u32[]{:S(2)}, u32[]{:S(2)}) collective-permute-start(bf16[48,128]{1,0:T(8,128)(2,1)S(1)} %reduce_sum.12), channel_id=1, source_target_pairs={{32,0},{33,1},{34,2},{35,3},{36,4},{37,5},{38,6},{39,7},{40,8},{41... | collective-permute-start | bytes 36872 | tf_op jit(solution)/shard_map/ppermute | solution.py:59
  138.4 13.5 %all-to-all-start.3 = ((bf16[4,720,128]{2,1,0:T(8,128)(2,1)}), bf16[4,720,128]{2,1,0:T(8,128)(2,1)S(1)}, u32[]{:S(2)}, u32[]{:S(2)}) async-start(bf16[4,720,128]{2,1,0:T(8,128)(2,1)} %broadcast_in_dim.16), calls=%async_computation.3 | async-start | bytes 1474560 | tf_op jit(solution)/shard_map/all_to_all | solution.py:63
  143.9 1.3 copy-start.1

commit v9 on v7

--- a/solution.py
+++ b/solution.py
@@ -71,7 +71,7 @@
     return jnp.sum(chunks.astype(F32), 0).astype(BF)
 
 
-def call(kernel, outs, specs, flops, scratch=()):
+def call(kernel, outs, specs, flops, scratch=(), vmem=20):
     def run(*args):
         moved = sum(a.size * a.dtype.itemsize for a in args) + sum(
             o.size * o.dtype.itemsize for o in outs
@@ -82,7 +82,7 @@
             in_specs=specs,
             out_specs=[VMEM] * len(outs),
             scratch_shapes=scratch,
-            compiler_params=pltpu.CompilerParams(vmem_limit_bytes=20 * 1024 * 1024),
+            compiler_params=pltpu.CompilerParams(vmem_limit_bytes=vmem * 1024 * 1024),
             cost_estimate=pl.CostEstimate(flops=flops, bytes_accessed=moved, transcendentals=0),
         )(*args)
 
@@ -285,6 +285,7 @@
         [hbm] * 2 + [VMEM],
         ROWS,
         [pltpu.VMEM((ROWS, D), BF), pltpu.SemaphoreType.DMA((2,))],
+        62,
     )(feats, text_embed, ids)
     image1 = shift(image0, -1)
     text1 = shift(text0, 1)

time: 150 us -> 150 us (level)
  local copies, waits for them, and re-layouts: 7.81 us -> 5.27 us
  Pallas kernels: 18.5 us -> 20.2 us
    unnamed x20 -> x18, local copies, waits for them, and re-layouts: 6.81 us -> 4.27 us
    pallas_call x8, Pallas kernels: 18.5 us -> 20.2 us  [run(): pl.pallas_call(kernel, out_shape=outs, in_specs=specs, out_specs=[VMEM] *...]
  transfers between devices with their start and end apart: 10 -> 10, of which waited for: 4 -> 3; matrix products, arithmetic and copies ran while one was open for 0% -> 0% of each run, Pallas kernels for 9% -> 10%
where the time goes in v9:
time: 150 us; the launch traced here: 149 us
  starting transfers between devices  59 us (39%)
  blocking collectives  52 us (35%)
  Pallas kernels  20.2 us (13%)
  waiting for transfers between devices  10.3 us (7%)
  local copies, waits for them, and re-layouts  5.27 us (4%)
  between operations  2.18 us (1%)
    all_to_all x3, blocking collectives, exchange(): lax.all_to_all(chunks, AXIS, 0, 0, axis_index_groups=groups, tiled=True)  52 us
    ppermute x4, starting transfers between devices, shift(): lax.ppermute(block, AXIS, [((i - 4 * distance) % N, i) for i in range(N)])  29.9 us
    ppermute x5, starting transfers between devices, move(): return lax.ppermute(block, AXIS, moves)  21.1 us
    pallas_call x8, Pallas kernels, run(): pl.pallas_call(kernel, out_shape=outs, in_specs=specs, out_specs=[VMEM] *...  20.2 us
    all_to_all x1, starting transfers between devices, exchange(): lax.all_to_all(chunks, AXIS, 0, 0, axis_index_groups=groups, tiled=True)  7.96 us
    ppermute x4, waiting for transfers between devices, shift(): lax.ppermute(block, AXIS, [((i - 4 * distance) % N, i) for i in range(N)])  7.27 us
    unnamed x18, local copies, waits for them, and re-layouts  4.27 us
  transfers between devices with their start and end apart: 10, of which 3 were waited for; matrix products, arithmetic and copies ran while one was open for 0% of the time, Pallas kernels for 10%

profile of v9, /device:TPU:1, one launch (start us, length us, event | category | flops | bytes accessed | tf_op | source)
XLA Modules:
  0.0 149.3 jit_solution(7128960041173282984)
XLA Ops:
  0.6 0.0 copy-start.4
  0.6 5.3 %collective-permute-start.1 = (bf16[288,1152]{1,0:T(8,128)(2,1)}, bf16[288,1152]{1,0:T(8,128)(2,1)S(1)}, u32[]{:S(2)}, u32[]{:S(2)}) collective-permute-start(bf16[288,1152]{1,0:T(8,128)(2,1)} %shard0_ref.1), channel_id=1, source_target_pairs={{2,0},{35,1},{0,2},{33,3},{6,4},{39,5},{4,6},{37,7},{10,8},{43,9},... | collective-permute-start | bytes 1990664 | tf_op jit(solution)/shard_map/ppermute | solution.py:59
  6.0 3.0 %shard_map.77 = (bf16[272,1152]{1,0:T(8,128)(2,1)}, bf16[272,1152]{1,0:T(8,128)(2,1)}) custom-call(bf16[256,1152]{1,0:T(8,128)(2,1)} %feats_ref.1, bf16[256,1152]{1,0:T(8,128)(2,1)} %text_ref.1, s32[1,256]{1,0:T(1,128)} %bitcast.8), custom_call_target="tpu_custom_call" | custom-call | flops 256 | bytes 2434048 | tf_op jit(solution)/shard_map/pallas_call | solution.py:79
  9.0 3.2 %collective-permute-start.2 = (bf16[272,1152]{1,0:T(8,128)(2,1)}, bf16[272,1152]{1,0:T(8,128)(2,1)S(1)}, u32[]{:S(2)}, u32[]{:S(2)}) collective-permute-start(bf16[272,1152]{1,0:T(8,128)(2,1)} %get-tuple-element.21.text_ref), channel_id=1, source_target_pairs={{508,0},{509,1},{510,2},{511,3},{0,4},{1,5},{2,6},{3,7},{4,8},{5,9... | collective-permute-start | bytes 1880072 | tf_op jit(solution)/shard_map/ppermute | solution.py:55
  12.3 12.5 %collective-permute-start.4 = (bf16[272,1152]{1,0:T(8,128)(2,1)}, bf16[272,1152]{1,0:T(8,128)(2,1)}, u32[]{:S(2)}, u32[]{:S(2)}) collective-permute-start(bf16[272,1152]{1,0:T(8,128)(2,1)} %get-tuple-element.23.image_ref.image0_ref), channel_id=1, source_target_pairs={{4,0},{5,1},{6,2},{7,3},{8,4},{9,5},{10,6},{11,7},{12,8},{13,9},{1... | collective-permute-start | bytes 1880072 | tf_op jit(solution)/shard_map/ppermute | solution.py:55
  24.8 3.8 %collective-permute-start = (bf16[288,1152]{1,0:T(8,128)(2,1)}, bf16[288,1152]{1,0:T(8,128)(2,1)S(1)}, u32[]{:S(2)}, u32[]{:S(2)}) collective-permute-start(bf16[288,1152]{1,0:T(8,128)(2,1)} %shard0_ref.1), channel_id=1, source_target_pairs={{1,0},{0,1},{3,2},{2,3},{5,4},{4,5},{7,6},{6,7},{9,8},{8,9},{11,10... | collective-permute-start | bytes 1990664 | tf_op jit(solution)/shard_map/ppermute | solution.py:59
  28.6 7.3 %collective-permute-done.2.text1_ref = bf16[272,1152]{1,0:T(8,128)(2,1)S(1)} collective-permute-done((bf16[272,1152]{1,0:T(8,128)(2,1)}, bf16[272,1152]{1,0:T(8,128)(2,1)S(1)}, u32[]{:S(2)}, u32[]{:S(2)}) %collective-permute-start.2) | collective-permute-done | bytes 626720 | tf_op jit(solution)/shard_map/ppermute | solution.py:55
  35.9 0.0 copy-start.7
  35.9 0.8 copy-done.7
  36.7 0.0 collective-permute-done.1.shard2_ref
  36.7 4.2 %collective-permute-start.3 = (bf16[288,1152]{1,0:T(8,128)(2,1)S(1)}, bf16[288,1152]{1,0:T(8,128)(2,1)S(1)}, u32[]{:S(2)}, u32[]{:S(2)}) collective-permute-start(bf16[288,1152]{1,0:T(8,128)(2,1)S(1)} %collective-permute-done.1.shard2_ref), channel_id=1, source_target_pairs={{1,0},{0,1},{3,2},{2,3},{5,4},{4,5},{7,6},{6,7},{9,8},{8,9},{11,10... | collective-permute-start | bytes 1990664 | tf_op jit(solution)/shard_map/ppermute | solution.py:59
  40.9 0.0 collective-permute-done.4.image1_ref
  40.9 5.8 %collective-permute-start.5 = (bf16[272,1152]{1,0:T(8,128)(2,1)}, bf16[272,1152]{1,0:T(8,128)(2,1)S(1)}, u32[]{:S(2)}, u32[]{:S(2)}) collective-permute-start(bf16[272,1152]{1,0:T(8,128)(2,1)} %collective-permute-done.4.image1_ref), channel_id=1, source_target_pairs={{4,0},{5,1},{6,2},{7,3},{8,4},{9,5},{10,6},{11,7},{12,8},{13,9},{1... | collective-permute-start | bytes 1880072 | tf_op jit(solution)/shard_map/ppermute | solution.py:55
  48.0 0.0 collective-permute-done.shard1_ref
  48.0 0.0 collective-permute-done.3.shard3_ref
  48.0 0.0 copy-done.4
  48.0 0.0 copy-start
  48.0 1.1 copy-done
  49.1 0.0 copy-start.5
  49.1 1.1 copy-done.5
  50.2 0.0 copy-start.6
  50.2 0.0 copy-start.8
  50.2 3.3 %shard_map.78 = (bf16[1152,1152]{1,0:T(8,128)(2,1)S(1)}, bf16[256,1152]{1,0:T(8,128)(2,1)S(1)}, f32[256,1152]{1,0:T(8,128)S(1)}) custom-call(s32[1]{0:T(128)} %bitcast.grp_ref, f32[1]{0:T(128)S(6)} %copy.8.scale_ref, f32[1]{0:T(128)S(6)} %copy.9.bias_ref, bf16[288,1152]{1,0:T(8,128)(2,1)S(1)} %copy-done.4, ...), custom_call_target="tpu_custom_call" | custom-call | flops 679477248 | bytes 8331276 | tf_op jit(solution)/shard_map/pallas_call | solution.py:79
  53.5 0.0 copy-done.6
  53.5 0.0 copy-done.8
  53.5 5.3 %shard_map.79 = (f32[1152,1152]{1,0:T(8,128)S(1)}, f32[256,1152]{1,0:T(8,128)S(1)}) custom-call(f32[1]{0:T(128)S(6)} %copy.8.scale_ref, f32[1]{0:T(128)S(6)} %copy.9.bias_ref, bf16[1152,1152]{1,0:T(8,128)(2,1)S(1)} %get-tuple-element.24.weight_ref, bf16[272,1152]{1,0:T(8,128)(2,1)S(1)} %copy-done.6, bf16[256,1152]{1,0:T(8,128)(2,1)S(1)} %get-tuple-element.25.raw_grad0_ref, ...), custom_call_target="tpu_custom_call" | custom-call | flops 2717908992 | bytes 13418504 | tf_op jit(solution)/shard_map/pallas_call | solution.py:79
  58.9 0.0 copy-start.2
  58.9 0.0 collective-permute-done.5.image_ref.image2_ref
  58.9 3.5 %shard_map.80 = (bf16[576,1152]{1,0:T(8,128)(2,1)S(1)}, bf16[1152,256]{1,0:T(8,128)(2,1)S(1)}, bf16[256,1152]{1,0:T(8,128)(2,1)S(1)}, bf16[256,1152]{1,0:T(8,128)(2,1)S(1)}, bf16[256,256]{1,0:T(8,128)(2,1)S(1)}) custom-call(s32[1]{0:T(128)} %bitcast.grp_ref, f32[1]{0:T(128)S(6)} %copy.8.scale_ref, f32[1]{0:T(128)S(6)} %copy.9.bias_ref, ...), custom_call_target="tpu_custom_call" | custom-call | flops 1358954496 | bytes 12443660 | tf_op jit(solution)/shard_map/pallas_call | solution.py:79
  62.4 0.0 copy-done.2
  62.4 4.7 %collective-permute-start.6 = (bf16[576,1152]{1,0:T(8,128)(2,1)S(1)}, bf16[576,1152]{1,0:T(8,128)(2,1)S(1)}, u32[]{:S(2)}, u32[]{:S(2)}) collective-permute-start(bf16[576,1152]{1,0:T(8,128)(2,1)S(1)} %get-tuple-element.33), channel_id=1, source_target_pairs={{1,0},{0,1},{3,2},{2,3},{5,4},{4,5},{7,6},{6,7},{9,8},{8,9},{11,10... | collective-permute-start | bytes 3981320 | tf_op jit(solution)/shard_map/ppermute | solution.py:59
  67.1 1.7 %shard_map.81 = (bf16[576,1152]{1,0:T(8,128)(2,1)S(1)}, bf16[256,1152]{1,0:T(8,128)(2,1)S(1)}) custom-call(s32[1]{0:T(128)} %bitcast.grp_ref, bf16[1152,256]{1,0:T(8,128)(2,1)S(1)} %get-tuple-element.28.turned_ref, bf16[256,1152]{1,0:T(8,128)(2,1)S(1)} %get-tuple-element.29.raw_grad_ref, ...), custom_call_target="tpu_custom_call" | custom-call | flops 679477248 | bytes 9125892 | tf_op jit(solution)/shard_map/pallas_call | solution.py:79
  68.8 1.0 collective-permute-done.6
  69.8 0.3 add_convert_fusion
  70.1 19.4 %all_to_all.20.chunks_ref = bf16[8,72,1152]{2,1,0:T(8,128)(2,1)S(1)} all-to-all(bf16[8,72,1152]{2,1,0:T(8,128)(2,1)S(1)} %bitcast.6), channel_id=1, replica_groups={{0,4,64,68,2,6,66,70},{477,449,29,1,511,483,63,35},{509,481,61,33,479,4..., dimensions={0} | all-to-all | bytes 2654208 | tf_op jit(solution)/shard_map/all_to_all | solution.py:63
  89.5 0.2 shard_map.82
  89.7 17.6 %all_to_all.21 = bf16[16,48,128]{2,1,0:T(8,128)(2,1)S(1)} all-to-all(bf16[16,48,128]{2,1,0:T(8,128)(2,1)S(1)} %bitcast.5), channel_id=1, replica_groups={{0,8,16,24,128,136,144,152,256,264,272,280,384,392,400,408},{1,9,17,25,..., dimensions={0} | all-to-all | bytes 393216 | tf_op jit(solution)/shard_map/all_to_all | solution.py:63
  107.3 3.0 %collective-permute-start.7 = (bf16[48,128]{1,0:T(8,128)(2,1)S(1)}, bf16[48,128]{1,0:T(8,128)(2,1)S(1)}, u32[]{:S(2)}, u32[]{:S(2)}) collective-permute-start(bf16[48,128]{1,0:T(8,128)(2,1)S(1)} %reduce_sum.12), channel_id=1, source_target_pairs={{32,0},{33,1},{34,2},{35,3},{36,4},{37,5},{38,6},{39,7},{40,8},{41... | collective-permute-start | bytes 36872 | tf_op jit(solution)/shard_map/ppermute | solution.py:59
  110.4 8.4 %collective-permute-start.8 = (bf16[256,1152]{1,0:T(8,128)(2,1)S(1)}, bf16[256,1152]{1,0:T(8,128)(2,1)S(1)}, u32[]{:S(2)}, u32[]{:S(2)}) collective-permute-start(bf16[256,1152]{1,0:T(8,128)(2,1)S(1)} %get-tuple-element.36), channel_id=1, source_target_pairs={{4,0},{5,1},{6,2},{7,3},{8,4},{9,5},{10,6},{11,7},{12,8},{13,9},{1... | collective-permute-start | bytes 1769480 | tf_op jit(solution)/shard_map/ppermute | solution.py:55
  118.7 0.0 collective-permute-done.7
  118.8 15.0 %all_to_all.22 = bf16[16,48,128]{2,1,0:T(8,128)(2,1)S(1)} all-to-all(bf16[16,48,128]{2,1,0:T(8,128)(2,1)S(1)} %broadcast_in_dim.4), channel_id=1, replica_groups={{0,8,16,24,128,136,144,152,256,264,272,280,384,392,400,408},{1,9,17,25,..., dimensions={0} | all-to-all | bytes 393216 | tf_op jit(solution)/shard_map/all_to_all | solution.py:63
  133.8 0.0 copy-start.1
  133.8 0.0 collective-permute-done.8.back_ref
  133.8 1.0 broadcast_in_dim.5
  134.8 8.0 %all-to-all-start.3 = ((bf16[4,720,128]{2,1,0:T(8,128)(2,1)}), bf16[4,720,128]{2,1,0:T(8,128)(2,1)S(1)}, u32[]{:S(2)}, u32[]{:S(2)}) async-start(bf16[4,720,128]{2,1,0:T(8,128)(2,1)} %broadcast_in_dim.5), calls=%async_computation.3 | async-start | bytes 1474560 | tf_op jit(solution)/shard_map/all_to_all | solution.py:63
  142.7 0.0 copy-done.1
  142.7 0.0 copy-start.3
  142.7 1.3 copy-done.3
  144.0 2.1 %shard_map.84 = f32[256,1152]{1,0:T(8,128)} custom-call(f32[1]{0:T(128)S(6)} %copy.8.scale_ref, f32[1]{0:T(128)S(6)} %copy.9.bias_ref, bf16[256,1152]{1,0:T(8,128)(2,1)S(1)} %get-tuple-element.30.image_unit_ref.image_unit2_ref, bf16[272,1152]{1,0:T(8,128)(2,1)S(1)} %collective-permute-done.5.image_ref.image2_ref, bf16[272,1152]{1,0:T(8,128)(2,1)S(1)} %copy-done.1, ...), custom_call_target="tpu_custom_call" | custom-call | flops 679477248 | bytes 4792328 | tf_op jit(solution)/shard_map/pallas_call | solution.py:79
  146.1 2.0 %all-to-all-done.3.tiles_ref = bf16[4,720,128]{2,1,0:T(8,128)(2,1)S(1)} async-done(((bf16[4,720,128]{2,1,0:T(8,128)(2,1)}), bf16[4,720,128]{2,1,0:T(8,128)(2,1)S(1)}, u32[]{:S(2)}, u32[]{:S(2)}) %all-to-all-start.3) | async-done | bytes 737312 | tf_op jit(solution)/shard_map/all_to_all | solution.py:63
  148.1 1.1 shard_map.83
  (4 shorter events, 0.1 us)
Async XLA Ops:
  0.6 47.4 %copy-start.4 = (bf16[288,1152]{1,0:T(8,128)(2,1)S(1)}, bf16[288,1152]{1,0:T(8,128)(2,1)}, u32[]{:S(2)}) copy-start(bf16[288,1152]{1,0:T(8,128)(2,1)} %shard0_ref.1) | copy-start | bytes 1990660
  0.6 36.1 %collective-permute-start.1 = (bf16[288,1152]{1,0:T(8,128)(2,1)}, bf16[288,1152]{1,0:T(8,128)(2,1)S(1)}, u32[]{:S(2)}, u32[]{:S(2)}) collective-permute-start(bf16[288,1152]{1,0:T(8,128)(2,1)} %shard0_ref.1), channel_id=1, source_target_pairs={{2,0},{35,1},{0,2},{33,3},{6,4},{39,5},{4,6},{37,7},{10,8},{43,9},... | collective-permute-start | bytes 1990664 | tf_op jit(solution)/shard_map/ppermute | solution.py:59
  9.0 26.8 %collective-permute-start.2 = (bf16[272,1152]{1,0:T(8,128)(2,1)}, bf16[272,1152]{1,0:T(8,128)(2,1)S(1)}, u32[]{:S(2)}, u32[]{:S(2)}) collective-permute-start(bf16[272,1152]{1,0:T(8,128)(2,1)} %get-tuple-element.21.text_ref), channel_id=1, source_target_pairs={{508,0},{509,1},{510,2},{511,3},{0,4},{1,5},{2,6},{3,7},{4,8},{5,9... | collective-permute-start | bytes 1880072 | tf_op jit(solution)/shard_map/ppermute | solution.py:55
  12.3 28.6 %collective-permute-start.4 = (bf16[272,1152]{1,0:T(8,128)(2,1)}, bf16[272,1152]{1,0:T(8,128)(2,1)}, u32[]{:S(2)}, u32[]{:S(2)}) collective-permute-start(bf16[272,1152]{1,0:T(8,128)(2,1)} %get-tuple-element.23.image_ref.image0_ref), channel_id=1, source_target_pairs={{4,0},{5,1},{6,2},{7,3},{8,4},{9,5},{10,6},{11,7},{12,8},{13,9},{1... | collective-permute-start | bytes 1880072 | tf_op jit(solution)/shard_map/ppermute | solution.py:55
  24.8 23.2 %collective-permute-start = (bf16[288,1152]{1,0:T(8,128)(2,1)}, bf16[288,1152]{1,0:T(8,128)(2,1)S(1)}, u32[]{:S(2)}, u32[]{:S(2)}) collective-permute-start(bf16[288,1152]{1,0:T(8,128)(2,1)} %shard0_ref.1), channel_id=1, source_target_pairs={{1,0},{0,1},{3,2},{2,3},{5,4},{4,5},{7,6},{6,7},{9,8},{8,9},{11,10... | collective-permute-start | bytes 1990664 | tf_op jit(solution)/shard_map/ppermute | solution.py:59
  35.9 0.8 copy-start.7
  36.7 11.3 %collective-permute-start.3 = (bf16[288,1152]{1,0:T(8,128)(2,1)S(1)}, bf16[288,1152]{1,0:T(8,128)(2,1)S(1)}, u32[]{:S(2)}, u32[]{:S(2)}) collective-permute-start(bf16[288,1152]{1,0:T(8,128)(2,1)S(1)} %collective-permute-done.1.shard2_ref), channel_id=1, source_target_pairs={{1,0},{0,1},{3,2},{2,3},{5,4},{4,5},{7,6},{6,7},{9,8},{8,9},{11,10... | collective-permute-start | bytes 1990664 | tf_op jit(solution)/shard_map/ppermute | solution.py:59
  40.9 18.0 %collective-permute-start.5 = (bf16[272,1152]{1,0:T(8,128)(2,1)}, bf16[272,1152]{1,0:T(8,128)(2,1)S(1)}, u32[]{:S(2)}, u32[]{:S(2)}) collective-permute-start(bf16[272,1152]{1,0:T(8,128)(2,1)} %collective-permute-done.4.image1_ref), channel_id=1, source_target_pairs={{4,0},{5,1},{6,2},{7,3},{8,4},{9,5},{10,6},{11,7},{12,8},{13,9},{1... | collective-permute-start | bytes 1880072 | tf_op jit(solution)/shard_map/ppermute | solution.py:55
  48.0 1.1 copy-start
  49.1 1.1 copy-start.5
  50.2 3.3 %copy-start.6 = (bf16[272,1152]{1,0:T(8,128)(2,1)S(1)}, bf16[272,1152]{1,0:T(8,128)(2,1)}, u32[]{:S(2)}) copy-start(bf16[272,1152]{1,0:T(8,128)(2,1)} %get-tuple-element.23.image_ref.image0_ref) | copy-start | bytes 1880068
  50.2 3.3 %copy-start.8 = (bf16[272,1152]{1,0:T(8,128)(2,1)S(1)}, bf16[272,1152]{1,0:T(8,128)(2,1)}, u32[]{:S(2)}) copy-start(bf16[272,1152]{1,0:T(8,128)(2,1)} %copy-done.7) | copy-start | bytes 1880068
  58.9 3.5 %copy-start.2 = (f32[256,1152]{1,0:T(8,128)}, f32[256,1152]{1,0:T(8,128)S(1)}, u32[]{:S(2)}) copy-start(f32[256,1152]{1,0:T(8,128)S(1)} %get-tuple-element.38.grad_ref) | copy-start | bytes 3538948
  62.4 7.4 %collective-permute-start.6 = (bf16[576,1152]{1,0:T(8,128)(2,1)S(1)}, bf16[576,1152]{1,0:T(8,128)(2,1)S(1)}, u32[]{:S(2)}, u32[]{:S(2)}) collective-permute-start(bf16[576,1152]{1,0:T(8,128)(2,1)S(1)} %get-tuple-element.33), channel_id=1, source_target_pairs={{1,0},{0,1},{3,2},{2,3},{5,4},{4,5},{7,6},{6,7},{9,8},{8,9},{11,10... | collective-permute-start | bytes 3981320 | tf_op jit(solution)/shard_map/ppermute | solution.py:59
  107.3 11.4 %collective-permute-start.7 = (bf16[48,128]{1,0:T(8,128)(2,1)S(1)}, bf16[48,128]{1,0:T(8,128)(2,1)S(1)}, u32[]{:S(2)}, u32[]{:S(2)}) collective-permute-start(bf16[48,128]{1,0:T(8,128)(2,1)S(1)} %reduce_sum.12), channel_id=1, source_target_pairs={{32,0},{33,1},{34,2},{35,3},{36,4},{37,5},{38,6},{39,7},{40,8},{41... | collective-permute-start | bytes 36872 | tf_op jit(solution)/shard_map/ppermute | solution.py:59
  110.4 23.4 %collective-permute-start.8 = (bf16[256,1152]{1,0:T(8,128)(2,1)S(1)}, bf16[256,1152]{1,0:T(8,128)(2,1)S(1)}, u32[]{:S(2)}, u32[]{:S(2)}) collective-permute-start(bf16[256,1152]{1,0:T(8,128)(2,1)S(1)} %get-tuple-element.36), channel_id=1, source_target_pairs={{4,0},{5,1},{6,2},{7,3},{8,4},{9,5},{10,6},{11,7},{12,8},{13,9},{1... | collective-permute-start | bytes 1769480 | tf_op jit(solution)/shard_map/ppermute | solution.py:55
  133.8 9.0 %copy-start.1 = (bf16[272,1152]{1,0:T(8,128)(2,1)S(1)}, bf16[272,1152]{1,0:T(8,128)(2,1)}, u32[]{:S(2)}) copy-start(bf16[272,1152]{1,0:T(8,128)(2,1)} %get-tuple-element.21.text_ref) | copy-start | bytes 1880068
  134.8 13.3 %all-to-all-start.3 = ((bf16[4,720,128]{2,1,0:T(8,128)(2,1)}), bf16[4,720,128]{2,1,0:T(8,128)(2,1)S(1)}, u32[]{:S(2)}, u32[]{:S(2)}) async-start(bf16[4,720,128]{2,1,0:T(8,128)(2,1)} %broadcast_in_dim.5), calls=%async_computation.3 | async-start | bytes 1474560 | tf_op jit(solution)/shard_map/all_to_all | solution.py:63
  142.7 1.3 copy-start.3

commit v10 on v9

--- a/solution.py
+++ b/solution.py
@@ -240,13 +240,14 @@
     core = grp_ref[0] % 2
     loads = load_quarters(core, part_ref, rows_ref, sems)
     add_quarters(core, turned_ref, raw_grad_ref[...], rows_ref, loads, keep_ref)
-    back_ref[...] = across(far_ref[...], image_unit_ref[...]).astype(BF)
+    back_ref[:ROWS, :] = across(far_ref[...], image_unit_ref[...]).astype(BF)
+    back_ref[ROWS:, :] = jnp.zeros((16, D), BF)
 
 
 def finish_kernel(scale_ref, bias_ref, image_unit2_ref, image2_ref, text_ref, grad_ref, back_ref, out_ref):
     image_unit2 = image_unit2_ref[...]
     near2 = pair(image_unit2, ids_down(image2_ref), text_ref, scale_ref[0], bias_ref[0])
-    out_ref[...] = scale_ref[0] * (grad_ref[...] + across(near2, image_unit2) + back_ref[...].astype(F32))
+    out_ref[...] = scale_ref[0] * (grad_ref[...] + across(near2, image_unit2) + back_ref[:ROWS, :].astype(F32))
 
 
 def pack_kernel(chunks_ref, out_ref):
@@ -313,7 +314,7 @@
     )(grp, *numbers, weight, image2, text1, part)
     keep, term = call(
         keep_kernel,
-        [shape(2 * SHARD, D, BF), shape(ROWS, D, BF)],
+        [shape(2 * SHARD, D, BF), packed],
         [SMEM] + [VMEM] * 4 + [anywhere],
         flops,
         scratch,

time: 150 us -> 152 us (1.013)
  blocking collectives: 52 us -> 35.1 us
  starting transfers between devices: 59 us -> 69 us
  waiting for transfers between devices: 10.3 us -> 17.7 us
    all_to_all x3 -> x2, blocking collectives: 52 us -> 35.1 us  [exchange(): lax.all_to_all(chunks, AXIS, 0, 0, axis_index_groups=groups, tiled=True)]
    all_to_all x1 -> x2, starting transfers between devices: 7.96 us -> 19.1 us  [exchange(): lax.all_to_all(chunks, AXIS, 0, 0, axis_index_groups=groups, tiled=True)]
    all_to_all x1 -> x2, waiting for transfers between devices: 2.02 us -> 6.48 us  [exchange(): lax.all_to_all(chunks, AXIS, 0, 0, axis_index_groups=groups, tiled=True)]
    ppermute x5, waiting for transfers between devices: 1 us -> 3.92 us  [move(): return lax.ppermute(block, AXIS, moves)]
  transfers between devices with their start and end apart: 10 -> 11, of which waited for: 3 -> 5; matrix products, arithmetic and copies ran while one was open for 0% -> 0% of each run, Pallas kernels for 10% -> 10%
where the time goes in v10:
time: 152 us; the launch traced here: 150 us
  starting transfers between devices  69 us (45%)
  blocking collectives  35.1 us (23%)
  Pallas kernels  20.9 us (14%)
  waiting for transfers between devices  17.7 us (12%)
  local copies, waits for them, and re-layouts  5.27 us (3%)
  between operations  2.16 us (1%)
    all_to_all x2, blocking collectives, exchange(): lax.all_to_all(chunks, AXIS, 0, 0, axis_index_groups=groups, tiled=True)  35.1 us
    ppermute x4, starting transfers between devices, shift(): lax.ppermute(block, AXIS, [((i - 4 * distance) % N, i) for i in range(N)])  28.8 us
    ppermute x5, starting transfers between devices, move(): return lax.ppermute(block, AXIS, moves)  21.1 us
    pallas_call x8, Pallas kernels, run(): pl.pallas_call(kernel, out_shape=outs, in_specs=specs, out_specs=[VMEM] *...  20.9 us
    all_to_all x2, starting transfers between devices, exchange(): lax.all_to_all(chunks, AXIS, 0, 0, axis_index_groups=groups, tiled=True)  19.1 us
    ppermute x4, waiting for transfers between devices, shift(): lax.ppermute(block, AXIS, [((i - 4 * distance) % N, i) for i in range(N)])  7.27 us
    all_to_all x2, waiting for transfers between devices, exchange(): lax.all_to_all(chunks, AXIS, 0, 0, axis_index_groups=groups, tiled=True)  6.48 us
    unnamed x18, local copies, waits for them, and re-layouts  4.27 us
  transfers between devices with their start and end apart: 11, of which 5 were waited for; matrix products, arithmetic and copies ran while one was open for 0% of the time, Pallas kernels for 10%

profile of v10, /device:TPU:1, one launch (start us, length us, event | category | flops | bytes accessed | tf_op | source)
XLA Modules:
  0.0 150.4 jit_solution(14429526133448785463)
XLA Ops:
  0.6 0.0 copy-start.4
  0.6 5.3 %collective-permute-start.1 = (bf16[288,1152]{1,0:T(8,128)(2,1)}, bf16[288,1152]{1,0:T(8,128)(2,1)S(1)}, u32[]{:S(2)}, u32[]{:S(2)}) collective-permute-start(bf16[288,1152]{1,0:T(8,128)(2,1)} %shard0_ref.1), channel_id=1, source_target_pairs={{2,0},{35,1},{0,2},{33,3},{6,4},{39,5},{4,6},{37,7},{10,8},{43,9},... | collective-permute-start | bytes 1990664 | tf_op jit(solution)/shard_map/ppermute | solution.py:59
  6.0 3.1 %shard_map.77 = (bf16[272,1152]{1,0:T(8,128)(2,1)}, bf16[272,1152]{1,0:T(8,128)(2,1)}) custom-call(bf16[256,1152]{1,0:T(8,128)(2,1)} %feats_ref.1, bf16[256,1152]{1,0:T(8,128)(2,1)} %text_ref.1, s32[1,256]{1,0:T(1,128)} %bitcast.7), custom_call_target="tpu_custom_call" | custom-call | flops 256 | bytes 2434048 | tf_op jit(solution)/shard_map/pallas_call | solution.py:79
  9.1 3.2 %collective-permute-start.2 = (bf16[272,1152]{1,0:T(8,128)(2,1)}, bf16[272,1152]{1,0:T(8,128)(2,1)S(1)}, u32[]{:S(2)}, u32[]{:S(2)}) collective-permute-start(bf16[272,1152]{1,0:T(8,128)(2,1)} %get-tuple-element.21.text_ref), channel_id=1, source_target_pairs={{508,0},{509,1},{510,2},{511,3},{0,4},{1,5},{2,6},{3,7},{4,8},{5,9... | collective-permute-start | bytes 1880072 | tf_op jit(solution)/shard_map/ppermute | solution.py:55
  12.3 12.5 %collective-permute-start.4 = (bf16[272,1152]{1,0:T(8,128)(2,1)}, bf16[272,1152]{1,0:T(8,128)(2,1)}, u32[]{:S(2)}, u32[]{:S(2)}) collective-permute-start(bf16[272,1152]{1,0:T(8,128)(2,1)} %get-tuple-element.23.image_ref.image0_ref), channel_id=1, source_target_pairs={{4,0},{5,1},{6,2},{7,3},{8,4},{9,5},{10,6},{11,7},{12,8},{13,9},{1... | collective-permute-start | bytes 1880072 | tf_op jit(solution)/shard_map/ppermute | solution.py:55
  24.8 3.8 %collective-permute-start = (bf16[288,1152]{1,0:T(8,128)(2,1)}, bf16[288,1152]{1,0:T(8,128)(2,1)S(1)}, u32[]{:S(2)}, u32[]{:S(2)}) collective-permute-start(bf16[288,1152]{1,0:T(8,128)(2,1)} %shard0_ref.1), channel_id=1, source_target_pairs={{1,0},{0,1},{3,2},{2,3},{5,4},{4,5},{7,6},{6,7},{9,8},{8,9},{11,10... | collective-permute-start | bytes 1990664 | tf_op jit(solution)/shard_map/ppermute | solution.py:59
  28.6 7.3 %collective-permute-done.2.text1_ref = bf16[272,1152]{1,0:T(8,128)(2,1)S(1)} collective-permute-done((bf16[272,1152]{1,0:T(8,128)(2,1)}, bf16[272,1152]{1,0:T(8,128)(2,1)S(1)}, u32[]{:S(2)}, u32[]{:S(2)}) %collective-permute-start.2) | collective-permute-done | bytes 626720 | tf_op jit(solution)/shard_map/ppermute | solution.py:55
  35.9 0.0 copy-start.7
  35.9 0.8 copy-done.7
  36.7 0.0 collective-permute-done.1.shard2_ref
  36.7 4.2 %collective-permute-start.3 = (bf16[288,1152]{1,0:T(8,128)(2,1)S(1)}, bf16[288,1152]{1,0:T(8,128)(2,1)S(1)}, u32[]{:S(2)}, u32[]{:S(2)}) collective-permute-start(bf16[288,1152]{1,0:T(8,128)(2,1)S(1)} %collective-permute-done.1.shard2_ref), channel_id=1, source_target_pairs={{1,0},{0,1},{3,2},{2,3},{5,4},{4,5},{7,6},{6,7},{9,8},{8,9},{11,10... | collective-permute-start | bytes 1990664 | tf_op jit(solution)/shard_map/ppermute | solution.py:59
  40.9 0.0 collective-permute-done.4.image1_ref
  40.9 5.8 %collective-permute-start.5 = (bf16[272,1152]{1,0:T(8,128)(2,1)}, bf16[272,1152]{1,0:T(8,128)(2,1)S(1)}, u32[]{:S(2)}, u32[]{:S(2)}) collective-permute-start(bf16[272,1152]{1,0:T(8,128)(2,1)} %collective-permute-done.4.image1_ref), channel_id=1, source_target_pairs={{4,0},{5,1},{6,2},{7,3},{8,4},{9,5},{10,6},{11,7},{12,8},{13,9},{1... | collective-permute-start | bytes 1880072 | tf_op jit(solution)/shard_map/ppermute | solution.py:55
  48.0 0.0 collective-permute-done.shard1_ref
  48.0 0.0 collective-permute-done.3.shard3_ref
  48.1 0.0 copy-done.4
  48.1 0.0 copy-start
  48.1 1.1 copy-done
  49.1 0.0 copy-start.5
  49.1 1.1 copy-done.5
  50.2 0.0 copy-start.6
  50.2 0.0 copy-start.8
  50.2 3.3 %shard_map.78 = (bf16[1152,1152]{1,0:T(8,128)(2,1)S(1)}, bf16[256,1152]{1,0:T(8,128)(2,1)S(1)}, f32[256,1152]{1,0:T(8,128)S(1)}) custom-call(s32[1]{0:T(128)} %bitcast.grp_ref, f32[1]{0:T(128)S(6)} %copy.8.scale_ref, f32[1]{0:T(128)S(6)} %copy.9.bias_ref, bf16[288,1152]{1,0:T(8,128)(2,1)S(1)} %copy-done.4, ...), custom_call_target="tpu_custom_call" | custom-call | flops 679477248 | bytes 8331276 | tf_op jit(solution)/shard_map/pallas_call | solution.py:79
  53.5 0.0 copy-done.6
  53.5 0.0 copy-done.8
  53.5 5.3 %shard_map.79 = (f32[1152,1152]{1,0:T(8,128)S(1)}, f32[256,1152]{1,0:T(8,128)S(1)}) custom-call(f32[1]{0:T(128)S(6)} %copy.8.scale_ref, f32[1]{0:T(128)S(6)} %copy.9.bias_ref, bf16[1152,1152]{1,0:T(8,128)(2,1)S(1)} %get-tuple-element.24.weight_ref, bf16[272,1152]{1,0:T(8,128)(2,1)S(1)} %copy-done.6, bf16[256,1152]{1,0:T(8,128)(2,1)S(1)} %get-tuple-element.25.raw_grad0_ref, ...), custom_call_target="tpu_custom_call" | custom-call | flops 2717908992 | bytes 13418504 | tf_op jit(solution)/shard_map/pallas_call | solution.py:79
  58.9 0.0 copy-start.2
  58.9 0.0 collective-permute-done.5.image_ref.image2_ref
  58.9 3.4 %shard_map.80 = (bf16[576,1152]{1,0:T(8,128)(2,1)S(1)}, bf16[1152,256]{1,0:T(8,128)(2,1)S(1)}, bf16[256,1152]{1,0:T(8,128)(2,1)S(1)}, bf16[256,1152]{1,0:T(8,128)(2,1)S(1)}, bf16[256,256]{1,0:T(8,128)(2,1)S(1)}) custom-call(s32[1]{0:T(128)} %bitcast.grp_ref, f32[1]{0:T(128)S(6)} %copy.8.scale_ref, f32[1]{0:T(128)S(6)} %copy.9.bias_ref, ...), custom_call_target="tpu_custom_call" | custom-call | flops 1358954496 | bytes 12443660 | tf_op jit(solution)/shard_map/pallas_call | solution.py:79
  62.3 0.0 copy-done.2
  62.4 4.7 %collective-permute-start.6 = (bf16[576,1152]{1,0:T(8,128)(2,1)S(1)}, bf16[576,1152]{1,0:T(8,128)(2,1)S(1)}, u32[]{:S(2)}, u32[]{:S(2)}) collective-permute-start(bf16[576,1152]{1,0:T(8,128)(2,1)S(1)} %get-tuple-element.33), channel_id=1, source_target_pairs={{1,0},{0,1},{3,2},{2,3},{5,4},{4,5},{7,6},{6,7},{9,8},{8,9},{11,10... | collective-permute-start | bytes 3981320 | tf_op jit(solution)/shard_map/ppermute | solution.py:59
  67.1 1.7 %shard_map.81 = (bf16[576,1152]{1,0:T(8,128)(2,1)S(1)}, bf16[272,1152]{1,0:T(8,128)(2,1)S(1)}) custom-call(s32[1]{0:T(128)} %bitcast.grp_ref, bf16[1152,256]{1,0:T(8,128)(2,1)S(1)} %get-tuple-element.28.turned_ref, bf16[256,1152]{1,0:T(8,128)(2,1)S(1)} %get-tuple-element.29.raw_grad_ref, ...), custom_call_target="tpu_custom_call" | custom-call | flops 679477248 | bytes 9162756 | tf_op jit(solution)/shard_map/pallas_call | solution.py:79
  68.8 1.0 collective-permute-done.6
  69.8 0.3 add_convert_fusion
  70.1 19.5 %all_to_all.20.chunks_ref = bf16[8,72,1152]{2,1,0:T(8,128)(2,1)S(1)} all-to-all(bf16[8,72,1152]{2,1,0:T(8,128)(2,1)S(1)} %bitcast.5), channel_id=1, replica_groups={{0,4,64,68,2,6,66,70},{477,449,29,1,511,483,63,35},{509,481,61,33,479,4..., dimensions={0} | all-to-all | bytes 2654208 | tf_op jit(solution)/shard_map/all_to_all | solution.py:63
  89.5 0.8 shard_map.82
  90.4 6.2 %all-to-all-start.1 = ((bf16[16,48,128]{2,1,0:T(8,128)(2,1)}), bf16[16,48,128]{2,1,0:T(8,128)(2,1)S(1)}, u32[]{:S(2)}, u32[]{:S(2)}) async-start(bf16[16,48,128]{2,1,0:T(8,128)(2,1)} %bitcast.3), calls=%async_computation.1 | async-start | bytes 393216 | tf_op jit(solution)/shard_map/all_to_all | solution.py:63
  96.6 7.3 %collective-permute-start.8 = (bf16[272,1152]{1,0:T(8,128)(2,1)S(1)}, bf16[272,1152]{1,0:T(8,128)(2,1)S(1)}, u32[]{:S(2)}, u32[]{:S(2)}) collective-permute-start(bf16[272,1152]{1,0:T(8,128)(2,1)S(1)} %get-tuple-element.36), channel_id=1, source_target_pairs={{4,0},{5,1},{6,2},{7,3},{8,4},{9,5},{10,6},{11,7},{12,8},{13,9},{1... | collective-permute-start | bytes 1880072 | tf_op jit(solution)/shard_map/ppermute | solution.py:55
  103.9 4.3 %all-to-all-done.1 = bf16[16,48,128]{2,1,0:T(8,128)(2,1)S(1)} async-done(((bf16[16,48,128]{2,1,0:T(8,128)(2,1)}), bf16[16,48,128]{2,1,0:T(8,128)(2,1)S(1)}, u32[]{:S(2)}, u32[]{:S(2)}) %all-to-all-start.1) | async-done | bytes 196640 | tf_op jit(solution)/shard_map/all_to_all | solution.py:63
  108.2 3.0 %collective-permute-start.7 = (bf16[48,128]{1,0:T(8,128)(2,1)S(1)}, bf16[48,128]{1,0:T(8,128)(2,1)S(1)}, u32[]{:S(2)}, u32[]{:S(2)}) collective-permute-start(bf16[48,128]{1,0:T(8,128)(2,1)S(1)} %reduce_sum.12), channel_id=1, source_target_pairs={{32,0},{33,1},{34,2},{35,3},{36,4},{37,5},{38,6},{39,7},{40,8},{41... | collective-permute-start | bytes 36872 | tf_op jit(solution)/shard_map/ppermute | solution.py:59
  111.2 2.9 %collective-permute-done.7 = bf16[48,128]{1,0:T(8,128)(2,1)S(1)} collective-permute-done((bf16[48,128]{1,0:T(8,128)(2,1)S(1)}, bf16[48,128]{1,0:T(8,128)(2,1)S(1)}, u32[]{:S(2)}, u32[]{:S(2)}) %collective-permute-start.7) | collective-permute-done | bytes 12320 | tf_op jit(solution)/shard_map/ppermute | solution.py:59
  114.2 15.6 %all_to_all.21 = bf16[16,48,128]{2,1,0:T(8,128)(2,1)S(1)} all-to-all(bf16[16,48,128]{2,1,0:T(8,128)(2,1)S(1)} %broadcast_in_dim.4), channel_id=1, replica_groups={{0,8,16,24,128,136,144,152,256,264,272,280,384,392,400,408},{1,9,17,25,..., dimensions={0} | all-to-all | bytes 393216 | tf_op jit(solution)/shard_map/all_to_all | solution.py:63
  129.8 0.0 copy-start.1
  129.9 0.0 collective-permute-done.8.back_ref
  129.9 1.0 broadcast_in_dim.5
  130.8 12.9 %all-to-all-start.3 = ((bf16[4,720,128]{2,1,0:T(8,128)(2,1)}), bf16[4,720,128]{2,1,0:T(8,128)(2,1)S(1)}, u32[]{:S(2)}, u32[]{:S(2)}) async-start(bf16[4,720,128]{2,1,0:T(8,128)(2,1)} %broadcast_in_dim.5), calls=%async_computation.3 | async-start | bytes 1474560 | tf_op jit(solution)/shard_map/all_to_all | solution.py:63
  143.8 0.0 copy-done.1
  143.8 0.0 copy-start.3
  143.8 1.3 copy-done.3
  145.0 2.1 %shard_map.84 = f32[256,1152]{1,0:T(8,128)} custom-call(f32[1]{0:T(128)S(6)} %copy.8.scale_ref, f32[1]{0:T(128)S(6)} %copy.9.bias_ref, bf16[256,1152]{1,0:T(8,128)(2,1)S(1)} %get-tuple-element.30.image_unit_ref.image_unit2_ref, bf16[272,1152]{1,0:T(8,128)(2,1)S(1)} %collective-permute-done.5.image_ref.image2_ref, bf16[272,1152]{1,0:T(8,128)(2,1)S(1)} %copy-done.1, ...), custom_call_target="tpu_custom_call" | custom-call | flops 679477248 | bytes 4829192 | tf_op jit(solution)/shard_map/pallas_call | solution.py:79
  147.1 2.2 %all-to-all-done.3.tiles_ref = bf16[4,720,128]{2,1,0:T(8,128)(2,1)S(1)} async-done(((bf16[4,720,128]{2,1,0:T(8,128)(2,1)}), bf16[4,720,128]{2,1,0:T(8,128)(2,1)S(1)}, u32[]{:S(2)}, u32[]{:S(2)}) %all-to-all-start.3) | async-done | bytes 737312 | tf_op jit(solution)/shard_map/all_to_all | solution.py:63
  149.3 1.1 shard_map.83
  (4 shorter events, 0.1 us)
Async XLA Ops:
  0.6 47.4 %copy-start.4 = (bf16[288,1152]{1,0:T(8,128)(2,1)S(1)}, bf16[288,1152]{1,0:T(8,128)(2,1)}, u32[]{:S(2)}) copy-start(bf16[288,1152]{1,0:T(8,128)(2,1)} %shard0_ref.1) | copy-start | bytes 1990660
  0.6 36.1 %collective-permute-start.1 = (bf16[288,1152]{1,0:T(8,128)(2,1)}, bf16[288,1152]{1,0:T(8,128)(2,1)S(1)}, u32[]{:S(2)}, u32[]{:S(2)}) collective-permute-start(bf16[288,1152]{1,0:T(8,128)(2,1)} %shard0_ref.1), channel_id=1, source_target_pairs={{2,0},{35,1},{0,2},{33,3},{6,4},{39,5},{4,6},{37,7},{10,8},{43,9},... | collective-permute-start | bytes 1990664 | tf_op jit(solution)/shard_map/ppermute | solution.py:59
  9.1 26.8 %collective-permute-start.2 = (bf16[272,1152]{1,0:T(8,128)(2,1)}, bf16[272,1152]{1,0:T(8,128)(2,1)S(1)}, u32[]{:S(2)}, u32[]{:S(2)}) collective-permute-start(bf16[272,1152]{1,0:T(8,128)(2,1)} %get-tuple-element.21.text_ref), channel_id=1, source_target_pairs={{508,0},{509,1},{510,2},{511,3},{0,4},{1,5},{2,6},{3,7},{4,8},{5,9... | collective-permute-start | bytes 1880072 | tf_op jit(solution)/shard_map/ppermute | solution.py:55
  12.3 28.6 %collective-permute-start.4 = (bf16[272,1152]{1,0:T(8,128)(2,1)}, bf16[272,1152]{1,0:T(8,128)(2,1)}, u32[]{:S(2)}, u32[]{:S(2)}) collective-permute-start(bf16[272,1152]{1,0:T(8,128)(2,1)} %get-tuple-element.23.image_ref.image0_ref), channel_id=1, source_target_pairs={{4,0},{5,1},{6,2},{7,3},{8,4},{9,5},{10,6},{11,7},{12,8},{13,9},{1... | collective-permute-start | bytes 1880072 | tf_op jit(solution)/shard_map/ppermute | solution.py:55
  24.8 23.2 %collective-permute-start = (bf16[288,1152]{1,0:T(8,128)(2,1)}, bf16[288,1152]{1,0:T(8,128)(2,1)S(1)}, u32[]{:S(2)}, u32[]{:S(2)}) collective-permute-start(bf16[288,1152]{1,0:T(8,128)(2,1)} %shard0_ref.1), channel_id=1, source_target_pairs={{1,0},{0,1},{3,2},{2,3},{5,4},{4,5},{7,6},{6,7},{9,8},{8,9},{11,10... | collective-permute-start | bytes 1990664 | tf_op jit(solution)/shard_map/ppermute | solution.py:59
  35.9 0.8 copy-start.7
  36.7 11.3 %collective-permute-start.3 = (bf16[288,1152]{1,0:T(8,128)(2,1)S(1)}, bf16[288,1152]{1,0:T(8,128)(2,1)S(1)}, u32[]{:S(2)}, u32[]{:S(2)}) collective-permute-start(bf16[288,1152]{1,0:T(8,128)(2,1)S(1)} %collective-permute-done.1.shard2_ref), channel_id=1, source_target_pairs={{1,0},{0,1},{3,2},{2,3},{5,4},{4,5},{7,6},{6,7},{9,8},{8,9},{11,10... | collective-permute-start | bytes 1990664 | tf_op jit(solution)/shard_map/ppermute | solution.py:59
  40.9 18.0 %collective-permute-start.5 = (bf16[272,1152]{1,0:T(8,128)(2,1)}, bf16[272,1152]{1,0:T(8,128)(2,1)S(1)}, u32[]{:S(2)}, u32[]{:S(2)}) collective-permute-start(bf16[272,1152]{1,0:T(8,128)(2,1)} %collective-permute-done.4.image1_ref), channel_id=1, source_target_pairs={{4,0},{5,1},{6,2},{7,3},{8,4},{9,5},{10,6},{11,7},{12,8},{13,9},{1... | collective-permute-start | bytes 1880072 | tf_op jit(solution)/shard_map/ppermute | solution.py:55
  48.1 1.1 copy-start
  49.1 1.1 copy-start.5
  50.2 3.3 %copy-start.6 = (bf16[272,1152]{1,0:T(8,128)(2,1)S(1)}, bf16[272,1152]{1,0:T(8,128)(2,1)}, u32[]{:S(2)}) copy-start(bf16[272,1152]{1,0:T(8,128)(2,1)} %get-tuple-element.23.image_ref.image0_ref) | copy-start | bytes 1880068
  50.2 3.3 %copy-start.8 = (bf16[272,1152]{1,0:T(8,128)(2,1)S(1)}, bf16[272,1152]{1,0:T(8,128)(2,1)}, u32[]{:S(2)}) copy-start(bf16[272,1152]{1,0:T(8,128)(2,1)} %copy-done.7) | copy-start | bytes 1880068
  58.9 3.5 %copy-start.2 = (f32[256,1152]{1,0:T(8,128)}, f32[256,1152]{1,0:T(8,128)S(1)}, u32[]{:S(2)}) copy-start(f32[256,1152]{1,0:T(8,128)S(1)} %get-tuple-element.38.grad_ref) | copy-start | bytes 3538948
  62.4 7.4 %collective-permute-start.6 = (bf16[576,1152]{1,0:T(8,128)(2,1)S(1)}, bf16[576,1152]{1,0:T(8,128)(2,1)S(1)}, u32[]{:S(2)}, u32[]{:S(2)}) collective-permute-start(bf16[576,1152]{1,0:T(8,128)(2,1)S(1)} %get-tuple-element.33), channel_id=1, source_target_pairs={{1,0},{0,1},{3,2},{2,3},{5,4},{4,5},{7,6},{6,7},{9,8},{8,9},{11,10... | collective-permute-start | bytes 3981320 | tf_op jit(solution)/shard_map/ppermute | solution.py:59
  90.4 17.8 %all-to-all-start.1 = ((bf16[16,48,128]{2,1,0:T(8,128)(2,1)}), bf16[16,48,128]{2,1,0:T(8,128)(2,1)S(1)}, u32[]{:S(2)}, u32[]{:S(2)}) async-start(bf16[16,48,128]{2,1,0:T(8,128)(2,1)} %bitcast.3), calls=%async_computation.1 | async-start | bytes 393216 | tf_op jit(solution)/shard_map/all_to_all | solution.py:63
  96.6 33.3 %collective-permute-start.8 = (bf16[272,1152]{1,0:T(8,128)(2,1)S(1)}, bf16[272,1152]{1,0:T(8,128)(2,1)S(1)}, u32[]{:S(2)}, u32[]{:S(2)}) collective-permute-start(bf16[272,1152]{1,0:T(8,128)(2,1)S(1)} %get-tuple-element.36), channel_id=1, source_target_pairs={{4,0},{5,1},{6,2},{7,3},{8,4},{9,5},{10,6},{11,7},{12,8},{13,9},{1... | collective-permute-start | bytes 1880072 | tf_op jit(solution)/shard_map/ppermute | solution.py:55
  108.2 5.9 %collective-permute-start.7 = (bf16[48,128]{1,0:T(8,128)(2,1)S(1)}, bf16[48,128]{1,0:T(8,128)(2,1)S(1)}, u32[]{:S(2)}, u32[]{:S(2)}) collective-permute-start(bf16[48,128]{1,0:T(8,128)(2,1)S(1)} %reduce_sum.12), channel_id=1, source_target_pairs={{32,0},{33,1},{34,2},{35,3},{36,4},{37,5},{38,6},{39,7},{40,8},{41... | collective-permute-start | bytes 36872 | tf_op jit(solution)/shard_map/ppermute | solution.py:59
  129.8 13.9 %copy-start.1 = (bf16[272,1152]{1,0:T(8,128)(2,1)S(1)}, bf16[272,1152]{1,0:T(8,128)(2,1)}, u32[]{:S(2)}) copy-start(bf16[272,1152]{1,0:T(8,128)(2,1)} %get-tuple-element.21.text_ref) | copy-start | bytes 1880068
  130.8 18.5 %all-to-all-start.3 = ((bf16[4,720,128]{2,1,0:T(8,128)(2,1)}), bf16[4,720,128]{2,1,0:T(8,128)(2,1)S(1)}, u32[]{:S(2)}, u32[]{:S(2)}) async-start(bf16[4,720,128]{2,1,0:T(8,128)(2,1)} %broadcast_in_dim.5), calls=%async_computation.3 | async-start | bytes 1474560 | tf_op jit(solution)/shard_map/all_to_all | solution.py:63
  143.8 1.3 copy-start.3

commit v11 on v9

--- a/solution.py
+++ b/solution.py
@@ -83,7 +83,7 @@
             out_specs=[VMEM] * len(outs),
             scratch_shapes=scratch,
             compiler_params=pltpu.CompilerParams(vmem_limit_bytes=vmem * 1024 * 1024),
-            cost_estimate=pl.CostEstimate(flops=flops, bytes_accessed=moved, transcendentals=0),
+            cost_estimate=pl.CostEstimate(flops=flops, bytes_accessed=moved if flops else 0, transcendentals=0),
         )(*args)
 
     return run
@@ -291,17 +291,17 @@
     text1 = shift(text0, 1)
     shard2 = move(proj_weight, swap_x((1, 3)))
     shard1 = move(proj_weight, CORES)
-    shard3 = move(lax.optimization_barrier((shard2, text1))[0], CORES)
+    shard3 = move(lax.optimization_barrier((shard2, text1, image1))[0], CORES)
     image2 = shift(image1, -1)
     weight, raw_grad0, grad = call(
-        own_kernel, [shape(D, D, BF), shape(ROWS, D, BF), shape(ROWS, D, F32)], [SMEM] * 3 + [hbm] * 4 + [VMEM] * 2, flops,
+        own_kernel, [shape(D, D, BF), shape(ROWS, D, BF), shape(ROWS, D, F32)], [SMEM] * 3 + [hbm] * 4 + [VMEM] * 2, 0,
         [pltpu.SemaphoreType.DMA((4,))],
     )(grp, *numbers, proj_weight, shard1, shard2, shard3, image0, text0)
     part, grad = call(
         next_kernel,
         [shape(D, D, F32), shape(ROWS, D, F32)],
         [SMEM] * 2 + [VMEM] * 7,
-        4 * flops,
+        0,
         [pltpu.VMEM((D, 2 * ROWS), BF), pltpu.VMEM((2 * ROWS, D), BF)],
     )(*numbers, weight, image0, raw_grad0, image1, text0, text1, grad)
     send, turned, raw_grad2, image_unit2, far = call(

time: 150 us -> 153 us (1.020)
  waiting for transfers between devices: 10.3 us -> 20.9 us
  starting transfers between devices: 59 us -> 53.4 us
  blocking collectives: 52 us -> 49.1 us
  Pallas kernels: 20.2 us -> 21.9 us
    ppermute x4, waiting for transfers between devices: 7.27 us -> 18.7 us  [shift(): lax.ppermute(block, AXIS, [((i - 4 * distance) % N, i) for i in range(N)])]
    ppermute x4, starting transfers between devices: 29.9 us -> 26 us  [shift(): lax.ppermute(block, AXIS, [((i - 4 * distance) % N, i) for i in range(N)])]
    all_to_all x3, blocking collectives: 52 us -> 49.1 us  [exchange(): lax.all_to_all(chunks, AXIS, 0, 0, axis_index_groups=groups, tiled=True)]
    ppermute x5, starting transfers between devices: 21.1 us -> 18.5 us  [move(): return lax.ppermute(block, AXIS, moves)]
    pallas_call x8, Pallas kernels: 20.2 us -> 21.9 us  [run(): pl.pallas_call(kernel, out_shape=outs, in_specs=specs, out_specs=[VMEM] *...]
    unnamed x18 -> x12, local copies, waits for them, and re-layouts: 4.27 us -> 3.43 us
  transfers between devices with their start and end apart: 10 -> 10, of which waited for: 3 -> 5; matrix products, arithmetic and copies ran while one was open for 0% -> 0% of each run, Pallas kernels for 10% -> 11%
where the time goes in v11:
time: 153 us; the launch traced here: 152 us
  starting transfers between devices  53.4 us (35%)
  blocking collectives  49.1 us (32%)
  Pallas kernels  21.9 us (14%)
  waiting for transfers between devices  20.9 us (14%)
  local copies, waits for them, and re-layouts  4.43 us (3%)
  between operations  2.14 us (1%)
    all_to_all x3, blocking collectives, exchange(): lax.all_to_all(chunks, AXIS, 0, 0, axis_index_groups=groups, tiled=True)  49.1 us
    ppermute x4, starting transfers between devices, shift(): lax.ppermute(block, AXIS, [((i - 4 * distance) % N, i) for i in range(N)])  26 us
    pallas_call x8, Pallas kernels, run(): pl.pallas_call(kernel, out_shape=outs, in_specs=specs, out_specs=[VMEM] *...  21.9 us
    ppermute x4, waiting for transfers between devices, shift(): lax.ppermute(block, AXIS, [((i - 4 * distance) % N, i) for i in range(N)])  18.7 us
    ppermute x5, starting transfers between devices, move(): return lax.ppermute(block, AXIS, moves)  18.5 us
    all_to_all x1, starting transfers between devices, exchange(): lax.all_to_all(chunks, AXIS, 0, 0, axis_index_groups=groups, tiled=True)  8.91 us
    unnamed x12, local copies, waits for them, and re-layouts  3.43 us
  transfers between devices with their start and end apart: 10, of which 5 were waited for; matrix products, arithmetic and copies ran while one was open for 0% of the time, Pallas kernels for 11%

profile of v11, /device:TPU:1, one launch (start us, length us, event | category | flops | bytes accessed | tf_op | source)
XLA Modules:
  0.0 152.3 jit_solution(13519788057466998891)
XLA Ops:
  0.6 0.0 copy-start.5
  0.6 5.3 %collective-permute-start.1 = (bf16[288,1152]{1,0:T(8,128)(2,1)}, bf16[288,1152]{1,0:T(8,128)(2,1)S(1)}, u32[]{:S(2)}, u32[]{:S(2)}) collective-permute-start(bf16[288,1152]{1,0:T(8,128)(2,1)} %shard0_ref.1), channel_id=1, source_target_pairs={{2,0},{35,1},{0,2},{33,3},{6,4},{39,5},{4,6},{37,7},{10,8},{43,9},... | collective-permute-start | bytes 1990664 | tf_op jit(solution)/shard_map/ppermute | solution.py:59
  6.0 3.0 %shard_map.77 = (bf16[272,1152]{1,0:T(8,128)(2,1)}, bf16[272,1152]{1,0:T(8,128)(2,1)}) custom-call(bf16[256,1152]{1,0:T(8,128)(2,1)} %feats_ref.1, bf16[256,1152]{1,0:T(8,128)(2,1)} %text_ref.1, s32[1,256]{1,0:T(1,128)} %bitcast.8), custom_call_target="tpu_custom_call" | custom-call | flops 256 | bytes 2434048 | tf_op jit(solution)/shard_map/pallas_call | solution.py:79
  9.0 13.8 %collective-permute-start.3 = (bf16[272,1152]{1,0:T(8,128)(2,1)}, bf16[272,1152]{1,0:T(8,128)(2,1)}, u32[]{:S(2)}, u32[]{:S(2)}) collective-permute-start(bf16[272,1152]{1,0:T(8,128)(2,1)} %get-tuple-element.22.image_ref.image0_ref), channel_id=1, source_target_pairs={{4,0},{5,1},{6,2},{7,3},{8,4},{9,5},{10,6},{11,7},{12,8},{13,9},{1... | collective-permute-start | bytes 1880072 | tf_op jit(solution)/shard_map/ppermute | solution.py:55
  22.9 1.9 %collective-permute-start.2 = (bf16[272,1152]{1,0:T(8,128)(2,1)}, bf16[272,1152]{1,0:T(8,128)(2,1)S(1)}, u32[]{:S(2)}, u32[]{:S(2)}) collective-permute-start(bf16[272,1152]{1,0:T(8,128)(2,1)} %get-tuple-element.21.text_ref), channel_id=1, source_target_pairs={{508,0},{509,1},{510,2},{511,3},{0,4},{1,5},{2,6},{3,7},{4,8},{5,9... | collective-permute-start | bytes 1880072 | tf_op jit(solution)/shard_map/ppermute | solution.py:55
  24.8 3.8 %collective-permute-start = (bf16[288,1152]{1,0:T(8,128)(2,1)}, bf16[288,1152]{1,0:T(8,128)(2,1)S(1)}, u32[]{:S(2)}, u32[]{:S(2)}) collective-permute-start(bf16[288,1152]{1,0:T(8,128)(2,1)} %shard0_ref.1), channel_id=1, source_target_pairs={{1,0},{0,1},{3,2},{2,3},{5,4},{4,5},{7,6},{6,7},{9,8},{8,9},{11,10... | collective-permute-start | bytes 1990664 | tf_op jit(solution)/shard_map/ppermute | solution.py:59
  28.6 6.3 %collective-permute-done.3.image1_ref = bf16[272,1152]{1,0:T(8,128)(2,1)} collective-permute-done((bf16[272,1152]{1,0:T(8,128)(2,1)}, bf16[272,1152]{1,0:T(8,128)(2,1)}, u32[]{:S(2)}, u32[]{:S(2)}) %collective-permute-start.3) | collective-permute-done | bytes 626720 | tf_op jit(solution)/shard_map/ppermute | solution.py:55
  34.9 9.5 %collective-permute-done.2.text1_ref = bf16[272,1152]{1,0:T(8,128)(2,1)S(1)} collective-permute-done((bf16[272,1152]{1,0:T(8,128)(2,1)}, bf16[272,1152]{1,0:T(8,128)(2,1)S(1)}, u32[]{:S(2)}, u32[]{:S(2)}) %collective-permute-start.2) | collective-permute-done | bytes 626720 | tf_op jit(solution)/shard_map/ppermute | solution.py:55
  44.4 0.0 collective-permute-done.1.shard2_ref
  44.4 4.7 %collective-permute-start.4 = (bf16[288,1152]{1,0:T(8,128)(2,1)S(1)}, bf16[288,1152]{1,0:T(8,128)(2,1)}, u32[]{:S(2)}, u32[]{:S(2)}) collective-permute-start(bf16[288,1152]{1,0:T(8,128)(2,1)S(1)} %collective-permute-done.1.shard2_ref), channel_id=1, source_target_pairs={{1,0},{0,1},{3,2},{2,3},{5,4},{4,5},{7,6},{6,7},{9,8},{8,9},{11,10... | collective-permute-start | bytes 1990664 | tf_op jit(solution)/shard_map/ppermute | solution.py:59
  49.1 1.9 %collective-permute-start.5 = (bf16[272,1152]{1,0:T(8,128)(2,1)}, bf16[272,1152]{1,0:T(8,128)(2,1)S(1)}, u32[]{:S(2)}, u32[]{:S(2)}) collective-permute-start(bf16[272,1152]{1,0:T(8,128)(2,1)} %collective-permute-done.3.image1_ref), channel_id=1, source_target_pairs={{4,0},{5,1},{6,2},{7,3},{8,4},{9,5},{10,6},{11,7},{12,8},{13,9},{1... | collective-permute-start | bytes 1880072 | tf_op jit(solution)/shard_map/ppermute | solution.py:55
  52.4 0.0 collective-permute-done.shard1_ref
  52.4 0.0 collective-permute-done.4.shard3_ref
  52.4 0.0 copy-done.5
  52.4 0.0 copy-start
  52.4 1.1 copy-done
  53.5 0.0 copy-start.2
  53.5 1.1 copy-done.2
  54.5 4.2 %shard_map.78 = (bf16[1152,1152]{1,0:T(8,128)(2,1)S(1)}, bf16[256,1152]{1,0:T(8,128)(2,1)S(1)}, f32[256,1152]{1,0:T(8,128)S(1)}) custom-call(s32[1]{0:T(128)} %bitcast.grp_ref, f32[1]{0:T(128)S(6)} %copy.8.scale_ref, f32[1]{0:T(128)S(6)} %copy.9.bias_ref, bf16[288,1152]{1,0:T(8,128)(2,1)S(1)} %copy-done.5, ...), custom_call_target="tpu_custom_call" | custom-call | tf_op jit(solution)/shard_map/pallas_call | solution.py:79
  58.7 5.3 %shard_map.79 = (f32[1152,1152]{1,0:T(8,128)S(1)}, f32[256,1152]{1,0:T(8,128)S(1)}) custom-call(f32[1]{0:T(128)S(6)} %copy.8.scale_ref, f32[1]{0:T(128)S(6)} %copy.9.bias_ref, bf16[1152,1152]{1,0:T(8,128)(2,1)S(1)} %get-tuple-element.24.weight_ref, bf16[272,1152]{1,0:T(8,128)(2,1)S(1)} %copy-done.2, bf16[256,1152]{1,0:T(8,128)(2,1)S(1)} %get-tuple-element.25.raw_grad0_ref, ...), custom_call_target="tpu_custom_call" | custom-call | tf_op jit(solution)/shard_map/pallas_call | solution.py:79
  64.1 0.0 copy-start.3
  64.1 2.9 %collective-permute-done.5.image_ref.image2_ref = bf16[272,1152]{1,0:T(8,128)(2,1)S(1)} collective-permute-done((bf16[272,1152]{1,0:T(8,128)(2,1)}, bf16[272,1152]{1,0:T(8,128)(2,1)S(1)}, u32[]{:S(2)}, u32[]{:S(2)}) %collective-permute-start.5) | collective-permute-done | bytes 626720 | tf_op jit(solution)/shard_map/ppermute | solution.py:55
  67.0 3.5 %shard_map.80 = (bf16[576,1152]{1,0:T(8,128)(2,1)S(1)}, bf16[1152,256]{1,0:T(8,128)(2,1)S(1)}, bf16[256,1152]{1,0:T(8,128)(2,1)S(1)}, bf16[256,1152]{1,0:T(8,128)(2,1)S(1)}, bf16[256,256]{1,0:T(8,128)(2,1)S(1)}) custom-call(s32[1]{0:T(128)} %bitcast.grp_ref, f32[1]{0:T(128)S(6)} %copy.8.scale_ref, f32[1]{0:T(128)S(6)} %copy.9.bias_ref, ...), custom_call_target="tpu_custom_call" | custom-call | flops 1358954496 | bytes 12443660 | tf_op jit(solution)/shard_map/pallas_call | solution.py:79
  70.4 0.0 copy-done.3
  70.5 2.7 %collective-permute-start.6 = (bf16[576,1152]{1,0:T(8,128)(2,1)S(1)}, bf16[576,1152]{1,0:T(8,128)(2,1)S(1)}, u32[]{:S(2)}, u32[]{:S(2)}) collective-permute-start(bf16[576,1152]{1,0:T(8,128)(2,1)S(1)} %get-tuple-element.33), channel_id=1, source_target_pairs={{1,0},{0,1},{3,2},{2,3},{5,4},{4,5},{7,6},{6,7},{9,8},{8,9},{11,10... | collective-permute-start | bytes 3981320 | tf_op jit(solution)/shard_map/ppermute | solution.py:59
  73.2 2.5 %shard_map.81 = (bf16[576,1152]{1,0:T(8,128)(2,1)S(1)}, bf16[256,1152]{1,0:T(8,128)(2,1)}) custom-call(s32[1]{0:T(128)} %bitcast.grp_ref, bf16[1152,256]{1,0:T(8,128)(2,1)S(1)} %get-tuple-element.28.turned_ref, bf16[256,1152]{1,0:T(8,128)(2,1)S(1)} %get-tuple-element.29.raw_grad_ref, bf16[256,1152]{1,0:T(8,128)(2,1)S(1)} %get-tuple-element.30.image_unit_ref.image_unit2_ref, ...), custom_call_target="tpu_custom_call" | custom-call | flops 679477248 | bytes 9125892 | tf_op jit(solution)/shard_map/pallas_call | solution.py:79
  75.6 0.2 collective-permute-done.6
  75.8 0.4 add_convert_fusion
  76.2 17.4 %all_to_all.20.chunks_ref = bf16[8,72,1152]{2,1,0:T(8,128)(2,1)S(1)} all-to-all(bf16[8,72,1152]{2,1,0:T(8,128)(2,1)S(1)} %bitcast.6), channel_id=1, replica_groups={{0,4,64,68,2,6,66,70},{477,449,29,1,511,483,63,35},{509,481,61,33,479,4..., dimensions={0} | all-to-all | bytes 2654208 | tf_op jit(solution)/shard_map/all_to_all | solution.py:63
  93.6 0.2 shard_map.82
  93.8 15.2 %all_to_all.21 = bf16[16,48,128]{2,1,0:T(8,128)(2,1)S(1)} all-to-all(bf16[16,48,128]{2,1,0:T(8,128)(2,1)S(1)} %bitcast.5), channel_id=1, replica_groups={{0,8,16,24,128,136,144,152,256,264,272,280,384,392,400,408},{1,9,17,25,..., dimensions={0} | all-to-all | bytes 393216 | tf_op jit(solution)/shard_map/all_to_all | solution.py:63
  109.1 1.9 %collective-permute-start.7 = (bf16[48,128]{1,0:T(8,128)(2,1)S(1)}, bf16[48,128]{1,0:T(8,128)(2,1)S(1)}, u32[]{:S(2)}, u32[]{:S(2)}) collective-permute-start(bf16[48,128]{1,0:T(8,128)(2,1)S(1)} %reduce_sum.12), channel_id=1, source_target_pairs={{32,0},{33,1},{34,2},{35,3},{36,4},{37,5},{38,6},{39,7},{40,8},{41... | collective-permute-start | bytes 36872 | tf_op jit(solution)/shard_map/ppermute | solution.py:59
  111.0 8.4 %collective-permute-start.8 = (bf16[256,1152]{1,0:T(8,128)(2,1)}, bf16[256,1152]{1,0:T(8,128)(2,1)S(1)}, u32[]{:S(2)}, u32[]{:S(2)}) collective-permute-start(bf16[256,1152]{1,0:T(8,128)(2,1)} %get-tuple-element.36), channel_id=1, source_target_pairs={{4,0},{5,1},{6,2},{7,3},{8,4},{9,5},{10,6},{11,7},{12,8},{13,9},{1... | collective-permute-start | bytes 1769480 | tf_op jit(solution)/shard_map/ppermute | solution.py:55
  119.4 0.0 collective-permute-done.7
  119.4 16.4 %all_to_all.22 = bf16[16,48,128]{2,1,0:T(8,128)(2,1)S(1)} all-to-all(bf16[16,48,128]{2,1,0:T(8,128)(2,1)S(1)} %broadcast_in_dim.4), channel_id=1, replica_groups={{0,8,16,24,128,136,144,152,256,264,272,280,384,392,400,408},{1,9,17,25,..., dimensions={0} | all-to-all | bytes 393216 | tf_op jit(solution)/shard_map/all_to_all | solution.py:63
  135.9 0.0 copy-start.1
  135.9 0.0 collective-permute-done.8.back_ref
  135.9 1.0 broadcast_in_dim.5
  136.9 8.9 %all-to-all-start.3 = ((bf16[4,720,128]{2,1,0:T(8,128)(2,1)}), bf16[4,720,128]{2,1,0:T(8,128)(2,1)S(1)}, u32[]{:S(2)}, u32[]{:S(2)}) async-start(bf16[4,720,128]{2,1,0:T(8,128)(2,1)} %broadcast_in_dim.5), calls=%async_computation.3 | async-start | bytes 1474560 | tf_op jit(solution)/shard_map/all_to_all | solution.py:63
  145.8 0.0 copy-done.1
  145.8 0.0 copy-start.4
  145.8 1.3 copy-done.4
  147.1 2.1 %shard_map.84 = f32[256,1152]{1,0:T(8,128)} custom-call(f32[1]{0:T(128)S(6)} %copy.8.scale_ref, f32[1]{0:T(128)S(6)} %copy.9.bias_ref, bf16[256,1152]{1,0:T(8,128)(2,1)S(1)} %get-tuple-element.30.image_unit_ref.image_unit2_ref, bf16[272,1152]{1,0:T(8,128)(2,1)S(1)} %collective-permute-done.5.image_ref.image2_ref, bf16[272,1152]{1,0:T(8,128)(2,1)S(1)} %copy-done.1, ...), custom_call_target="tpu_custom_call" | custom-call | flops 679477248 | bytes 4792328 | tf_op jit(solution)/shard_map/pallas_call | solution.py:79
  149.2 2.0 %all-to-all-done.3.tiles_ref = bf16[4,720,128]{2,1,0:T(8,128)(2,1)S(1)} async-done(((bf16[4,720,128]{2,1,0:T(8,128)(2,1)}), bf16[4,720,128]{2,1,0:T(8,128)(2,1)S(1)}, u32[]{:S(2)}, u32[]{:S(2)}) %all-to-all-start.3) | async-done | bytes 737312 | tf_op jit(solution)/shard_map/all_to_all | solution.py:63
  151.2 1.1 shard_map.83
  (4 shorter events, 0.1 us)
Async XLA Ops:
  0.6 51.8 %copy-start.5 = (bf16[288,1152]{1,0:T(8,128)(2,1)S(1)}, bf16[288,1152]{1,0:T(8,128)(2,1)}, u32[]{:S(2)}) copy-start(bf16[288,1152]{1,0:T(8,128)(2,1)} %shard0_ref.1) | copy-start | bytes 1990660
  0.6 43.8 %collective-permute-start.1 = (bf16[288,1152]{1,0:T(8,128)(2,1)}, bf16[288,1152]{1,0:T(8,128)(2,1)S(1)}, u32[]{:S(2)}, u32[]{:S(2)}) collective-permute-start(bf16[288,1152]{1,0:T(8,128)(2,1)} %shard0_ref.1), channel_id=1, source_target_pairs={{2,0},{35,1},{0,2},{33,3},{6,4},{39,5},{4,6},{37,7},{10,8},{43,9},... | collective-permute-start | bytes 1990664 | tf_op jit(solution)/shard_map/ppermute | solution.py:59
  9.0 25.9 %collective-permute-start.3 = (bf16[272,1152]{1,0:T(8,128)(2,1)}, bf16[272,1152]{1,0:T(8,128)(2,1)}, u32[]{:S(2)}, u32[]{:S(2)}) collective-permute-start(bf16[272,1152]{1,0:T(8,128)(2,1)} %get-tuple-element.22.image_ref.image0_ref), channel_id=1, source_target_pairs={{4,0},{5,1},{6,2},{7,3},{8,4},{9,5},{10,6},{11,7},{12,8},{13,9},{1... | collective-permute-start | bytes 1880072 | tf_op jit(solution)/shard_map/ppermute | solution.py:55
  22.9 21.5 %collective-permute-start.2 = (bf16[272,1152]{1,0:T(8,128)(2,1)}, bf16[272,1152]{1,0:T(8,128)(2,1)S(1)}, u32[]{:S(2)}, u32[]{:S(2)}) collective-permute-start(bf16[272,1152]{1,0:T(8,128)(2,1)} %get-tuple-element.21.text_ref), channel_id=1, source_target_pairs={{508,0},{509,1},{510,2},{511,3},{0,4},{1,5},{2,6},{3,7},{4,8},{5,9... | collective-permute-start | bytes 1880072 | tf_op jit(solution)/shard_map/ppermute | solution.py:55
  24.8 27.6 %collective-permute-start = (bf16[288,1152]{1,0:T(8,128)(2,1)}, bf16[288,1152]{1,0:T(8,128)(2,1)S(1)}, u32[]{:S(2)}, u32[]{:S(2)}) collective-permute-start(bf16[288,1152]{1,0:T(8,128)(2,1)} %shard0_ref.1), channel_id=1, source_target_pairs={{1,0},{0,1},{3,2},{2,3},{5,4},{4,5},{7,6},{6,7},{9,8},{8,9},{11,10... | collective-permute-start | bytes 1990664 | tf_op jit(solution)/shard_map/ppermute | solution.py:59
  44.4 8.0 %collective-permute-start.4 = (bf16[288,1152]{1,0:T(8,128)(2,1)S(1)}, bf16[288,1152]{1,0:T(8,128)(2,1)}, u32[]{:S(2)}, u32[]{:S(2)}) collective-permute-start(bf16[288,1152]{1,0:T(8,128)(2,1)S(1)} %collective-permute-done.1.shard2_ref), channel_id=1, source_target_pairs={{1,0},{0,1},{3,2},{2,3},{5,4},{4,5},{7,6},{6,7},{9,8},{8,9},{11,10... | collective-permute-start | bytes 1990664 | tf_op jit(solution)/shard_map/ppermute | solution.py:59
  49.1 17.8 %collective-permute-start.5 = (bf16[272,1152]{1,0:T(8,128)(2,1)}, bf16[272,1152]{1,0:T(8,128)(2,1)S(1)}, u32[]{:S(2)}, u32[]{:S(2)}) collective-permute-start(bf16[272,1152]{1,0:T(8,128)(2,1)} %collective-permute-done.3.image1_ref), channel_id=1, source_target_pairs={{4,0},{5,1},{6,2},{7,3},{8,4},{9,5},{10,6},{11,7},{12,8},{13,9},{1... | collective-permute-start | bytes 1880072 | tf_op jit(solution)/shard_map/ppermute | solution.py:55
  52.4 1.1 copy-start
  53.5 1.1 copy-start.2
  64.1 6.4 %copy-start.3 = (f32[256,1152]{1,0:T(8,128)}, f32[256,1152]{1,0:T(8,128)S(1)}, u32[]{:S(2)}) copy-start(f32[256,1152]{1,0:T(8,128)S(1)} %get-tuple-element.38.grad_ref) | copy-start | bytes 3538948
  70.5 5.4 %collective-permute-start.6 = (bf16[576,1152]{1,0:T(8,128)(2,1)S(1)}, bf16[576,1152]{1,0:T(8,128)(2,1)S(1)}, u32[]{:S(2)}, u32[]{:S(2)}) collective-permute-start(bf16[576,1152]{1,0:T(8,128)(2,1)S(1)} %get-tuple-element.33), channel_id=1, source_target_pairs={{1,0},{0,1},{3,2},{2,3},{5,4},{4,5},{7,6},{6,7},{9,8},{8,9},{11,10... | collective-permute-start | bytes 3981320 | tf_op jit(solution)/shard_map/ppermute | solution.py:59
  109.1 10.3 %collective-permute-start.7 = (bf16[48,128]{1,0:T(8,128)(2,1)S(1)}, bf16[48,128]{1,0:T(8,128)(2,1)S(1)}, u32[]{:S(2)}, u32[]{:S(2)}) collective-permute-start(bf16[48,128]{1,0:T(8,128)(2,1)S(1)} %reduce_sum.12), channel_id=1, source_target_pairs={{32,0},{33,1},{34,2},{35,3},{36,4},{37,5},{38,6},{39,7},{40,8},{41... | collective-permute-start | bytes 36872 | tf_op jit(solution)/shard_map/ppermute | solution.py:59
  111.0 24.9 %collective-permute-start.8 = (bf16[256,1152]{1,0:T(8,128)(2,1)}, bf16[256,1152]{1,0:T(8,128)(2,1)S(1)}, u32[]{:S(2)}, u32[]{:S(2)}) collective-permute-start(bf16[256,1152]{1,0:T(8,128)(2,1)} %get-tuple-element.36), channel_id=1, source_target_pairs={{4,0},{5,1},{6,2},{7,3},{8,4},{9,5},{10,6},{11,7},{12,8},{13,9},{1... | collective-permute-start | bytes 1769480 | tf_op jit(solution)/shard_map/ppermute | solution.py:55
  135.9 9.9 %copy-start.1 = (bf16[272,1152]{1,0:T(8,128)(2,1)S(1)}, bf16[272,1152]{1,0:T(8,128)(2,1)}, u32[]{:S(2)}) copy-start(bf16[272,1152]{1,0:T(8,128)(2,1)} %get-tuple-element.21.text_ref) | copy-start | bytes 1880068
  136.9 14.3 %all-to-all-start.3 = ((bf16[4,720,128]{2,1,0:T(8,128)(2,1)}), bf16[4,720,128]{2,1,0:T(8,128)(2,1)S(1)}, u32[]{:S(2)}, u32[]{:S(2)}) async-start(bf16[4,720,128]{2,1,0:T(8,128)(2,1)} %broadcast_in_dim.5), calls=%async_computation.3 | async-start | bytes 1474560 | tf_op jit(solution)/shard_map/all_to_all | solution.py:63
  145.8 1.3 copy-start.4
